TPU v7x, 32 devices: a whole 2x2x4 slice. The times are simulated.
32 devices in a mesh: gcm: 4 (over y, core), crm: 8 (over z, x).
Axes of the slice: x: 2, y: 2, z: 4, core: 2. Of those that a mesh axis runs over, the one named last changes fastest.
Arguments:
- tracer: float32 [72, 32, 2048], P(None, 'gcm', 'crm'), may hold values from -6 to 6
- wind_x: float32 [72, 32, 2048], P(None, 'gcm', 'crm'), may hold values from -4 to 4
- wind_y: float32 [72, 32, 2048], P(None, 'gcm', 'crm'), may hold values from -4 to 4
- drops: bfloat16 [4096, 33, 256], P(('gcm', 'crm')), may hold values from 0 to 1
- owner: int32 [4096, 1], P(('gcm', 'crm')), may hold values from 0 to 31, as said below
- counts: int32 [4096], P(('gcm', 'crm')), may hold values from 0 to 4, as said below
- collision: bfloat16 [33, 1089], replicated, may hold values from -0.1875 to 0.1875
- growth: float32 [33], replicated, may hold values from -4 to 4
Outputs:
- tracer_next: float32 [72, 32, 2048], P(None, 'gcm', 'crm')
- drops_next: bfloat16 [4096, 33, 256], P(('gcm', 'crm'))
- power: float32 [16, 8192], P(None, ('gcm', 'crm'))
Inputs may be any that keep to these rules, and one draw needn't show every extreme that they name: Owner index in gcm-then-crm device order; among the 128 columns of one device no owner appears more than 8 times, and some owner appears exactly 8 times. `counts`: how cloudy the columns are differs from device to device.
All inputs are finite; a program needn't handle non-finite values.
Results may differ from a plain program's by a relative error of at most 0.0018.
Values may be sent and summed in bfloat16 or wider, within the bound.
No kernel may reach another device: no remote copies, remote signals or barrier semaphores. Data moves between devices by JAX's collectives and lax.ppermute only.
A program may use at most 128 MiB of HBM per device.

v0:
```python
import functools

import jax
import jax.numpy as jnp
import numpy as np
from jax import lax
from jax.experimental import pallas as pl
from jax.experimental.pallas import tpu as pltpu
from jax.sharding import PartitionSpec as P

CRM_X = 16
CRM_LEV = 16
DYN_STEPS = 2

DT_DYN = 0.04
DT_CRM = 0.05
DT_PHYS = 0.5
HIGH = lax.Precision.HIGHEST
F32 = jnp.float32
BF16 = jnp.bfloat16
GROUP = 8
CHUNK = 8
MIB = 1024 * 1024


def gll_tables():
    inv_root = 1.0 / np.sqrt(5.0)
    gll_nodes = np.array([-1.0, -inv_root, inv_root, 1.0])
    weights = np.array([1.0, 5.0, 5.0, 1.0]) / 6.0
    legendre = (5.0 * gll_nodes**3 - 3.0 * gll_nodes) / 2.0
    derivative = np.zeros((4, 4))
    for i in range(4):
        for j in range(4):
            if i != j:
                derivative[i, j] = legendre[i] / (legendre[j] * (gll_nodes[i] - gll_nodes[j]))
    derivative[0, 0] = -3.0
    derivative[3, 3] = 3.0
    return (2.0 * derivative, weights)


def level_tables(levels, crm_levels):
    spacing = levels / crm_levels
    centres = (np.arange(crm_levels) + 0.5) * spacing - 0.5
    hats = np.maximum(0.0, 1.0 - np.abs(np.arange(levels)[None, :] - centres[:, None]) / spacing)
    down_map = hats / hats.sum(axis=1, keepdims=True)
    up_map = hats.T / hats.T.sum(axis=1, keepdims=True)
    return (down_map, up_map)


DERIV, WEIGHTS = gll_tables()


def iota(shape, axis):
    return lax.broadcasted_iota(jnp.int32, shape, axis)


def derivative_terms(shape, axis):
    phase = iota(shape, axis) % 4
    terms = []
    for shift in range(-3, 4):
        value = jnp.zeros(shape, F32)
        for i in range(4):
            if 0 <= i + shift < 4:
                value = jnp.where(phase == i, F32(DERIV[i, i + shift]), value)
        terms.append((shift, value))
    return terms


def along(x, terms, axis):
    size = x.shape[axis]
    total = None
    for shift, value in terms:
        moved = x if shift == 0 else pltpu.roll(x, (-shift) % size, axis)
        part = value[None] * moved
        total = part if total is None else total + part
    return total


def tendency(x, u, v, row_terms, col_terms):
    halves = []
    for h in range(x.shape[2] // 128):
        cut = slice(128 * h, 128 * h + 128)
        q = x[:, :, cut]
        grad_x = along(q, row_terms, 1)
        grad_y = along(q, col_terms, 2)
        halves.append(-(u[:, :, cut] * grad_x + v[:, :, cut] * grad_y))
    return jnp.concatenate(halves, axis=2)


def pack_kernel(q_hbm, u_hbm, v_hbm, right_ref, left_ref, q_ref, u_ref, v_ref, sems):
    copies = []
    for i, (src, dst) in enumerate(((q_hbm, q_ref), (u_hbm, u_ref), (v_hbm, v_ref))):
        copies.append(pltpu.make_async_copy(src, dst, sems.at[i]))
    for copy in copies:
        copy.start()
    for copy in copies:
        copy.wait()
    lane = iota((8, 128), 1)

    def body(group, carry):
        right = jnp.zeros((8, 128), F32)
        left = jnp.zeros((8, 128), F32)
        for j in range(4):
            for f, ref in enumerate((q_ref, u_ref, v_ref)):
                start = 32 * j + 8 * f
                here = (lane >= start) & (lane < start + 8)
                x = ref[group * 4 + j]
                right = jnp.where(here, pltpu.roll(x[:, 128:256], (start - 120) % 128, 1), right)
                first = x[:, 0:128]
                if start:
                    first = pltpu.roll(first, start, 1)
                left = jnp.where(here, first, left)
        right_ref[group] = right
        left_ref[group] = left
        return carry

    lax.fori_loop(0, right_ref.shape[0], body, 0)


def put_rows(x, levels, top_ref, bot_ref, i):
    top_ref[i, levels, :] = x[:, 0, :]
    bot_ref[i, levels, :] = x[:, 7, :]


def first_kernel(q_ref, u_ref, v_ref, tend_ref, top_ref, bot_ref):
    row_terms = derivative_terms((8, 128), 0)
    col_terms = derivative_terms((8, 128), 1)

    def body(chunk, carry):
        levels = pl.ds(pl.multiple_of(chunk * CHUNK, CHUNK), CHUNK)
        q = q_ref[levels]
        tend = tendency(q, u_ref[levels], v_ref[levels], row_terms, col_terms)
        tend_ref[levels] = tend
        put_rows(tend, levels, top_ref, bot_ref, 0)
        put_rows(q, levels, top_ref, bot_ref, 1)
        return carry

    lax.fori_loop(0, q_ref.shape[0] // CHUNK, body, 0)


def strip_kernel(
    left_ref, right_ref, top_main, bot_main,
    q_ref, u_ref, v_ref, tend_ref, top_ref, bot_ref,
):
    row_terms = derivative_terms((8, 128), 0)
    col_terms = derivative_terms((8, 128), 1)
    lane = iota((8, 128), 1)
    top_ref[:, :, 0:256] = top_main[...]
    bot_ref[:, :, 0:256] = bot_main[...]

    def body(chunk, carry):
        tiles = [[], [], []]
        for half in range(CHUNK // 4):
            west = left_ref[chunk * (CHUNK // 4) + half]
            east = right_ref[chunk * (CHUNK // 4) + half]
            for j in range(4):
                for f in range(3):
                    start = 32 * j + 8 * f
                    a = pltpu.roll(east, 128 - start, 1) if start else east
                    b = pltpu.roll(west, (120 - start) % 128, 1)
                    tiles[f].append(jnp.where(lane < 8, a, jnp.where(lane >= 120, b, 0.0)))
        q, u, v = [jnp.stack(tile, axis=0) for tile in tiles]
        levels = pl.ds(pl.multiple_of(chunk * CHUNK, CHUNK), CHUNK)
        q_ref[levels] = q
        u_ref[levels] = u
        v_ref[levels] = v
        tend = tendency(q, u, v, row_terms, col_terms)
        tend_ref[levels] = tend
        for i, x in enumerate((tend, q)):
            top_ref[i, levels, 256:384] = x[:, 0, :]
            bot_ref[i, levels, 256:384] = x[:, 7, :]
        return carry

    lax.fori_loop(0, q_ref.shape[0] // CHUNK, body, 0)


def assemble_chunk(x, up, down):
    shape = x.shape
    row = iota(shape, 1)
    partner = jnp.where(
        row == 0,
        jnp.broadcast_to(up[:, None, :], shape),
        jnp.where(
            row == 7,
            jnp.broadcast_to(down[:, None, :], shape),
            jnp.where(row == 3, pltpu.roll(x, 7, 1), pltpu.roll(x, 1, 1)),
        ),
    )
    x = jnp.where((row % 4 == 0) | (row % 4 == 3), 0.5 * (x + partner), x)
    col = iota(shape, 2)
    partner = jnp.where(
        col % 4 == 3, pltpu.roll(x, shape[2] - 1, 2), pltpu.roll(x, 1, 2)
    )
    return jnp.where((col % 4 == 0) | (col % 4 == 3), 0.5 * (x + partner), x)


def join(main, strip):
    return jnp.concatenate([main, strip], axis=2)


def second_kernel(
    q_ref, u_ref, v_ref, tend_ref, q_strip, u_strip, v_strip, tend_strip, up_ref, down_ref,
    state_ref, smooth_ref, next_ref, top_ref, bot_ref,
):
    row_terms = derivative_terms((8, 128), 0)
    col_terms = derivative_terms((8, 128), 1)

    def body(chunk, carry):
        levels = pl.ds(pl.multiple_of(chunk * CHUNK, CHUNK), CHUNK)
        q = join(q_ref[levels], q_strip[levels])
        change = assemble_chunk(
            join(tend_ref[levels], tend_strip[levels]), up_ref[0, levels, :], down_ref[0, levels, :]
        )
        smooth = assemble_chunk(q, up_ref[1, levels, :], down_ref[1, levels, :])
        smooth_ref[levels] = smooth[:, :, 0:256]
        state = q + DT_DYN * change
        state_ref[levels] = state[:, :, 0:256]
        tend = tendency(
            state, join(u_ref[levels], u_strip[levels]), join(v_ref[levels], v_strip[levels]),
            row_terms, col_terms,
        )
        next_ref[levels] = tend
        put_rows(tend, levels, top_ref, bot_ref, 0)
        return carry

    lax.fori_loop(0, q_ref.shape[0] // CHUNK, body, 0)


def third_kernel(
    q_ref, state_ref, smooth_ref, tend_ref, up_ref, down_ref, down_map_ref,
    base_ref, cell_ref, near_ref, far_ref,
):
    cols = cell_ref.shape[0]
    half = cols // 2
    phase = iota((8, 256), 0) % 4
    row_weight = jnp.where((phase == 0) | (phase == 3), F32(WEIGHTS[0]), F32(WEIGHTS[1]))
    near_rows = jnp.where(iota((8, 256), 0) < 4, row_weight, 0.0)
    far_rows = row_weight - near_rows

    def body(chunk, carry):
        levels = pl.ds(pl.multiple_of(chunk * CHUNK, CHUNK), CHUNK)
        change = assemble_chunk(tend_ref[levels], up_ref[0, levels, :], down_ref[0, levels, :])
        moved = (state_ref[levels] + DT_DYN * change[:, :, 0:256]) - q_ref[levels]
        base_ref[levels] = smooth_ref[levels] + moved
        near_ref[levels, :] = jnp.sum(moved * near_rows[None], axis=1)
        far_ref[levels, :] = jnp.sum(moved * far_rows[None], axis=1)
        return carry

    lax.fori_loop(0, q_ref.shape[0] // CHUNK, body, 0)
    point = iota((256, cols), 0)
    element = iota((256, cols), 1)
    weight = jnp.where(
        (point % 4 == 0) | (point % 4 == 3), F32(WEIGHTS[0]), F32(WEIGHTS[1])
    ) * F32(0.25 / (DYN_STEPS * DT_DYN))
    near_cols = jnp.where(point // 4 == element, weight, 0.0)
    far_cols = jnp.where(point // 4 + half == element, weight, 0.0)
    means = jnp.dot(near_ref[...], near_cols, precision=HIGH, preferred_element_type=F32)
    means += jnp.dot(far_ref[...], far_cols, precision=HIGH, preferred_element_type=F32)
    forcing = jnp.dot(down_map_ref[...], means, precision=HIGH, preferred_element_type=F32)
    forcing = forcing.T.astype(BF16)
    cells = cell_ref.shape[1]
    spread = (iota((CRM_LEV, cells), 1) // CRM_X == iota((CRM_LEV, cells), 0)).astype(BF16)
    cell_ref[...] = DT_CRM * jnp.dot(forcing, spread, preferred_element_type=F32)


def crm_kernel(
    order_ref, count_ref, place_ref, drops_ref, cell_ref, slot_ref, coef_ref, tail_coef_ref,
    growth_ref,
    final_ref, heat_ref, send_ref, state_ref, pair_ref, tail_ref, heat_cell_ref, echo_cell_ref,
):
    bins = drops_ref.shape[1]
    cells = drops_ref.shape[2]
    cols = drops_ref.shape[0]
    coef = coef_ref[...]
    tail_coef = tail_coef_ref[...]
    growth = growth_ref[...]
    state_ref[...] = jnp.zeros(state_ref.shape, F32)
    mass = (iota((40, cells), 0) + 1).astype(F32) / F32(bins)

    def grow(k, which):
        grown = state_ref[k] + growth * cell_ref[pl.ds(which, 1), :]
        for h in range(cells // 128):
            cut = slice(128 * h, 128 * h + 128)
            g = grown[0:32, cut]
            last = grown[32:40, cut]
            for s in range(8):
                rolled = g if s == 0 else pltpu.roll(g, 32 - s, 0)
                for a in range(2):
                    other = rolled
                    if a:
                        other = jnp.concatenate([rolled[8:], rolled[:8]], axis=0)
                    d = 8 * a + s
                    pair_ref[k, 32 * d : 32 * d + 32, cut] = (g * other).astype(BF16)
            at = 64 * (k % 4)
            tail_ref[k // 4, at : at + 16, cut] = (g[0:16] * g[16:32]).astype(BF16)
            tail_ref[k // 4, at + 16 : at + 48, cut] = (g * last[0:1]).astype(BF16)
            tail = jnp.concatenate([last * last, jnp.zeros((8, 128), F32)], axis=0)
            tail_ref[k // 4, at + 48 : at + 64, cut] = tail.astype(BF16)
        return grown

    def group(index, carry):
        base = index * GROUP
        which = [order_ref[base + k] for k in range(GROUP)]
        count = [count_ref[base + k] for k in range(GROUP)]
        for k in range(GROUP):
            state_ref[k, 0:bins, :] = drops_ref[which[k]].astype(F32)

        def step(s, c):
            for q in range(GROUP // 4):
                grown = [grow(4 * q + k, which[4 * q + k]) for k in range(4)]
                tails = jnp.dot(tail_coef, tail_ref[q], preferred_element_type=F32)
                for k in range(4):
                    slot = 4 * q + k
                    change = jnp.dot(coef, pair_ref[slot], preferred_element_type=F32)
                    change = change + tails[80 * k : 80 * k + 80]
                    moved = grown[k] + (change[0:40] + change[40:80])
                    state_ref[slot] = jnp.where(s < count[slot], moved, state_ref[slot])
            return c

        lax.fori_loop(0, count[0], step, 0)
        for k in range(GROUP):
            final = state_ref[k, 0:bins, :]
            initial = drops_ref[which[k]].astype(F32)
            final_ref[which[k]] = final.astype(BF16)
            weighted = mass[0:bins] * final
            heat = jnp.sum(mass[0:bins] * (final - initial), axis=0, keepdims=True)
            echo = jnp.sum(weighted * weighted, axis=0, keepdims=True)
            heat_cell_ref[pl.ds(which[k], 1), :] = heat
            echo_cell_ref[pl.ds(which[k], 1), :] = echo
        return carry

    lax.fori_loop(0, cols // GROUP, group, 0)
    means = jnp.where(
        iota((CRM_LEV, cells), 1) // CRM_X == iota((CRM_LEV, cells), 0), F32(1.0 / CRM_X), 0.0
    )
    contract = (((1,), (1,)), ((), ()))
    heat = lax.dot_general(
        means, heat_cell_ref[...], contract, precision=HIGH, preferred_element_type=F32
    )
    heat = heat.astype(BF16).astype(F32)
    heat_ref[...] = heat
    echo = lax.dot_general(
        means, echo_cell_ref[...], contract, precision=HIGH, preferred_element_type=F32
    )
    echo = jnp.log(1.0 + echo)

    devices = send_ref.shape[0]
    slots = 2 * cols
    capacity = slots // devices
    onehot = (slot_ref[...] == iota((slots, cols), 0)).astype(F32)
    packed = lax.dot_general(echo, onehot, contract, precision=HIGH, preferred_element_type=F32)
    coarse = packed.astype(BF16).astype(F32)
    rest = packed - coarse
    middle = rest.astype(BF16).astype(F32)
    pieces = (coarse, middle, rest - middle)
    lane = iota((CRM_LEV, 128), 1)
    near = heat
    far = pltpu.roll(heat, 64, 1)
    sides = jnp.where(
        lane == 1, pltpu.roll(heat, 65, 1), jnp.where(lane == 62, pltpu.roll(heat, 63, 1), heat)
    )
    n_gcm = place_ref[1]
    n_crm = place_ref[2]
    for d in range(devices):
        away = d // n_crm - place_ref[0]
        below = (away == 1) | (away == 1 - n_gcm)
        above = (away == -1) | (away == n_gcm - 1)
        block = jnp.where(below, far, jnp.where(above, near, sides))
        tile, offset = divmod(d * capacity, 128)
        for i, piece in enumerate(pieces):
            moved = pltpu.roll(
                piece[:, 128 * tile : 128 * tile + 128], (64 + i * capacity - offset) % 128, 1
            )
            start = 64 + i * capacity
            block = jnp.where((lane >= start) & (lane < start + capacity), moved, block)
        send_ref[d] = block.astype(BF16)


def last_kernel(around_ref, base_ref, own_ref, got_ref, up_map_ref, out_ref, power_ref, *back_refs):
    cols = own_ref.shape[1]
    half = cols // 2
    element = iota((cols, 256), 0)
    col = iota((cols, 256), 1)
    phase = col % 4
    edge = (phase == 0) | (phase == 3)
    other = jnp.where(phase == 0, col // 4 - 1, col // 4 + 1)

    def spread(centre, start, west, west_lane, east, east_lane):
        inside = jnp.where(element == col // 4 + start, jnp.where(edge, 0.5, 1.0), 0.0)
        beside = edge & (element == other + start) & (other >= 0) & (other < half)
        middle = jnp.where(beside, 0.5, inside).astype(BF16)
        from_west = jnp.where((col == 0) & (element == west_lane), 0.5, 0.0).astype(BF16)
        from_east = jnp.where((col == 255) & (element == east_lane), 0.5, 0.0).astype(BF16)
        total = jnp.dot(centre, middle, preferred_element_type=F32)
        total += jnp.dot(west, from_west, preferred_element_type=F32)
        total += jnp.dot(east, from_east, preferred_element_type=F32)
        return total

    own = own_ref[...].astype(BF16)
    up, down, left, right, up_left, up_right, down_left, down_right = [
        got_ref[around_ref[i]] for i in range(8)
    ]
    above = spread(up, 0, up_left, half - 1, up_right, 0)
    near = spread(own, 0, left, half - 1, right, 0)
    far = spread(own, half, left, half - 2, right, 1)
    below = spread(down, 0, down_left, half - 1, down_right, 0)
    parts = (
        0.5 * (above + near), near, 0.5 * (near + far), far, 0.5 * (far + below),
    )
    up_map = up_map_ref[...]
    for part, ref in zip(parts, back_refs):
        ref[...] = DT_PHYS * jnp.dot(up_map, part, precision=HIGH, preferred_element_type=F32)

    devices = got_ref.shape[0]
    slots = power_ref.shape[1]
    capacity = slots // devices
    lane = iota((CRM_LEV, 128), 1)
    tiles = [jnp.zeros((CRM_LEV, 128), F32) for _ in range(slots // 128)]
    for d in range(devices):
        block = got_ref[d].astype(F32)
        fine = pltpu.roll(block, 128 - 2 * capacity, 1) + pltpu.roll(block, 128 - capacity, 1)
        tile, offset = divmod(d * capacity, 128)
        moved = pltpu.roll(block + fine, (offset - 64) % 128, 1)
        tiles[tile] = jnp.where((lane >= offset) & (lane < offset + capacity), moved, tiles[tile])
    power_ref[...] = jnp.concatenate(tiles, axis=1)

    def body(chunk, carry):
        levels = pl.ds(pl.multiple_of(chunk * CHUNK, CHUNK), CHUNK)
        shape = (CHUNK, 8, 256)
        row = iota(shape, 1)
        wide = [jnp.broadcast_to(ref[levels, :][:, None, :], shape) for ref in back_refs]
        back = jnp.where(
            row == 0,
            wide[0],
            jnp.where(
                row < 3,
                wide[1],
                jnp.where(row < 5, wide[2], jnp.where(row < 7, wide[3], wide[4])),
            ),
        )
        out_ref[levels] = base_ref[levels] + back
        return carry

    lax.fori_loop(0, base_ref.shape[0] // CHUNK, body, 0)


def call(kernel, outs, args, scratch=(), sems=(), flops=10_000_000):
    spaces = {
        "s": pl.BlockSpec(memory_space=pltpu.SMEM),
        "v": pl.BlockSpec(memory_space=pltpu.VMEM),
        "h": pl.BlockSpec(memory_space=pl.ANY),
    }
    return pl.pallas_call(
        kernel,
        out_shape=[jax.ShapeDtypeStruct(s, t) for s, t in outs],
        in_specs=[spaces[kind] for kind, _ in args],
        out_specs=[spaces["v"]] * len(outs),
        scratch_shapes=[pltpu.VMEM(s, t) for s, t in scratch] + list(sems),
        compiler_params=pltpu.CompilerParams(vmem_limit_bytes=40 * MIB),
        cost_estimate=pl.CostEstimate(flops=flops, bytes_accessed=4_000_000, transcendentals=0),
    )(*[value for _, value in args])


def v(*values):
    return [("v", value) for value in values]


def shift(value, rows, cols):
    n_gcm = lax.axis_size("gcm")
    n_crm = lax.axis_size("crm")
    pairs = []
    for g in range(n_gcm):
        for c in range(n_crm):
            target = ((g + rows) % n_gcm) * n_crm + (c + cols) % n_crm
            pairs.append((g * n_crm + c, target))
    return lax.ppermute(value, ("gcm", "crm"), pairs)


def pair_table(bins):
    table = np.zeros((bins * bins, 576), np.float32)

    def put(column, i, j):
        table[i * bins + j, column] = 1.0
        table[j * bins + i, column] = 1.0

    for d in range(16):
        for b in range(32):
            put(32 * d + b, b, (b + d) % 32)
    for b in range(16):
        put(512 + b, b, b + 16)
    for b in range(32):
        put(528 + b, b, 32)
    put(560, 32, 32)
    return table


def rank_order(counts):
    total = counts.shape[0]
    index = jnp.arange(total, dtype=jnp.int32)
    ahead = (counts[None, :] > counts[:, None]) | (
        (counts[None, :] == counts[:, None]) & (index[None, :] < index[:, None])
    )
    rank = jnp.sum(ahead.astype(jnp.int32), axis=1)
    match = rank[None, :] == index[:, None]
    order = jnp.sum(jnp.where(match, index[None, :], 0), axis=1)
    ordered = jnp.sum(jnp.where(match, counts[None, :], 0), axis=1)
    return order, ordered


def shards(tracer, wind_x, wind_y, drops, owner, counts, collision, growth):
    devices = lax.axis_size("gcm") * lax.axis_size("crm")
    levels, row_count, col_count = tracer.shape
    col_total, bins, cells = drops.shape
    field = (tracer.shape, F32)
    strip = ((levels, row_count, 128), F32)
    rows = ((2, levels, col_count), F32)
    wide = col_count + 128
    down_map, up_map = level_tables(levels, CRM_LEV)

    to_right, to_left = call(
        pack_kernel,
        [((levels // 4, 8, 128), F32)] * 2,
        [("h", tracer), ("h", wind_x), ("h", wind_y)],
        [field] * 3,
        [pltpu.SemaphoreType.DMA((3,))],
    )
    from_left = shift(to_right, 0, 1)
    from_right = shift(to_left, 0, -1)
    tend, top, bot = call(first_kernel, [field, rows, rows], v(tracer, wind_x, wind_y))
    q_strip, u_strip, v_strip, tend_strip, top, bot = call(
        strip_kernel,
        [strip] * 4 + [((2, levels, wide), F32)] * 2,
        v(from_left, from_right, top, bot),
    )
    state, smooth, tend, top, bot = call(
        second_kernel,
        [field, field, ((levels, row_count, wide), F32)] + [((1, levels, wide), F32)] * 2,
        v(tracer, wind_x, wind_y, tend, q_strip, u_strip, v_strip, tend_strip)
        + v(shift(bot, 1, 0), shift(top, -1, 0)),
    )
    base, cell_forcing = call(
        third_kernel,
        [field, ((col_total, cells), F32)],
        v(tracer, state, smooth, tend, shift(bot, 1, 0), shift(top, -1, 0))
        + v(jnp.asarray(down_map, F32)),
        [((levels, col_count), F32), ((levels, col_count), F32)],
    )

    capacity = 2 * col_total // devices
    owners = owner[:, 0]
    index = jnp.arange(col_total, dtype=jnp.int32)
    same = (owners[:, None] == owners[None, :]) & (index[:, None] < index[None, :])
    slot_of = owners * capacity + jnp.sum(same.astype(jnp.int32), axis=0)
    order, ordered = rank_order(counts)
    table = jnp.asarray(pair_table(bins), BF16)
    coef = DT_CRM * jnp.dot(collision, table, preferred_element_type=F32)
    coarse = lax.reduce_precision(coef, 8, 7)
    fine = coef - coarse
    pad = ((0, 40 - bins), (0, 0))
    coef = jnp.concatenate([jnp.pad(coarse, pad), jnp.pad(fine, pad)], axis=0).astype(BF16)
    tail = coef[:, 512:]
    tail_coef = jnp.concatenate(
        [jnp.pad(tail, ((0, 0), (64 * k, 192 - 64 * k))) for k in range(4)], axis=0
    )
    growth_rows = jnp.broadcast_to(jnp.pad(growth, (0, 40 - bins))[:, None], (40, cells))
    n_gcm = lax.axis_size("gcm")
    n_crm = lax.axis_size("crm")
    g = lax.axis_index("gcm").astype(jnp.int32)
    c = lax.axis_index("crm").astype(jnp.int32)
    place = jnp.stack([g, jnp.int32(n_gcm), jnp.int32(n_crm)])

    final, heat, send = call(
        crm_kernel,
        [((col_total, bins, cells), BF16), ((CRM_LEV, col_total), F32),
         ((devices, CRM_LEV, 128), BF16)],
        [("s", order), ("s", ordered), ("s", place)]
        + v(drops, cell_forcing, slot_of[None, :], coef[:, :512], tail_coef, growth_rows),
        [((GROUP, 40, cells), F32), ((GROUP, 512, cells), BF16),
         ((GROUP // 4, 256, cells), BF16),
         ((col_total, cells), F32), ((col_total, cells), F32)],
        flops=10_000_000_000,
    )
    got = lax.all_to_all(send, ("gcm", "crm"), split_axis=0, concat_axis=0, tiled=True)
    up = (g + n_gcm - 1) % n_gcm * n_crm
    same_row = g * n_crm
    down = (g + 1) % n_gcm * n_crm
    west = (c + n_crm - 1) % n_crm
    east = (c + 1) % n_crm
    around = jnp.stack(
        [up + c, down + c, same_row + west, same_row + east,
         up + west, up + east, down + west, down + east]
    )
    tracer_next, power = call(
        last_kernel,
        [field, ((CRM_LEV, devices * capacity), F32)],
        [("s", around)] + v(base, heat, got, jnp.asarray(up_map, F32)),
        [((levels, col_count), F32)] * 5,
    )
    return (tracer_next, final, power)


def solution(mesh):
    return jax.shard_map(
        shards,
        mesh=mesh,
        in_specs=(
            P(None, "gcm", "crm"),
            P(None, "gcm", "crm"),
            P(None, "gcm", "crm"),
            P(("gcm", "crm"), None, None),
            P(("gcm", "crm"), None),
            P(("gcm", "crm")),
            P(),
            P(),
        ),
        out_specs=(P(None, "gcm", "crm"), P(("gcm", "crm"), None, None), P(None, ("gcm", "crm"))),
        check_vma=False,
    )
```

profile of v0, /device:TPU:0, one launch (start us, length us, event | category | flops | bytes accessed | tf_op | source)
XLA Modules:
  0.0 113.4 jit_solution(13284237753689687078)
XLA Ops:
  0.6 0.0 copy-start
  0.6 0.0 copy-start.1
  0.7 1.1 copy-done.1
  1.7 1.1 copy-done.3
  2.8 1.1 copy-done.5
  3.9 2.1 %shard_map.131 = (f32[18,8,128]{2,1,0:T(8,128)S(1)}, f32[18,8,128]{2,1,0:T(8,128)S(1)}) custom-call(f32[72,8,256]{2,1,0:T(8,128)S(1)} %copy-done.1, f32[72,8,256]{2,1,0:T(8,128)S(1)} %copy-done.3, f32[72,8,256]{2,1,0:T(8,128)S(1)} %copy-done.5), custom_call_target="tpu_custom_call" | custom-call | flops 10000000 | bytes 4000000 | tf_op jit(solution)/shard_map/pallas_call | solution.py:453
  5.9 0.0 copy-start.10
  6.0 3.0 %collective-permute-start = (f32[18,8,128]{2,1,0:T(8,128)S(1)}, f32[18,8,128]{2,1,0:T(8,128)S(1)}, u32[]{:S(2)}, u32[]{:S(2)}) collective-permute-start(f32[18,8,128]{2,1,0:T(8,128)S(1)} %get-tuple-element.27), channel_id=1, source_target_pairs={{0,1},{1,2},{2,3},{3,4},{4,5},{5,6},{6,7},{7,0},{8,9},{9,10},{10,1... | collective-permute-start | bytes 221192 | tf_op jit(solution)/shard_map/ppermute | solution.py:476
  9.0 3.1 %collective-permute-start.1 = (f32[18,8,128]{2,1,0:T(8,128)S(1)}, f32[18,8,128]{2,1,0:T(8,128)S(1)}, u32[]{:S(2)}, u32[]{:S(2)}) collective-permute-start(f32[18,8,128]{2,1,0:T(8,128)S(1)} %get-tuple-element.28), channel_id=1, source_target_pairs={{0,7},{1,0},{2,1},{3,2},{4,3},{5,4},{6,5},{7,6},{8,15},{9,8},{10,9... | collective-permute-start | bytes 221192 | tf_op jit(solution)/shard_map/ppermute | solution.py:476
  12.1 0.0 copy-done
  12.1 1.7 %reduce-precision_convert_fusion = (bf16[33,576]{1,0:T(8,128)(2,1)S(1)}, bf16[33,576]{1,0:T(8,128)(2,1)S(1)}) fusion(bf16[1089,576]{1,0:T(8,128)(2,1)} %constant.65.clone, bf16[33,1089]{1,0:T(8,128)(2,1)S(1)} %copy-done), kind=kOutput, calls=%fused_computation.22 | convolution fusion | flops 41494464 | bytes 1402434 | tf_op jit(solution)/shard_map/dot_general | solution.py:556
  13.8 1.6 %shard_map.130 = (f32[72,8,256]{2,1,0:T(8,128)S(1)}, f32[2,72,256]{2,1,0:T(8,128)S(1)}, f32[2,72,256]{2,1,0:T(8,128)S(1)}) custom-call(f32[72,8,256]{2,1,0:T(8,128)S(1)} %copy-done.1, f32[72,8,256]{2,1,0:T(8,128)S(1)} %copy-done.3, f32[72,8,256]{2,1,0:T(8,128)S(1)} %copy-done.5), custom_call_target="tpu_custom_call" | custom-call | flops 10000000 | bytes 4000000 | tf_op jit(solution)/shard_map/pallas_call | solution.py:453
  15.4 0.2 convert_reduce_fusion.1
  15.6 0.1 select_reduce_fusion
  15.7 0.1 fusion.10.tail_coef_ref
  15.8 0.0 copy-start.11
  15.8 0.0 copy-start.12
  15.8 0.0 copy-start.2
  15.9 0.0 copy-start.4
  15.9 0.0 copy-start.6
  15.9 3.0 %copy.16.drops_ref = bf16[128,33,256]{2,1,0:T(8,128)(2,1)S(1)} copy(bf16[128,33,256]{2,0,1:T(8,128)(2,1)} %param.14) | data formatting | bytes 4325376 | tf_op args[3]
  18.9 0.0 copy-done.11
  18.9 0.1 convert_reduce_fusion
  19.0 0.0 collective-permute-done.left_ref
  19.0 0.0 collective-permute-done.1.right_ref
  19.0 0.0 copy-start.9
  19.0 1.9 %shard_map.132 = (f32[72,8,128]{2,1,0:T(8,128)S(1)}, f32[72,8,128]{2,1,0:T(8,128)S(1)}, f32[72,8,128]{2,1,0:T(8,128)S(1)}, f32[72,8,128]{2,1,0:T(8,128)S(1)}, f3...) custom-call(f32[18,8,128]{2,1,0:T(8,128)S(1)} %collective-permute-done.left_ref, ...), custom_call_target="tpu_custom_call" | custom-call | flops 10000000 | bytes 4000000 | tf_op jit(solution)/shard_map/pallas_call | solution.py:453
  20.9 0.1 collective-permute-start.2
  21.0 1.7 %collective-permute-start.3 = (f32[2,72,384]{2,1,0:T(8,128)S(1)}, f32[2,72,384]{2,1,0:T(8,128)S(1)}, u32[]{:S(2)}, u32[]{:S(2)}) collective-permute-start(f32[2,72,384]{2,1,0:T(8,128)S(1)} %get-tuple-element.36), channel_id=1, source_target_pairs={{0,24},{1,25},{2,26},{3,27},{4,28},{5,29},{6,30},{7,31},{8,0},{9,1... | collective-permute-start | bytes 663560 | tf_op jit(solution)/shard_map/ppermute | solution.py:476
  22.7 4.0 %collective-permute-done.2.up_ref = f32[2,72,384]{2,1,0:T(8,128)S(1)} collective-permute-done((f32[2,72,384]{2,1,0:T(8,128)S(1)}, f32[2,72,384]{2,1,0:T(8,128)S(1)}, u32[]{:S(2)}, u32[]{:S(2)}) %collective-permute-start.2) | collective-permute-done | bytes 221216 | tf_op jit(solution)/shard_map/ppermute | solution.py:476
  26.7 1.2 %collective-permute-done.3.down_ref = f32[2,72,384]{2,1,0:T(8,128)S(1)} collective-permute-done((f32[2,72,384]{2,1,0:T(8,128)S(1)}, f32[2,72,384]{2,1,0:T(8,128)S(1)}, u32[]{:S(2)}, u32[]{:S(2)}) %collective-permute-start.3) | collective-permute-done | bytes 221216 | tf_op jit(solution)/shard_map/ppermute | solution.py:476
  27.8 0.0 copy-done.2
  27.9 3.3 %shard_map.133 = (f32[72,8,256]{2,1,0:T(8,128)S(1)}, f32[72,8,256]{2,1,0:T(8,128)S(1)}, f32[72,8,384]{2,1,0:T(8,128)S(1)}, f32[1,72,384]{2,1,0:T(8,128)S(1)}, f32[1,72,384]{2,1,0:T(8,128)S(1)}) custom-call(f32[72,8,256]{2,1,0:T(8,128)S(1)} %copy-done.2, f32[72,8,256]{2,1,0:T(8,128)S(1)} %copy-done.4, f32[72,8,256]{2,1,0:T(8,128)S(1)} %copy-done.6, ...), custom_call_target="tpu_custom_call" | custom-call | flops 10000000 | bytes 4000000 | tf_op jit(solution)/shard_map/pallas_call | solution.py:453
  31.1 0.7 collective-permute-start.4
  31.8 1.3 %collective-permute-start.5 = (f32[1,72,384]{2,1,0:T(8,128)S(1)}, f32[1,72,384]{2,1,0:T(8,128)S(1)}, u32[]{:S(2)}, u32[]{:S(2)}) collective-permute-start(f32[1,72,384]{2,1,0:T(8,128)S(1)} %get-tuple-element.41), channel_id=1, source_target_pairs={{0,24},{1,25},{2,26},{3,27},{4,28},{5,29},{6,30},{7,31},{8,0},{9,1... | collective-permute-start | bytes 331784 | tf_op jit(solution)/shard_map/ppermute | solution.py:476
  33.2 0.1 pad_add_fusion.place_ref
  33.2 2.3 %collective-permute-done.4.up_ref = f32[1,72,384]{2,1,0:T(8,128)S(1)} collective-permute-done((f32[1,72,384]{2,1,0:T(8,128)S(1)}, f32[1,72,384]{2,1,0:T(8,128)S(1)}, u32[]{:S(2)}, u32[]{:S(2)}) %collective-permute-start.4) | collective-permute-done | bytes 110624 | tf_op jit(solution)/shard_map/ppermute | solution.py:476
  35.5 0.4 collective-permute-done.5.down_ref
  35.9 2.0 %shard_map.134 = (f32[72,8,256]{2,1,0:T(8,128)S(1)}, f32[128,256]{1,0:T(8,128)S(1)}) custom-call(f32[72,8,256]{2,1,0:T(8,128)S(1)} %copy-done.2, f32[72,8,256]{2,1,0:T(8,128)S(1)} %get-tuple-element.37.state_ref, f32[72,8,256]{2,1,0:T(8,128)S(1)} %get-tuple-element.38.smooth_ref, f32[72,8,384]{2,1,0:T(8,128)S(1)} %get-tuple-element.39.tend_ref, ...), custom_call_target="tpu_custom_call" | custom-call | flops 10000000 | bytes 4000000 | tf_op jit(solution)/shard_map/pallas_call | solution.py:453
  38.0 0.1 broadcast_in_dim.13.growth_ref
  38.1 61.4 %shard_map.135 = (bf16[128,33,256]{2,1,0:T(8,128)(2,1)S(1)}, f32[16,128]{1,0:T(8,128)S(1)}, bf16[32,16,128]{2,1,0:T(8,128)(2,1)S(1)}) custom-call(s32[128]{0:T(128)S(1)} %get-tuple-element.56.order_ref, s32[128]{0:T(128)S(1)} %get-tuple-element.55.count_ref, s32[3]{0:T(128)S(1)} %pad_add_fusion.place_ref, bf16[128,33,256]{2,1,0:T(8,128)(2,1)S(1)} %copy.16.drops_ref, ...), custom_call_target="tpu_custom_call" | custom-call | flops 10000000000 | bytes 4000000 | tf_op jit(solution)/shard_map/pallas_call | solution.py:453
  99.5 0.0 copy-start.7
  99.5 0.6 copy-done.7
  100.2 3.1 %all-to-all-start = ((bf16[32,16,128]{2,1,0:T(8,128)(2,1)}), bf16[32,16,128]{2,1,0:T(8,128)(2,1)S(1)}, u32[]{:S(2)}, u32[]{:S(2)}) async-start(bf16[32,16,128]{2,1,0:T(8,128)(2,1)} %copy-done.7), calls=%async_computation | async-start | bytes 262144 | tf_op jit(solution)/shard_map/all_to_all | solution.py:583
  103.4 0.1 stack.41.around_ref
  103.5 1.8 %copy.17 = bf16[128,33,256]{2,0,1:T(8,128)(2,1)} copy(bf16[128,33,256]{2,1,0:T(8,128)(2,1)S(1)} %get-tuple-element.53) | data formatting | bytes 4325376
  105.3 5.8 %all-to-all-done.got_ref = bf16[32,16,128]{2,1,0:T(8,128)(2,1)S(1)} async-done(((bf16[32,16,128]{2,1,0:T(8,128)(2,1)}), bf16[32,16,128]{2,1,0:T(8,128)(2,1)S(1)}, u32[]{:S(2)}, u32[]{:S(2)}) %all-to-all-start) | async-done | bytes 131104 | tf_op jit(solution)/shard_map/all_to_all | solution.py:583
  111.1 2.3 %shard_map.136 = (f32[72,8,256]{2,1,0:T(8,128)}, f32[16,256]{1,0:T(8,128)}) custom-call(s32[8]{0:T(128)S(1)} %stack.41.around_ref, f32[72,8,256]{2,1,0:T(8,128)S(1)} %get-tuple-element.42.base_ref, f32[16,128]{1,0:T(8,128)S(1)} %get-tuple-element.44.own_ref, bf16[32,16,128]{2,1,0:T(8,128)(2,1)S(1)} %all-to-all-done.got_ref, f32[72,16]{1,0:T(8,128)S(1)} %copy-done.8), custom_call_target="tpu_custom_call" | custom-call | flops 10000000 | bytes 4000000 | tf_op jit(solution)/shard_map/pallas_call | solution.py:453
  (14 shorter events, 0.1 us)
Async XLA Ops:
  0.6 11.4 %copy-start = (bf16[33,1089]{1,0:T(8,128)(2,1)S(1)}, bf16[33,1089]{1,0:T(8,128)(2,1)}, u32[]{:S(2)}) copy-start(bf16[33,1089]{1,0:T(8,128)(2,1)} %param.17) | copy-start | bytes 215626
  0.6 1.1 copy-start.1
  1.7 1.1 copy-start.3
  2.8 1.1 copy-start.5
  5.9 9.5 %copy-start.10 = (s32[128]{0:T(128)S(1)}, s32[128]{0:T(128)}, u32[]{:S(2)}) copy-start(s32[128]{0:T(128)} %param.16) | copy-start | bytes 1540
  6.0 13.0 %collective-permute-start = (f32[18,8,128]{2,1,0:T(8,128)S(1)}, f32[18,8,128]{2,1,0:T(8,128)S(1)}, u32[]{:S(2)}, u32[]{:S(2)}) collective-permute-start(f32[18,8,128]{2,1,0:T(8,128)S(1)} %get-tuple-element.27), channel_id=1, source_target_pairs={{0,1},{1,2},{2,3},{3,4},{4,5},{5,6},{6,7},{7,0},{8,9},{9,10},{10,1... | collective-permute-start | bytes 221192 | tf_op jit(solution)/shard_map/ppermute | solution.py:476
  9.0 10.1 %collective-permute-start.1 = (f32[18,8,128]{2,1,0:T(8,128)S(1)}, f32[18,8,128]{2,1,0:T(8,128)S(1)}, u32[]{:S(2)}, u32[]{:S(2)}) collective-permute-start(f32[18,8,128]{2,1,0:T(8,128)S(1)} %get-tuple-element.28), channel_id=1, source_target_pairs={{0,7},{1,0},{2,1},{3,2},{4,3},{5,4},{6,5},{7,6},{8,15},{9,8},{10,9... | collective-permute-start | bytes 221192 | tf_op jit(solution)/shard_map/ppermute | solution.py:476
  15.8 3.1 %copy-start.11 = (f32[33]{0:T(128)S(1)}, f32[33]{0:T(128)}, u32[]{:S(2)}) copy-start(f32[33]{0:T(128)} %param.18) | copy-start | bytes 400
  15.8 3.1 %copy-start.12 = (s32[128,1]{0,1:T(1,128)S(1)}, s32[128,1]{0,1:T(1,128)}, u32[]{:S(2)}) copy-start(s32[128,1]{0,1:T(1,128)} %param.15) | copy-start | bytes 1540
  15.8 12.0 %copy-start.2 = (f32[72,8,256]{2,1,0:T(8,128)S(1)}, f32[72,8,256]{2,1,0:T(8,128)}, u32[]{:S(2)}) copy-start(f32[72,8,256]{2,1,0:T(8,128)} %q_ref.5) | copy-start | bytes 1769476
  15.9 12.0 %copy-start.4 = (f32[72,8,256]{2,1,0:T(8,128)S(1)}, f32[72,8,256]{2,1,0:T(8,128)}, u32[]{:S(2)}) copy-start(f32[72,8,256]{2,1,0:T(8,128)} %u_ref.3) | copy-start | bytes 1769476
  15.9 12.0 %copy-start.6 = (f32[72,8,256]{2,1,0:T(8,128)S(1)}, f32[72,8,256]{2,1,0:T(8,128)}, u32[]{:S(2)}) copy-start(f32[72,8,256]{2,1,0:T(8,128)} %v_ref.3) | copy-start | bytes 1769476
  19.0 16.9 %copy-start.9 = (f32[16,72]{1,0:T(8,128)S(1)}, f32[16,72]{1,0:T(8,128)}, u32[]{:S(2)}) copy-start(f32[16,72]{1,0:T(8,128)} %constant.64.clone.down_map_ref) | copy-start | bytes 13828
  20.9 5.8 %collective-permute-start.2 = (f32[2,72,384]{2,1,0:T(8,128)S(1)}, f32[2,72,384]{2,1,0:T(8,128)S(1)}, u32[]{:S(2)}, u32[]{:S(2)}) collective-permute-start(f32[2,72,384]{2,1,0:T(8,128)S(1)} %get-tuple-element.35), channel_id=1, source_target_pairs={{0,8},{1,9},{2,10},{3,11},{4,12},{5,13},{6,14},{7,15},{8,16},{9,17... | collective-permute-start | bytes 663560 | tf_op jit(solution)/shard_map/ppermute | solution.py:476
  21.0 6.9 %collective-permute-start.3 = (f32[2,72,384]{2,1,0:T(8,128)S(1)}, f32[2,72,384]{2,1,0:T(8,128)S(1)}, u32[]{:S(2)}, u32[]{:S(2)}) collective-permute-start(f32[2,72,384]{2,1,0:T(8,128)S(1)} %get-tuple-element.36), channel_id=1, source_target_pairs={{0,24},{1,25},{2,26},{3,27},{4,28},{5,29},{6,30},{7,31},{8,0},{9,1... | collective-permute-start | bytes 663560 | tf_op jit(solution)/shard_map/ppermute | solution.py:476
  31.1 4.4 %collective-permute-start.4 = (f32[1,72,384]{2,1,0:T(8,128)S(1)}, f32[1,72,384]{2,1,0:T(8,128)S(1)}, u32[]{:S(2)}, u32[]{:S(2)}) collective-permute-start(f32[1,72,384]{2,1,0:T(8,128)S(1)} %get-tuple-element.40), channel_id=1, source_target_pairs={{0,8},{1,9},{2,10},{3,11},{4,12},{5,13},{6,14},{7,15},{8,16},{9,17... | collective-permute-start | bytes 331784 | tf_op jit(solution)/shard_map/ppermute | solution.py:476
  31.8 4.1 %collective-permute-start.5 = (f32[1,72,384]{2,1,0:T(8,128)S(1)}, f32[1,72,384]{2,1,0:T(8,128)S(1)}, u32[]{:S(2)}, u32[]{:S(2)}) collective-permute-start(f32[1,72,384]{2,1,0:T(8,128)S(1)} %get-tuple-element.41), channel_id=1, source_target_pairs={{0,24},{1,25},{2,26},{3,27},{4,28},{5,29},{6,30},{7,31},{8,0},{9,1... | collective-permute-start | bytes 331784 | tf_op jit(solution)/shard_map/ppermute | solution.py:476
  99.5 0.7 copy-start.7
  100.2 10.9 %all-to-all-start = ((bf16[32,16,128]{2,1,0:T(8,128)(2,1)}), bf16[32,16,128]{2,1,0:T(8,128)(2,1)S(1)}, u32[]{:S(2)}, u32[]{:S(2)}) async-start(bf16[32,16,128]{2,1,0:T(8,128)(2,1)} %copy-done.7), calls=%async_computation | async-start | bytes 262144 | tf_op jit(solution)/shard_map/all_to_all | solution.py:583
  103.5 7.6 %copy-start.8 = (f32[72,16]{1,0:T(8,128)S(1)}, f32[72,16]{1,0:T(8,128)}, u32[]{:S(2)}) copy-start(f32[72,16]{1,0:T(8,128)} %constant.66.clone.up_map_ref) | copy-start | bytes 13828
where the time goes:
time: 113 us
  Pallas kernels  74.6 us (66%)
  waiting for transfers between devices  13.6 us (12%)
  starting transfers between devices  13.1 us (12%)
  local copies, waits for them, and re-layouts  8.93 us (8%)
  matrix products  1.68 us (1%)
    pallas_call x7, Pallas kernels, call(): pl.pallas_call(kernel, out_shape=[jax.ShapeDtypeStruct(s, t) for s, t in...  74.6 us
    ppermute x6, starting transfers between devices, shift(): return lax.ppermute(value, ('gcm', 'crm'), pairs)  9.91 us
    unnamed x28, local copies, waits for them, and re-layouts  8.76 us
    ppermute x6, waiting for transfers between devices, shift(): return lax.ppermute(value, ('gcm', 'crm'), pairs)  7.84 us
    all_to_all x1, waiting for transfers between devices, shards(): lax.all_to_all(send, ('gcm', 'crm'), split_axis=0, concat_axis=0, tiled=T...  5.76 us
    all_to_all x1, starting transfers between devices, shards(): lax.all_to_all(send, ('gcm', 'crm'), split_axis=0, concat_axis=0, tiled=T...  3.15 us
  transfers between devices with their start and end apart: 7, of which 5 were waited for; matrix products, arithmetic and copies ran while one was open for 6% of the time, Pallas kernels for 1%

commit v1 on v0

--- a/solution.py
+++ b/solution.py
@@ -264,38 +264,34 @@
 
 
 def crm_kernel(
-    order_ref, count_ref, place_ref, drops_ref, cell_ref, slot_ref, coef_ref, tail_coef_ref,
-    growth_ref,
-    final_ref, heat_ref, send_ref, state_ref, pair_ref, tail_ref, heat_cell_ref, echo_cell_ref,
+    order_ref, count_ref, place_ref, drops_ref, cell_ref, slot_ref, coef_ref, growth_ref,
+    final_ref, heat_ref, send_ref, state_ref, pair_ref, twice_ref, heat_cell_ref, echo_cell_ref,
 ):
     bins = drops_ref.shape[1]
     cells = drops_ref.shape[2]
     cols = drops_ref.shape[0]
     coef = coef_ref[...]
-    tail_coef = tail_coef_ref[...]
     growth = growth_ref[...]
     state_ref[...] = jnp.zeros(state_ref.shape, F32)
     mass = (iota((40, cells), 0) + 1).astype(F32) / F32(bins)
 
-    def grow(k, which):
+    def grow(k, which, zero):
         grown = state_ref[k] + growth * cell_ref[pl.ds(which, 1), :]
         for h in range(cells // 128):
             cut = slice(128 * h, 128 * h + 128)
             g = grown[0:32, cut]
             last = grown[32:40, cut]
-            for s in range(8):
-                rolled = g if s == 0 else pltpu.roll(g, 32 - s, 0)
-                for a in range(2):
-                    other = rolled
-                    if a:
-                        other = jnp.concatenate([rolled[8:], rolled[:8]], axis=0)
-                    d = 8 * a + s
-                    pair_ref[k, 32 * d : 32 * d + 32, cut] = (g * other).astype(BF16)
-            at = 64 * (k % 4)
-            tail_ref[k // 4, at : at + 16, cut] = (g[0:16] * g[16:32]).astype(BF16)
-            tail_ref[k // 4, at + 16 : at + 48, cut] = (g * last[0:1]).astype(BF16)
+            twice_ref[2 * k + h, 0:32, :] = g
+            twice_ref[2 * k + h, 32:48, :] = g[0:16]
+            for d in range(16):
+                other = g if d % 8 == 0 else twice_ref[2 * k + h, pl.ds(zero + d, 32), :]
+                if d == 8:
+                    other = jnp.concatenate([g[8:], g[:8]], axis=0)
+                pair_ref[k, 32 * d : 32 * d + 32, cut] = (g * other).astype(BF16)
+            pair_ref[k, 512:528, cut] = (g[0:16] * g[16:32]).astype(BF16)
+            pair_ref[k, 528:560, cut] = (g * last[0:1]).astype(BF16)
             tail = jnp.concatenate([last * last, jnp.zeros((8, 128), F32)], axis=0)
-            tail_ref[k // 4, at + 48 : at + 64, cut] = tail.astype(BF16)
+            pair_ref[k, 560:576, cut] = tail.astype(BF16)
         return grown
 
     def group(index, carry):
@@ -306,15 +302,11 @@
             state_ref[k, 0:bins, :] = drops_ref[which[k]].astype(F32)
 
         def step(s, c):
-            for q in range(GROUP // 4):
-                grown = [grow(4 * q + k, which[4 * q + k]) for k in range(4)]
-                tails = jnp.dot(tail_coef, tail_ref[q], preferred_element_type=F32)
-                for k in range(4):
-                    slot = 4 * q + k
-                    change = jnp.dot(coef, pair_ref[slot], preferred_element_type=F32)
-                    change = change + tails[80 * k : 80 * k + 80]
-                    moved = grown[k] + (change[0:40] + change[40:80])
-                    state_ref[slot] = jnp.where(s < count[slot], moved, state_ref[slot])
+            for k in range(GROUP):
+                grown = grow(k, which[k], place_ref[3])
+                change = jnp.dot(coef, pair_ref[k], preferred_element_type=F32)
+                moved = grown + (change[0:40] + change[40:80])
+                state_ref[k] = jnp.where(s < count[k], moved, state_ref[k])
             return c
 
         lax.fori_loop(0, count[0], step, 0)
@@ -558,25 +550,21 @@
     fine = coef - coarse
     pad = ((0, 40 - bins), (0, 0))
     coef = jnp.concatenate([jnp.pad(coarse, pad), jnp.pad(fine, pad)], axis=0).astype(BF16)
-    tail = coef[:, 512:]
-    tail_coef = jnp.concatenate(
-        [jnp.pad(tail, ((0, 0), (64 * k, 192 - 64 * k))) for k in range(4)], axis=0
-    )
     growth_rows = jnp.broadcast_to(jnp.pad(growth, (0, 40 - bins))[:, None], (40, cells))
     n_gcm = lax.axis_size("gcm")
     n_crm = lax.axis_size("crm")
     g = lax.axis_index("gcm").astype(jnp.int32)
     c = lax.axis_index("crm").astype(jnp.int32)
-    place = jnp.stack([g, jnp.int32(n_gcm), jnp.int32(n_crm)])
+    place = jnp.stack([g, jnp.int32(n_gcm), jnp.int32(n_crm), jnp.int32(0)])
 
     final, heat, send = call(
         crm_kernel,
         [((col_total, bins, cells), BF16), ((CRM_LEV, col_total), F32),
          ((devices, CRM_LEV, 128), BF16)],
         [("s", order), ("s", ordered), ("s", place)]
-        + v(drops, cell_forcing, slot_of[None, :], coef[:, :512], tail_coef, growth_rows),
-        [((GROUP, 40, cells), F32), ((GROUP, 512, cells), BF16),
-         ((GROUP // 4, 256, cells), BF16),
+        + v(drops, cell_forcing, slot_of[None, :], coef, growth_rows),
+        [((GROUP, 40, cells), F32), ((GROUP, 576, cells), BF16),
+         ((2 * GROUP, 48, 128), F32),
          ((col_total, cells), F32), ((col_total, cells), F32)],
         flops=10_000_000_000,
     )

time: 113 us -> 102 us (0.903); the launches traced: 113 us -> 101 us
  Pallas kernels: 74.6 us -> 23.6 us
  starting transfers between devices: 13.1 us -> 54.5 us
  local copies, waits for them, and re-layouts: 8.93 us -> 7.21 us
  matrix products: 1.68 us -> 0.33 us
    pallas_call x7, Pallas kernels: 74.6 us -> 23.6 us  [call(): pl.pallas_call(kernel, out_shape=[jax.ShapeDtypeStruct(s, t) for s, t in...]
    all_to_all x1, starting transfers between devices: 3.15 us -> 44.6 us  [shards(): lax.all_to_all(send, ('gcm', 'crm'), split_axis=0, concat_axis=0, tiled=T...]
    unnamed x28 -> x32, local copies, waits for them, and re-layouts: 8.76 us -> 7.05 us
    dot_general x1, matrix products: 1.68 us -> 0.33 us  [shards(): coef = DT_CRM * jnp.dot(collision, table, preferred_element_type=F32)]
  transfers between devices with their start and end apart: 7 -> 7, of which waited for: 5 -> 5; matrix products, arithmetic and copies ran while one was open for 6% -> 4% of each run, Pallas kernels for 1% -> 2%
where the time goes in v1:
time: 102 us; the launch traced here: 101 us
  starting transfers between devices  54.5 us (53%)
  Pallas kernels  23.6 us (23%)
  waiting for transfers between devices  13.6 us (13%)
  local copies, waits for them, and re-layouts  7.21 us (7%)
    all_to_all x1, starting transfers between devices, shards(): lax.all_to_all(send, ('gcm', 'crm'), split_axis=0, concat_axis=0, tiled=T...  44.6 us
    pallas_call x7, Pallas kernels, call(): pl.pallas_call(kernel, out_shape=[jax.ShapeDtypeStruct(s, t) for s, t in...  23.6 us
    ppermute x6, starting transfers between devices, shift(): return lax.ppermute(value, ('gcm', 'crm'), pairs)  9.91 us
    ppermute x6, waiting for transfers between devices, shift(): return lax.ppermute(value, ('gcm', 'crm'), pairs)  7.84 us
    unnamed x32, local copies, waits for them, and re-layouts  7.05 us
    all_to_all x1, waiting for transfers between devices, shards(): lax.all_to_all(send, ('gcm', 'crm'), split_axis=0, concat_axis=0, tiled=T...  5.76 us
  transfers between devices with their start and end apart: 7, of which 5 were waited for; matrix products, arithmetic and copies ran while one was open for 4% of the time, Pallas kernels for 2%

profile of v1, /device:TPU:0, one launch (start us, length us, event | category | flops | bytes accessed | tf_op | source)
XLA Modules:
  0.0 100.7 jit_solution(1377987941163845485)
XLA Ops:
  0.6 0.0 copy-start
  0.6 0.0 copy-start.1
  0.7 1.1 %copy-done.1 = f32[72,8,256]{2,1,0:T(8,128)S(1)} copy-done((f32[72,8,256]{2,1,0:T(8,128)S(1)}, f32[72,8,256]{2,1,0:T(8,128)}, u32[]{:S(2)}) %copy-start.1) | copy-done | bytes 589848
  1.7 1.1 %copy-done.3 = f32[72,8,256]{2,1,0:T(8,128)S(1)} copy-done((f32[72,8,256]{2,1,0:T(8,128)S(1)}, f32[72,8,256]{2,1,0:T(8,128)}, u32[]{:S(2)}) %copy-start.3) | copy-done | bytes 589848
  2.8 1.1 %copy-done.5 = f32[72,8,256]{2,1,0:T(8,128)S(1)} copy-done((f32[72,8,256]{2,1,0:T(8,128)S(1)}, f32[72,8,256]{2,1,0:T(8,128)}, u32[]{:S(2)}) %copy-start.5) | copy-done | bytes 589848
  3.9 2.1 %shard_map.131 = (f32[18,8,128]{2,1,0:T(8,128)S(1)}, f32[18,8,128]{2,1,0:T(8,128)S(1)}) custom-call(f32[72,8,256]{2,1,0:T(8,128)S(1)} %copy-done.1, f32[72,8,256]{2,1,0:T(8,128)S(1)} %copy-done.3, f32[72,8,256]{2,1,0:T(8,128)S(1)} %copy-done.5), custom_call_target="tpu_custom_call" | custom-call | flops 10000000 | bytes 4000000 | tf_op jit(solution)/shard_map/pallas_call | solution.py:445
  6.0 3.0 %collective-permute-start = (f32[18,8,128]{2,1,0:T(8,128)S(1)}, f32[18,8,128]{2,1,0:T(8,128)S(1)}, u32[]{:S(2)}, u32[]{:S(2)}) collective-permute-start(f32[18,8,128]{2,1,0:T(8,128)S(1)} %get-tuple-element.27), channel_id=1, source_target_pairs={{0,1},{1,2},{2,3},{3,4},{4,5},{5,6},{6,7},{7,0},{8,9},{9,10},{10,1... | collective-permute-start | bytes 221192 | tf_op jit(solution)/shard_map/ppermute | solution.py:468
  8.9 3.1 %collective-permute-start.1 = (f32[18,8,128]{2,1,0:T(8,128)S(1)}, f32[18,8,128]{2,1,0:T(8,128)S(1)}, u32[]{:S(2)}, u32[]{:S(2)}) collective-permute-start(f32[18,8,128]{2,1,0:T(8,128)S(1)} %get-tuple-element.28), channel_id=1, source_target_pairs={{0,7},{1,0},{2,1},{3,2},{4,3},{5,4},{6,5},{7,6},{8,15},{9,8},{10,9... | collective-permute-start | bytes 221192 | tf_op jit(solution)/shard_map/ppermute | solution.py:468
  12.0 1.6 %shard_map.130 = (f32[72,8,256]{2,1,0:T(8,128)S(1)}, f32[2,72,256]{2,1,0:T(8,128)S(1)}, f32[2,72,256]{2,1,0:T(8,128)S(1)}) custom-call(f32[72,8,256]{2,1,0:T(8,128)S(1)} %copy-done.1, f32[72,8,256]{2,1,0:T(8,128)S(1)} %copy-done.3, f32[72,8,256]{2,1,0:T(8,128)S(1)} %copy-done.5), custom_call_target="tpu_custom_call" | custom-call | flops 10000000 | bytes 4000000 | tf_op jit(solution)/shard_map/pallas_call | solution.py:445
  13.7 0.0 copy-done.12
  13.7 0.2 convert_reduce_fusion.1
  13.8 0.1 select_reduce_fusion
  14.0 0.0 copy-done.10
  14.0 0.0 copy-start.13
  14.0 0.0 copy-start.11
  14.0 0.0 copy-start.14
  14.0 1.3 %copy.16.drops_ref = bf16[128,33,256]{2,1,0:T(8,128)(2,1)S(1)} copy(bf16[128,33,256]{2,0,1:T(8,128)(2,1)S(1)} %copy-done.10) | data formatting | bytes 4325376 | tf_op args[3]
  15.3 0.0 copy-start.2
  15.3 0.0 copy-start.4
  15.3 0.0 copy-start.6
  15.4 0.3 reduce-precision_convert_fusion
  15.7 0.1 convert_reduce_fusion
  15.8 0.0 collective-permute-done.left_ref
  15.8 0.0 collective-permute-done.1.right_ref
  15.9 0.0 copy-start.9
  15.9 1.9 %shard_map.132 = (f32[72,8,128]{2,1,0:T(8,128)S(1)}, f32[72,8,128]{2,1,0:T(8,128)S(1)}, f32[72,8,128]{2,1,0:T(8,128)S(1)}, f32[72,8,128]{2,1,0:T(8,128)S(1)}, f3...) custom-call(f32[18,8,128]{2,1,0:T(8,128)S(1)} %collective-permute-done.left_ref, ...), custom_call_target="tpu_custom_call" | custom-call | flops 10000000 | bytes 4000000 | tf_op jit(solution)/shard_map/pallas_call | solution.py:445
  17.7 0.1 collective-permute-start.2
  17.8 1.7 %collective-permute-start.3 = (f32[2,72,384]{2,1,0:T(8,128)S(1)}, f32[2,72,384]{2,1,0:T(8,128)S(1)}, u32[]{:S(2)}, u32[]{:S(2)}) collective-permute-start(f32[2,72,384]{2,1,0:T(8,128)S(1)} %get-tuple-element.36), channel_id=1, source_target_pairs={{0,24},{1,25},{2,26},{3,27},{4,28},{5,29},{6,30},{7,31},{8,0},{9,1... | collective-permute-start | bytes 663560 | tf_op jit(solution)/shard_map/ppermute | solution.py:468
  19.5 4.0 %collective-permute-done.2.up_ref = f32[2,72,384]{2,1,0:T(8,128)S(1)} collective-permute-done((f32[2,72,384]{2,1,0:T(8,128)S(1)}, f32[2,72,384]{2,1,0:T(8,128)S(1)}, u32[]{:S(2)}, u32[]{:S(2)}) %collective-permute-start.2) | collective-permute-done | bytes 221216 | tf_op jit(solution)/shard_map/ppermute | solution.py:468
  23.5 1.2 %collective-permute-done.3.down_ref = f32[2,72,384]{2,1,0:T(8,128)S(1)} collective-permute-done((f32[2,72,384]{2,1,0:T(8,128)S(1)}, f32[2,72,384]{2,1,0:T(8,128)S(1)}, u32[]{:S(2)}, u32[]{:S(2)}) %collective-permute-start.3) | collective-permute-done | bytes 221216 | tf_op jit(solution)/shard_map/ppermute | solution.py:468
  24.7 0.0 copy-done.4
  24.7 3.3 %shard_map.133 = (f32[72,8,256]{2,1,0:T(8,128)S(1)}, f32[72,8,256]{2,1,0:T(8,128)S(1)}, f32[72,8,384]{2,1,0:T(8,128)S(1)}, f32[1,72,384]{2,1,0:T(8,128)S(1)}, f32[1,72,384]{2,1,0:T(8,128)S(1)}) custom-call(f32[72,8,256]{2,1,0:T(8,128)S(1)} %copy-done.2, f32[72,8,256]{2,1,0:T(8,128)S(1)} %copy-done.4, f32[72,8,256]{2,1,0:T(8,128)S(1)} %copy-done.6, ...), custom_call_target="tpu_custom_call" | custom-call | flops 10000000 | bytes 4000000 | tf_op jit(solution)/shard_map/pallas_call | solution.py:445
  28.0 0.7 collective-permute-start.4
  28.7 1.3 %collective-permute-start.5 = (f32[1,72,384]{2,1,0:T(8,128)S(1)}, f32[1,72,384]{2,1,0:T(8,128)S(1)}, u32[]{:S(2)}, u32[]{:S(2)}) collective-permute-start(f32[1,72,384]{2,1,0:T(8,128)S(1)} %get-tuple-element.41), channel_id=1, source_target_pairs={{0,24},{1,25},{2,26},{3,27},{4,28},{5,29},{6,30},{7,31},{8,0},{9,1... | collective-permute-start | bytes 331784 | tf_op jit(solution)/shard_map/ppermute | solution.py:468
  30.0 0.1 pad_add_fusion.place_ref
  30.1 2.3 %collective-permute-done.4.up_ref = f32[1,72,384]{2,1,0:T(8,128)S(1)} collective-permute-done((f32[1,72,384]{2,1,0:T(8,128)S(1)}, f32[1,72,384]{2,1,0:T(8,128)S(1)}, u32[]{:S(2)}, u32[]{:S(2)}) %collective-permute-start.4) | collective-permute-done | bytes 110624 | tf_op jit(solution)/shard_map/ppermute | solution.py:468
  32.4 0.4 collective-permute-done.5.down_ref
  32.8 2.0 %shard_map.134 = (f32[72,8,256]{2,1,0:T(8,128)S(1)}, f32[128,256]{1,0:T(8,128)S(1)}) custom-call(f32[72,8,256]{2,1,0:T(8,128)S(1)} %copy-done.2, f32[72,8,256]{2,1,0:T(8,128)S(1)} %get-tuple-element.37.state_ref, f32[72,8,256]{2,1,0:T(8,128)S(1)} %get-tuple-element.38.smooth_ref, f32[72,8,384]{2,1,0:T(8,128)S(1)} %get-tuple-element.39.tend_ref, ...), custom_call_target="tpu_custom_call" | custom-call | flops 10000000 | bytes 4000000 | tf_op jit(solution)/shard_map/pallas_call | solution.py:445
  34.8 0.1 broadcast_in_dim.13.growth_ref
  34.9 10.4 %shard_map.135 = (bf16[128,33,256]{2,1,0:T(8,128)(2,1)S(1)}, f32[16,128]{1,0:T(8,128)S(1)}, bf16[32,16,128]{2,1,0:T(8,128)(2,1)S(1)}) custom-call(s32[128]{0:T(128)S(1)} %get-tuple-element.56.order_ref, s32[128]{0:T(128)S(1)} %get-tuple-element.55.count_ref, s32[4]{0:T(128)S(1)} %pad_add_fusion.place_ref, bf16[128,33,256]{2,1,0:T(8,128)(2,1)S(1)} %copy.16.drops_ref, ...), custom_call_target="tpu_custom_call" | custom-call | flops 10000000000 | bytes 4000000 | tf_op jit(solution)/shard_map/pallas_call | solution.py:445
  45.4 0.0 copy-start.7
  45.4 0.6 copy-done.7
  46.0 44.6 %all-to-all-start = ((bf16[32,16,128]{2,1,0:T(8,128)(2,1)}), bf16[32,16,128]{2,1,0:T(8,128)(2,1)S(1)}, u32[]{:S(2)}, u32[]{:S(2)}) async-start(bf16[32,16,128]{2,1,0:T(8,128)(2,1)} %copy-done.7), calls=%async_computation | async-start | bytes 262144 | tf_op jit(solution)/shard_map/all_to_all | solution.py:571
  90.7 0.1 stack.41.around_ref
  90.8 1.8 %copy.17 = bf16[128,33,256]{2,0,1:T(8,128)(2,1)} copy(bf16[128,33,256]{2,1,0:T(8,128)(2,1)S(1)} %get-tuple-element.53) | data formatting | bytes 4325376
  92.6 5.8 %all-to-all-done.got_ref = bf16[32,16,128]{2,1,0:T(8,128)(2,1)S(1)} async-done(((bf16[32,16,128]{2,1,0:T(8,128)(2,1)}), bf16[32,16,128]{2,1,0:T(8,128)(2,1)S(1)}, u32[]{:S(2)}, u32[]{:S(2)}) %all-to-all-start) | async-done | bytes 131104 | tf_op jit(solution)/shard_map/all_to_all | solution.py:571
  98.4 0.0 copy-done.8
  98.4 2.3 %shard_map.136 = (f32[72,8,256]{2,1,0:T(8,128)}, f32[16,256]{1,0:T(8,128)}) custom-call(s32[8]{0:T(128)S(1)} %stack.41.around_ref, f32[72,8,256]{2,1,0:T(8,128)S(1)} %get-tuple-element.42.base_ref, f32[16,128]{1,0:T(8,128)S(1)} %get-tuple-element.44.own_ref, bf16[32,16,128]{2,1,0:T(8,128)(2,1)S(1)} %all-to-all-done.got_ref, f32[72,16]{1,0:T(8,128)S(1)} %copy-done.8), custom_call_target="tpu_custom_call" | custom-call | flops 10000000 | bytes 4000000 | tf_op jit(solution)/shard_map/pallas_call | solution.py:445
  (15 shorter events, 0.0 us)
Async XLA Ops:
  0.6 14.7 %copy-start = (bf16[33,1089]{1,0:T(8,128)(2,1)S(1)}, bf16[33,1089]{1,0:T(8,128)(2,1)}, u32[]{:S(2)}) copy-start(bf16[33,1089]{1,0:T(8,128)(2,1)} %param.17) | copy-start | bytes 215626
  0.6 1.1 %copy-start.1 = (f32[72,8,256]{2,1,0:T(8,128)S(1)}, f32[72,8,256]{2,1,0:T(8,128)}, u32[]{:S(2)}) copy-start(f32[72,8,256]{2,1,0:T(8,128)} %q_ref.5) | copy-start | bytes 1769476
  1.7 1.1 %copy-start.3 = (f32[72,8,256]{2,1,0:T(8,128)S(1)}, f32[72,8,256]{2,1,0:T(8,128)}, u32[]{:S(2)}) copy-start(f32[72,8,256]{2,1,0:T(8,128)} %u_ref.3) | copy-start | bytes 1769476
  2.8 1.1 %copy-start.5 = (f32[72,8,256]{2,1,0:T(8,128)S(1)}, f32[72,8,256]{2,1,0:T(8,128)}, u32[]{:S(2)}) copy-start(f32[72,8,256]{2,1,0:T(8,128)} %v_ref.3) | copy-start | bytes 1769476
  3.9 9.8 %copy-start.12 = (s32[128]{0:T(128)S(1)}, s32[128]{0:T(128)}, u32[]{:S(2)}) copy-start(s32[128]{0:T(128)} %param.16) | copy-start | bytes 1540
  3.9 10.1 %copy-start.10 = (bf16[128,33,256]{2,0,1:T(8,128)(2,1)S(1)}, bf16[128,33,256]{2,0,1:T(8,128)(2,1)}, u32[]{:S(2)}) copy-start(bf16[128,33,256]{2,0,1:T(8,128)(2,1)} %param.14) | copy-start | bytes 6488068
  6.0 9.9 %collective-permute-start = (f32[18,8,128]{2,1,0:T(8,128)S(1)}, f32[18,8,128]{2,1,0:T(8,128)S(1)}, u32[]{:S(2)}, u32[]{:S(2)}) collective-permute-start(f32[18,8,128]{2,1,0:T(8,128)S(1)} %get-tuple-element.27), channel_id=1, source_target_pairs={{0,1},{1,2},{2,3},{3,4},{4,5},{5,6},{6,7},{7,0},{8,9},{9,10},{10,1... | collective-permute-start | bytes 221192 | tf_op jit(solution)/shard_map/ppermute | solution.py:468
  8.9 6.9 %collective-permute-start.1 = (f32[18,8,128]{2,1,0:T(8,128)S(1)}, f32[18,8,128]{2,1,0:T(8,128)S(1)}, u32[]{:S(2)}, u32[]{:S(2)}) collective-permute-start(f32[18,8,128]{2,1,0:T(8,128)S(1)} %get-tuple-element.28), channel_id=1, source_target_pairs={{0,7},{1,0},{2,1},{3,2},{4,3},{5,4},{6,5},{7,6},{8,15},{9,8},{10,9... | collective-permute-start | bytes 221192 | tf_op jit(solution)/shard_map/ppermute | solution.py:468
  14.0 1.3 %copy-start.13 = (f32[33]{0:T(128)S(1)}, f32[33]{0:T(128)}, u32[]{:S(2)}) copy-start(f32[33]{0:T(128)} %param.18) | copy-start | bytes 400
  14.0 1.4 %copy-start.11 = (bf16[1089,576]{1,0:T(8,128)(2,1)S(1)}, bf16[1089,576]{1,0:T(8,128)(2,1)}, u32[]{:S(2)}) copy-start(bf16[1089,576]{1,0:T(8,128)(2,1)} %constant.66.clone) | copy-start | bytes 3763588
  14.0 1.7 %copy-start.14 = (s32[128,1]{0,1:T(1,128)S(1)}, s32[128,1]{0,1:T(1,128)}, u32[]{:S(2)}) copy-start(s32[128,1]{0,1:T(1,128)} %param.15) | copy-start | bytes 1540
  15.3 9.4 %copy-start.2 = (f32[72,8,256]{2,1,0:T(8,128)S(1)}, f32[72,8,256]{2,1,0:T(8,128)}, u32[]{:S(2)}) copy-start(f32[72,8,256]{2,1,0:T(8,128)} %q_ref.5) | copy-start | bytes 1769476
  15.3 9.4 %copy-start.4 = (f32[72,8,256]{2,1,0:T(8,128)S(1)}, f32[72,8,256]{2,1,0:T(8,128)}, u32[]{:S(2)}) copy-start(f32[72,8,256]{2,1,0:T(8,128)} %u_ref.3) | copy-start | bytes 1769476
  15.3 9.4 %copy-start.6 = (f32[72,8,256]{2,1,0:T(8,128)S(1)}, f32[72,8,256]{2,1,0:T(8,128)}, u32[]{:S(2)}) copy-start(f32[72,8,256]{2,1,0:T(8,128)} %v_ref.3) | copy-start | bytes 1769476
  15.9 16.9 %copy-start.9 = (f32[16,72]{1,0:T(8,128)S(1)}, f32[16,72]{1,0:T(8,128)}, u32[]{:S(2)}) copy-start(f32[16,72]{1,0:T(8,128)} %constant.65.clone.down_map_ref) | copy-start | bytes 13828
  17.7 5.8 %collective-permute-start.2 = (f32[2,72,384]{2,1,0:T(8,128)S(1)}, f32[2,72,384]{2,1,0:T(8,128)S(1)}, u32[]{:S(2)}, u32[]{:S(2)}) collective-permute-start(f32[2,72,384]{2,1,0:T(8,128)S(1)} %get-tuple-element.35), channel_id=1, source_target_pairs={{0,8},{1,9},{2,10},{3,11},{4,12},{5,13},{6,14},{7,15},{8,16},{9,17... | collective-permute-start | bytes 663560 | tf_op jit(solution)/shard_map/ppermute | solution.py:468
  17.8 6.9 %collective-permute-start.3 = (f32[2,72,384]{2,1,0:T(8,128)S(1)}, f32[2,72,384]{2,1,0:T(8,128)S(1)}, u32[]{:S(2)}, u32[]{:S(2)}) collective-permute-start(f32[2,72,384]{2,1,0:T(8,128)S(1)} %get-tuple-element.36), channel_id=1, source_target_pairs={{0,24},{1,25},{2,26},{3,27},{4,28},{5,29},{6,30},{7,31},{8,0},{9,1... | collective-permute-start | bytes 663560 | tf_op jit(solution)/shard_map/ppermute | solution.py:468
  28.0 4.4 %collective-permute-start.4 = (f32[1,72,384]{2,1,0:T(8,128)S(1)}, f32[1,72,384]{2,1,0:T(8,128)S(1)}, u32[]{:S(2)}, u32[]{:S(2)}) collective-permute-start(f32[1,72,384]{2,1,0:T(8,128)S(1)} %get-tuple-element.40), channel_id=1, source_target_pairs={{0,8},{1,9},{2,10},{3,11},{4,12},{5,13},{6,14},{7,15},{8,16},{9,17... | collective-permute-start | bytes 331784 | tf_op jit(solution)/shard_map/ppermute | solution.py:468
  28.7 4.1 %collective-permute-start.5 = (f32[1,72,384]{2,1,0:T(8,128)S(1)}, f32[1,72,384]{2,1,0:T(8,128)S(1)}, u32[]{:S(2)}, u32[]{:S(2)}) collective-permute-start(f32[1,72,384]{2,1,0:T(8,128)S(1)} %get-tuple-element.41), channel_id=1, source_target_pairs={{0,24},{1,25},{2,26},{3,27},{4,28},{5,29},{6,30},{7,31},{8,0},{9,1... | collective-permute-start | bytes 331784 | tf_op jit(solution)/shard_map/ppermute | solution.py:468
  45.4 0.7 copy-start.7
  46.0 52.4 %all-to-all-start = ((bf16[32,16,128]{2,1,0:T(8,128)(2,1)}), bf16[32,16,128]{2,1,0:T(8,128)(2,1)S(1)}, u32[]{:S(2)}, u32[]{:S(2)}) async-start(bf16[32,16,128]{2,1,0:T(8,128)(2,1)} %copy-done.7), calls=%async_computation | async-start | bytes 262144 | tf_op jit(solution)/shard_map/all_to_all | solution.py:571
  90.8 7.6 %copy-start.8 = (f32[72,16]{1,0:T(8,128)S(1)}, f32[72,16]{1,0:T(8,128)}, u32[]{:S(2)}) copy-start(f32[72,16]{1,0:T(8,128)} %constant.67.clone.up_map_ref) | copy-start | bytes 13828

commit v2 on v1

--- a/solution.py
+++ b/solution.py
@@ -305,7 +305,7 @@
             for k in range(GROUP):
                 grown = grow(k, which[k], place_ref[3])
                 change = jnp.dot(coef, pair_ref[k], preferred_element_type=F32)
-                moved = grown + (change[0:40] + change[40:80])
+                moved = grown + DT_CRM * change[0:40]
                 state_ref[k] = jnp.where(s < count[k], moved, state_ref[k])
             return c
 
@@ -545,11 +545,8 @@
     slot_of = owners * capacity + jnp.sum(same.astype(jnp.int32), axis=0)
     order, ordered = rank_order(counts)
     table = jnp.asarray(pair_table(bins), BF16)
-    coef = DT_CRM * jnp.dot(collision, table, preferred_element_type=F32)
-    coarse = lax.reduce_precision(coef, 8, 7)
-    fine = coef - coarse
-    pad = ((0, 40 - bins), (0, 0))
-    coef = jnp.concatenate([jnp.pad(coarse, pad), jnp.pad(fine, pad)], axis=0).astype(BF16)
+    coef = jnp.dot(collision, table, preferred_element_type=F32)
+    coef = jnp.pad(coef.astype(BF16), ((0, 48 - bins), (0, 0)))
     growth_rows = jnp.broadcast_to(jnp.pad(growth, (0, 40 - bins))[:, None], (40, cells))
     n_gcm = lax.axis_size("gcm")
     n_crm = lax.axis_size("crm")

time: 102 us -> 99.3 us (0.974)
  starting transfers between devices: 54.5 us -> 53 us
    all_to_all x1, starting transfers between devices: 44.6 us -> 43.1 us  [shards(): lax.all_to_all(send, ('gcm', 'crm'), split_axis=0, concat_axis=0, tiled=T...]
where the time goes in v2:
time: 99.3 us; the launch traced here: 98.8 us
  starting transfers between devices  53 us (53%)
  Pallas kernels  23.2 us (23%)
  waiting for transfers between devices  13.6 us (14%)
  local copies, waits for them, and re-layouts  7.23 us (7%)
    all_to_all x1, starting transfers between devices, shards(): lax.all_to_all(send, ('gcm', 'crm'), split_axis=0, concat_axis=0, tiled=T...  43.1 us
    pallas_call x7, Pallas kernels, call(): pl.pallas_call(kernel, out_shape=[jax.ShapeDtypeStruct(s, t) for s, t in...  23.2 us
    ppermute x6, starting transfers between devices, shift(): return lax.ppermute(value, ('gcm', 'crm'), pairs)  9.91 us
    ppermute x6, waiting for transfers between devices, shift(): return lax.ppermute(value, ('gcm', 'crm'), pairs)  7.84 us
    unnamed x32, local copies, waits for them, and re-layouts  7.05 us
    all_to_all x1, waiting for transfers between devices, shards(): lax.all_to_all(send, ('gcm', 'crm'), split_axis=0, concat_axis=0, tiled=T...  5.76 us
  transfers between devices with their start and end apart: 7, of which 5 were waited for; matrix products, arithmetic and copies ran while one was open for 4% of the time, Pallas kernels for 2%

profile of v2, /device:TPU:0, one launch (start us, length us, event | category | flops | bytes accessed | tf_op | source)
XLA Modules:
  0.0 98.8 jit_solution(15068117345945574241)
XLA Ops:
  0.6 0.0 copy-start
  0.6 0.0 copy-start.1
  0.7 1.1 %copy-done.1 = f32[72,8,256]{2,1,0:T(8,128)S(1)} copy-done((f32[72,8,256]{2,1,0:T(8,128)S(1)}, f32[72,8,256]{2,1,0:T(8,128)}, u32[]{:S(2)}) %copy-start.1) | copy-done | bytes 589848
  1.7 1.1 %copy-done.3 = f32[72,8,256]{2,1,0:T(8,128)S(1)} copy-done((f32[72,8,256]{2,1,0:T(8,128)S(1)}, f32[72,8,256]{2,1,0:T(8,128)}, u32[]{:S(2)}) %copy-start.3) | copy-done | bytes 589848
  2.8 1.1 %copy-done.5 = f32[72,8,256]{2,1,0:T(8,128)S(1)} copy-done((f32[72,8,256]{2,1,0:T(8,128)S(1)}, f32[72,8,256]{2,1,0:T(8,128)}, u32[]{:S(2)}) %copy-start.5) | copy-done | bytes 589848
  3.9 2.1 %shard_map.131 = (f32[18,8,128]{2,1,0:T(8,128)S(1)}, f32[18,8,128]{2,1,0:T(8,128)S(1)}) custom-call(f32[72,8,256]{2,1,0:T(8,128)S(1)} %copy-done.1, f32[72,8,256]{2,1,0:T(8,128)S(1)} %copy-done.3, f32[72,8,256]{2,1,0:T(8,128)S(1)} %copy-done.5), custom_call_target="tpu_custom_call" | custom-call | flops 10000000 | bytes 4000000 | tf_op jit(solution)/shard_map/pallas_call | solution.py:445
  6.0 3.0 %collective-permute-start = (f32[18,8,128]{2,1,0:T(8,128)S(1)}, f32[18,8,128]{2,1,0:T(8,128)S(1)}, u32[]{:S(2)}, u32[]{:S(2)}) collective-permute-start(f32[18,8,128]{2,1,0:T(8,128)S(1)} %get-tuple-element.27), channel_id=1, source_target_pairs={{0,1},{1,2},{2,3},{3,4},{4,5},{5,6},{6,7},{7,0},{8,9},{9,10},{10,1... | collective-permute-start | bytes 221192 | tf_op jit(solution)/shard_map/ppermute | solution.py:468
  8.9 3.1 %collective-permute-start.1 = (f32[18,8,128]{2,1,0:T(8,128)S(1)}, f32[18,8,128]{2,1,0:T(8,128)S(1)}, u32[]{:S(2)}, u32[]{:S(2)}) collective-permute-start(f32[18,8,128]{2,1,0:T(8,128)S(1)} %get-tuple-element.28), channel_id=1, source_target_pairs={{0,7},{1,0},{2,1},{3,2},{4,3},{5,4},{6,5},{7,6},{8,15},{9,8},{10,9... | collective-permute-start | bytes 221192 | tf_op jit(solution)/shard_map/ppermute | solution.py:468
  12.0 1.6 %shard_map.130 = (f32[72,8,256]{2,1,0:T(8,128)S(1)}, f32[2,72,256]{2,1,0:T(8,128)S(1)}, f32[2,72,256]{2,1,0:T(8,128)S(1)}) custom-call(f32[72,8,256]{2,1,0:T(8,128)S(1)} %copy-done.1, f32[72,8,256]{2,1,0:T(8,128)S(1)} %copy-done.3, f32[72,8,256]{2,1,0:T(8,128)S(1)} %copy-done.5), custom_call_target="tpu_custom_call" | custom-call | flops 10000000 | bytes 4000000 | tf_op jit(solution)/shard_map/pallas_call | solution.py:445
  13.7 0.0 copy-done.12
  13.7 0.2 convert_reduce_fusion.1
  13.8 0.1 select_reduce_fusion
  14.0 0.0 copy-done.10
  14.0 0.0 copy-start.13
  14.0 0.0 copy-start.11
  14.0 0.0 copy-start.14
  14.0 1.3 %copy.16.drops_ref = bf16[128,33,256]{2,1,0:T(8,128)(2,1)S(1)} copy(bf16[128,33,256]{2,0,1:T(8,128)(2,1)S(1)} %copy-done.10) | data formatting | bytes 4325376 | tf_op args[3]
  15.3 0.0 copy-done.13
  15.3 0.0 copy-start.2
  15.3 0.0 copy-start.4
  15.3 0.0 copy-start.6
  15.4 0.3 fusion
  15.7 0.1 convert_reduce_fusion
  15.8 0.0 collective-permute-done.left_ref
  15.8 0.0 collective-permute-done.1.right_ref
  15.8 0.0 copy-start.9
  15.9 1.9 %shard_map.132 = (f32[72,8,128]{2,1,0:T(8,128)S(1)}, f32[72,8,128]{2,1,0:T(8,128)S(1)}, f32[72,8,128]{2,1,0:T(8,128)S(1)}, f32[72,8,128]{2,1,0:T(8,128)S(1)}, f3...) custom-call(f32[18,8,128]{2,1,0:T(8,128)S(1)} %collective-permute-done.left_ref, ...), custom_call_target="tpu_custom_call" | custom-call | flops 10000000 | bytes 4000000 | tf_op jit(solution)/shard_map/pallas_call | solution.py:445
  17.7 0.1 collective-permute-start.2
  17.8 1.7 %collective-permute-start.3 = (f32[2,72,384]{2,1,0:T(8,128)S(1)}, f32[2,72,384]{2,1,0:T(8,128)S(1)}, u32[]{:S(2)}, u32[]{:S(2)}) collective-permute-start(f32[2,72,384]{2,1,0:T(8,128)S(1)} %get-tuple-element.36), channel_id=1, source_target_pairs={{0,24},{1,25},{2,26},{3,27},{4,28},{5,29},{6,30},{7,31},{8,0},{9,1... | collective-permute-start | bytes 663560 | tf_op jit(solution)/shard_map/ppermute | solution.py:468
  19.5 4.0 %collective-permute-done.2.up_ref = f32[2,72,384]{2,1,0:T(8,128)S(1)} collective-permute-done((f32[2,72,384]{2,1,0:T(8,128)S(1)}, f32[2,72,384]{2,1,0:T(8,128)S(1)}, u32[]{:S(2)}, u32[]{:S(2)}) %collective-permute-start.2) | collective-permute-done | bytes 221216 | tf_op jit(solution)/shard_map/ppermute | solution.py:468
  23.5 1.2 %collective-permute-done.3.down_ref = f32[2,72,384]{2,1,0:T(8,128)S(1)} collective-permute-done((f32[2,72,384]{2,1,0:T(8,128)S(1)}, f32[2,72,384]{2,1,0:T(8,128)S(1)}, u32[]{:S(2)}, u32[]{:S(2)}) %collective-permute-start.3) | collective-permute-done | bytes 221216 | tf_op jit(solution)/shard_map/ppermute | solution.py:468
  24.7 0.0 copy-done.4
  24.7 3.3 %shard_map.133 = (f32[72,8,256]{2,1,0:T(8,128)S(1)}, f32[72,8,256]{2,1,0:T(8,128)S(1)}, f32[72,8,384]{2,1,0:T(8,128)S(1)}, f32[1,72,384]{2,1,0:T(8,128)S(1)}, f32[1,72,384]{2,1,0:T(8,128)S(1)}) custom-call(f32[72,8,256]{2,1,0:T(8,128)S(1)} %copy-done.2, f32[72,8,256]{2,1,0:T(8,128)S(1)} %copy-done.4, f32[72,8,256]{2,1,0:T(8,128)S(1)} %copy-done.6, ...), custom_call_target="tpu_custom_call" | custom-call | flops 10000000 | bytes 4000000 | tf_op jit(solution)/shard_map/pallas_call | solution.py:445
  28.0 0.7 collective-permute-start.4
  28.7 1.3 %collective-permute-start.5 = (f32[1,72,384]{2,1,0:T(8,128)S(1)}, f32[1,72,384]{2,1,0:T(8,128)S(1)}, u32[]{:S(2)}, u32[]{:S(2)}) collective-permute-start(f32[1,72,384]{2,1,0:T(8,128)S(1)} %get-tuple-element.41), channel_id=1, source_target_pairs={{0,24},{1,25},{2,26},{3,27},{4,28},{5,29},{6,30},{7,31},{8,0},{9,1... | collective-permute-start | bytes 331784 | tf_op jit(solution)/shard_map/ppermute | solution.py:468
  30.0 0.1 pad_add_fusion.place_ref
  30.1 2.3 %collective-permute-done.4.up_ref = f32[1,72,384]{2,1,0:T(8,128)S(1)} collective-permute-done((f32[1,72,384]{2,1,0:T(8,128)S(1)}, f32[1,72,384]{2,1,0:T(8,128)S(1)}, u32[]{:S(2)}, u32[]{:S(2)}) %collective-permute-start.4) | collective-permute-done | bytes 110624 | tf_op jit(solution)/shard_map/ppermute | solution.py:468
  32.4 0.4 collective-permute-done.5.down_ref
  32.8 2.0 %shard_map.134 = (f32[72,8,256]{2,1,0:T(8,128)S(1)}, f32[128,256]{1,0:T(8,128)S(1)}) custom-call(f32[72,8,256]{2,1,0:T(8,128)S(1)} %copy-done.2, f32[72,8,256]{2,1,0:T(8,128)S(1)} %get-tuple-element.37.state_ref, f32[72,8,256]{2,1,0:T(8,128)S(1)} %get-tuple-element.38.smooth_ref, f32[72,8,384]{2,1,0:T(8,128)S(1)} %get-tuple-element.39.tend_ref, ...), custom_call_target="tpu_custom_call" | custom-call | flops 10000000 | bytes 4000000 | tf_op jit(solution)/shard_map/pallas_call | solution.py:445
  34.9 0.1 broadcast_in_dim.13.growth_ref
  34.9 10.1 %shard_map.135 = (bf16[128,33,256]{2,1,0:T(8,128)(2,1)S(1)}, f32[16,128]{1,0:T(8,128)S(1)}, bf16[32,16,128]{2,1,0:T(8,128)(2,1)S(1)}) custom-call(s32[128]{0:T(128)S(1)} %get-tuple-element.56.order_ref, s32[128]{0:T(128)S(1)} %get-tuple-element.55.count_ref, s32[4]{0:T(128)S(1)} %pad_add_fusion.place_ref, bf16[128,33,256]{2,1,0:T(8,128)(2,1)S(1)} %copy.16.drops_ref, ...), custom_call_target="tpu_custom_call" | custom-call | flops 10000000000 | bytes 4000000 | tf_op jit(solution)/shard_map/pallas_call | solution.py:445
  45.0 0.0 copy-start.7
  45.0 0.6 copy-done.7
  45.7 43.1 %all-to-all-start = ((bf16[32,16,128]{2,1,0:T(8,128)(2,1)}), bf16[32,16,128]{2,1,0:T(8,128)(2,1)S(1)}, u32[]{:S(2)}, u32[]{:S(2)}) async-start(bf16[32,16,128]{2,1,0:T(8,128)(2,1)} %copy-done.7), calls=%async_computation | async-start | bytes 262144 | tf_op jit(solution)/shard_map/all_to_all | solution.py:568
  88.8 0.1 stack.41.around_ref
  88.9 1.8 %copy.17 = bf16[128,33,256]{2,0,1:T(8,128)(2,1)} copy(bf16[128,33,256]{2,1,0:T(8,128)(2,1)S(1)} %get-tuple-element.53) | data formatting | bytes 4325376
  90.7 5.8 %all-to-all-done.got_ref = bf16[32,16,128]{2,1,0:T(8,128)(2,1)S(1)} async-done(((bf16[32,16,128]{2,1,0:T(8,128)(2,1)}), bf16[32,16,128]{2,1,0:T(8,128)(2,1)S(1)}, u32[]{:S(2)}, u32[]{:S(2)}) %all-to-all-start) | async-done | bytes 131104 | tf_op jit(solution)/shard_map/all_to_all | solution.py:568
  96.5 2.3 %shard_map.136 = (f32[72,8,256]{2,1,0:T(8,128)}, f32[16,256]{1,0:T(8,128)}) custom-call(s32[8]{0:T(128)S(1)} %stack.41.around_ref, f32[72,8,256]{2,1,0:T(8,128)S(1)} %get-tuple-element.42.base_ref, f32[16,128]{1,0:T(8,128)S(1)} %get-tuple-element.44.own_ref, bf16[32,16,128]{2,1,0:T(8,128)(2,1)S(1)} %all-to-all-done.got_ref, f32[72,16]{1,0:T(8,128)S(1)} %copy-done.8), custom_call_target="tpu_custom_call" | custom-call | flops 10000000 | bytes 4000000 | tf_op jit(solution)/shard_map/pallas_call | solution.py:445
  (15 shorter events, 0.0 us)
Async XLA Ops:
  0.6 14.7 %copy-start = (bf16[33,1089]{1,0:T(8,128)(2,1)S(1)}, bf16[33,1089]{1,0:T(8,128)(2,1)}, u32[]{:S(2)}) copy-start(bf16[33,1089]{1,0:T(8,128)(2,1)} %param.17) | copy-start | bytes 215626
  0.6 1.1 %copy-start.1 = (f32[72,8,256]{2,1,0:T(8,128)S(1)}, f32[72,8,256]{2,1,0:T(8,128)}, u32[]{:S(2)}) copy-start(f32[72,8,256]{2,1,0:T(8,128)} %q_ref.5) | copy-start | bytes 1769476
  1.7 1.1 %copy-start.3 = (f32[72,8,256]{2,1,0:T(8,128)S(1)}, f32[72,8,256]{2,1,0:T(8,128)}, u32[]{:S(2)}) copy-start(f32[72,8,256]{2,1,0:T(8,128)} %u_ref.3) | copy-start | bytes 1769476
  2.8 1.1 %copy-start.5 = (f32[72,8,256]{2,1,0:T(8,128)S(1)}, f32[72,8,256]{2,1,0:T(8,128)}, u32[]{:S(2)}) copy-start(f32[72,8,256]{2,1,0:T(8,128)} %v_ref.3) | copy-start | bytes 1769476
  3.9 9.8 %copy-start.12 = (s32[128]{0:T(128)S(1)}, s32[128]{0:T(128)}, u32[]{:S(2)}) copy-start(s32[128]{0:T(128)} %param.16) | copy-start | bytes 1540
  3.9 10.1 %copy-start.10 = (bf16[128,33,256]{2,0,1:T(8,128)(2,1)S(1)}, bf16[128,33,256]{2,0,1:T(8,128)(2,1)}, u32[]{:S(2)}) copy-start(bf16[128,33,256]{2,0,1:T(8,128)(2,1)} %param.14) | copy-start | bytes 6488068
  6.0 9.9 %collective-permute-start = (f32[18,8,128]{2,1,0:T(8,128)S(1)}, f32[18,8,128]{2,1,0:T(8,128)S(1)}, u32[]{:S(2)}, u32[]{:S(2)}) collective-permute-start(f32[18,8,128]{2,1,0:T(8,128)S(1)} %get-tuple-element.27), channel_id=1, source_target_pairs={{0,1},{1,2},{2,3},{3,4},{4,5},{5,6},{6,7},{7,0},{8,9},{9,10},{10,1... | collective-permute-start | bytes 221192 | tf_op jit(solution)/shard_map/ppermute | solution.py:468
  8.9 6.9 %collective-permute-start.1 = (f32[18,8,128]{2,1,0:T(8,128)S(1)}, f32[18,8,128]{2,1,0:T(8,128)S(1)}, u32[]{:S(2)}, u32[]{:S(2)}) collective-permute-start(f32[18,8,128]{2,1,0:T(8,128)S(1)} %get-tuple-element.28), channel_id=1, source_target_pairs={{0,7},{1,0},{2,1},{3,2},{4,3},{5,4},{6,5},{7,6},{8,15},{9,8},{10,9... | collective-permute-start | bytes 221192 | tf_op jit(solution)/shard_map/ppermute | solution.py:468
  14.0 1.3 %copy-start.13 = (f32[33]{0:T(128)S(1)}, f32[33]{0:T(128)}, u32[]{:S(2)}) copy-start(f32[33]{0:T(128)} %param.18) | copy-start | bytes 400
  14.0 1.4 %copy-start.11 = (bf16[1089,576]{1,0:T(8,128)(2,1)S(1)}, bf16[1089,576]{1,0:T(8,128)(2,1)}, u32[]{:S(2)}) copy-start(bf16[1089,576]{1,0:T(8,128)(2,1)} %constant.64.clone) | copy-start | bytes 3763588
  14.0 1.7 %copy-start.14 = (s32[128,1]{0,1:T(1,128)S(1)}, s32[128,1]{0,1:T(1,128)}, u32[]{:S(2)}) copy-start(s32[128,1]{0,1:T(1,128)} %param.15) | copy-start | bytes 1540
  15.3 9.4 %copy-start.2 = (f32[72,8,256]{2,1,0:T(8,128)S(1)}, f32[72,8,256]{2,1,0:T(8,128)}, u32[]{:S(2)}) copy-start(f32[72,8,256]{2,1,0:T(8,128)} %q_ref.5) | copy-start | bytes 1769476
  15.3 9.4 %copy-start.4 = (f32[72,8,256]{2,1,0:T(8,128)S(1)}, f32[72,8,256]{2,1,0:T(8,128)}, u32[]{:S(2)}) copy-start(f32[72,8,256]{2,1,0:T(8,128)} %u_ref.3) | copy-start | bytes 1769476
  15.3 9.4 %copy-start.6 = (f32[72,8,256]{2,1,0:T(8,128)S(1)}, f32[72,8,256]{2,1,0:T(8,128)}, u32[]{:S(2)}) copy-start(f32[72,8,256]{2,1,0:T(8,128)} %v_ref.3) | copy-start | bytes 1769476
  15.8 17.0 %copy-start.9 = (f32[16,72]{1,0:T(8,128)S(1)}, f32[16,72]{1,0:T(8,128)}, u32[]{:S(2)}) copy-start(f32[16,72]{1,0:T(8,128)} %constant.63.clone.down_map_ref) | copy-start | bytes 13828
  17.7 5.8 %collective-permute-start.2 = (f32[2,72,384]{2,1,0:T(8,128)S(1)}, f32[2,72,384]{2,1,0:T(8,128)S(1)}, u32[]{:S(2)}, u32[]{:S(2)}) collective-permute-start(f32[2,72,384]{2,1,0:T(8,128)S(1)} %get-tuple-element.35), channel_id=1, source_target_pairs={{0,8},{1,9},{2,10},{3,11},{4,12},{5,13},{6,14},{7,15},{8,16},{9,17... | collective-permute-start | bytes 663560 | tf_op jit(solution)/shard_map/ppermute | solution.py:468
  17.8 6.9 %collective-permute-start.3 = (f32[2,72,384]{2,1,0:T(8,128)S(1)}, f32[2,72,384]{2,1,0:T(8,128)S(1)}, u32[]{:S(2)}, u32[]{:S(2)}) collective-permute-start(f32[2,72,384]{2,1,0:T(8,128)S(1)} %get-tuple-element.36), channel_id=1, source_target_pairs={{0,24},{1,25},{2,26},{3,27},{4,28},{5,29},{6,30},{7,31},{8,0},{9,1... | collective-permute-start | bytes 663560 | tf_op jit(solution)/shard_map/ppermute | solution.py:468
  28.0 4.4 %collective-permute-start.4 = (f32[1,72,384]{2,1,0:T(8,128)S(1)}, f32[1,72,384]{2,1,0:T(8,128)S(1)}, u32[]{:S(2)}, u32[]{:S(2)}) collective-permute-start(f32[1,72,384]{2,1,0:T(8,128)S(1)} %get-tuple-element.40), channel_id=1, source_target_pairs={{0,8},{1,9},{2,10},{3,11},{4,12},{5,13},{6,14},{7,15},{8,16},{9,17... | collective-permute-start | bytes 331784 | tf_op jit(solution)/shard_map/ppermute | solution.py:468
  28.7 4.1 %collective-permute-start.5 = (f32[1,72,384]{2,1,0:T(8,128)S(1)}, f32[1,72,384]{2,1,0:T(8,128)S(1)}, u32[]{:S(2)}, u32[]{:S(2)}) collective-permute-start(f32[1,72,384]{2,1,0:T(8,128)S(1)} %get-tuple-element.41), channel_id=1, source_target_pairs={{0,24},{1,25},{2,26},{3,27},{4,28},{5,29},{6,30},{7,31},{8,0},{9,1... | collective-permute-start | bytes 331784 | tf_op jit(solution)/shard_map/ppermute | solution.py:468
  45.0 0.7 copy-start.7
  45.7 50.8 %all-to-all-start = ((bf16[32,16,128]{2,1,0:T(8,128)(2,1)}), bf16[32,16,128]{2,1,0:T(8,128)(2,1)S(1)}, u32[]{:S(2)}, u32[]{:S(2)}) async-start(bf16[32,16,128]{2,1,0:T(8,128)(2,1)} %copy-done.7), calls=%async_computation | async-start | bytes 262144 | tf_op jit(solution)/shard_map/all_to_all | solution.py:568
  88.9 7.6 %copy-start.8 = (f32[72,16]{1,0:T(8,128)S(1)}, f32[72,16]{1,0:T(8,128)}, u32[]{:S(2)}) copy-start(f32[72,16]{1,0:T(8,128)} %constant.65.clone.up_map_ref) | copy-start | bytes 13828

commit v3 on v0

--- a/solution.py
+++ b/solution.py
@@ -18,7 +18,7 @@
 HIGH = lax.Precision.HIGHEST
 F32 = jnp.float32
 BF16 = jnp.bfloat16
-GROUP = 8
+GROUP = 16
 CHUNK = 8
 MIB = 1024 * 1024
 
@@ -266,7 +266,8 @@
 def crm_kernel(
     order_ref, count_ref, place_ref, drops_ref, cell_ref, slot_ref, coef_ref, tail_coef_ref,
     growth_ref,
-    final_ref, heat_ref, send_ref, state_ref, pair_ref, tail_ref, heat_cell_ref, echo_cell_ref,
+    final_ref, heat_ref, send_ref, state_ref, pair_ref, tail_ref, twice_ref,
+    heat_cell_ref, echo_cell_ref,
 ):
     bins = drops_ref.shape[1]
     cells = drops_ref.shape[2]
@@ -277,20 +278,19 @@
     state_ref[...] = jnp.zeros(state_ref.shape, F32)
     mass = (iota((40, cells), 0) + 1).astype(F32) / F32(bins)
 
-    def grow(k, which):
+    def grow(k, which, zero):
         grown = state_ref[k] + growth * cell_ref[pl.ds(which, 1), :]
         for h in range(cells // 128):
             cut = slice(128 * h, 128 * h + 128)
             g = grown[0:32, cut]
             last = grown[32:40, cut]
-            for s in range(8):
-                rolled = g if s == 0 else pltpu.roll(g, 32 - s, 0)
-                for a in range(2):
-                    other = rolled
-                    if a:
-                        other = jnp.concatenate([rolled[8:], rolled[:8]], axis=0)
-                    d = 8 * a + s
-                    pair_ref[k, 32 * d : 32 * d + 32, cut] = (g * other).astype(BF16)
+            twice_ref[2 * k + h, 0:32, :] = g
+            twice_ref[2 * k + h, 32:48, :] = g[0:16]
+            for d in range(16):
+                other = g if d % 8 == 0 else twice_ref[2 * k + h, pl.ds(zero + d, 32), :]
+                if d == 8:
+                    other = jnp.concatenate([g[8:], g[:8]], axis=0)
+                pair_ref[k, 32 * d : 32 * d + 32, cut] = (g * other).astype(BF16)
             at = 64 * (k % 4)
             tail_ref[k // 4, at : at + 16, cut] = (g[0:16] * g[16:32]).astype(BF16)
             tail_ref[k // 4, at + 16 : at + 48, cut] = (g * last[0:1]).astype(BF16)
@@ -307,7 +307,7 @@
 
         def step(s, c):
             for q in range(GROUP // 4):
-                grown = [grow(4 * q + k, which[4 * q + k]) for k in range(4)]
+                grown = [grow(4 * q + k, which[4 * q + k], place_ref[3]) for k in range(4)]
                 tails = jnp.dot(tail_coef, tail_ref[q], preferred_element_type=F32)
                 for k in range(4):
                     slot = 4 * q + k
@@ -567,7 +567,7 @@
     n_crm = lax.axis_size("crm")
     g = lax.axis_index("gcm").astype(jnp.int32)
     c = lax.axis_index("crm").astype(jnp.int32)
-    place = jnp.stack([g, jnp.int32(n_gcm), jnp.int32(n_crm)])
+    place = jnp.stack([g, jnp.int32(n_gcm), jnp.int32(n_crm), jnp.int32(0)])
 
     final, heat, send = call(
         crm_kernel,
@@ -577,6 +577,7 @@
         + v(drops, cell_forcing, slot_of[None, :], coef[:, :512], tail_coef, growth_rows),
         [((GROUP, 40, cells), F32), ((GROUP, 512, cells), BF16),
          ((GROUP // 4, 256, cells), BF16),
+         ((2 * GROUP, 48, 128), F32),
          ((col_total, cells), F32), ((col_total, cells), F32)],
         flops=10_000_000_000,
     )

time: 113 us -> 108 us (0.956)
  Pallas kernels: 74.6 us -> 23.8 us
  starting transfers between devices: 13.1 us -> 57.7 us
    pallas_call x7, Pallas kernels: 74.6 us -> 23.8 us  [call(): pl.pallas_call(kernel, out_shape=[jax.ShapeDtypeStruct(s, t) for s, t in...]
    all_to_all x1, starting transfers between devices: 3.15 us -> 47.8 us  [shards(): lax.all_to_all(send, ('gcm', 'crm'), split_axis=0, concat_axis=0, tiled=T...]
  transfers between devices with their start and end apart: 7 -> 7, of which waited for: 5 -> 5; matrix products, arithmetic and copies ran while one was open for 6% -> 7% of each run, Pallas kernels for 1% -> 1%
where the time goes in v3:
time: 108 us; the launch traced here: 107 us
  starting transfers between devices  57.7 us (53%)
  Pallas kernels  23.8 us (22%)
  waiting for transfers between devices  13.6 us (13%)
  local copies, waits for them, and re-layouts  8.93 us (8%)
  matrix products  1.68 us (2%)
    all_to_all x1, starting transfers between devices, shards(): lax.all_to_all(send, ('gcm', 'crm'), split_axis=0, concat_axis=0, tiled=T...  47.8 us
    pallas_call x7, Pallas kernels, call(): pl.pallas_call(kernel, out_shape=[jax.ShapeDtypeStruct(s, t) for s, t in...  23.8 us
    ppermute x6, starting transfers between devices, shift(): return lax.ppermute(value, ('gcm', 'crm'), pairs)  9.91 us
    unnamed x28, local copies, waits for them, and re-layouts  8.76 us
    ppermute x6, waiting for transfers between devices, shift(): return lax.ppermute(value, ('gcm', 'crm'), pairs)  7.84 us
    all_to_all x1, waiting for transfers between devices, shards(): lax.all_to_all(send, ('gcm', 'crm'), split_axis=0, concat_axis=0, tiled=T...  5.76 us
  transfers between devices with their start and end apart: 7, of which 5 were waited for; matrix products, arithmetic and copies ran while one was open for 7% of the time, Pallas kernels for 1%

profile of v3, /device:TPU:0, one launch (start us, length us, event | category | flops | bytes accessed | tf_op | source)
XLA Modules:
  0.0 107.3 jit_solution(12930958599682069692)
XLA Ops:
  0.6 0.0 copy-start
  0.6 0.0 copy-start.1
  0.7 1.1 %copy-done.1 = f32[72,8,256]{2,1,0:T(8,128)S(1)} copy-done((f32[72,8,256]{2,1,0:T(8,128)S(1)}, f32[72,8,256]{2,1,0:T(8,128)}, u32[]{:S(2)}) %copy-start.1) | copy-done | bytes 589848
  1.7 1.1 copy-done.3
  2.8 1.1 copy-done.5
  3.9 2.1 %shard_map.131 = (f32[18,8,128]{2,1,0:T(8,128)S(1)}, f32[18,8,128]{2,1,0:T(8,128)S(1)}) custom-call(f32[72,8,256]{2,1,0:T(8,128)S(1)} %copy-done.1, f32[72,8,256]{2,1,0:T(8,128)S(1)} %copy-done.3, f32[72,8,256]{2,1,0:T(8,128)S(1)} %copy-done.5), custom_call_target="tpu_custom_call" | custom-call | flops 10000000 | bytes 4000000 | tf_op jit(solution)/shard_map/pallas_call | solution.py:453
  5.9 0.0 copy-start.10
  6.0 3.0 %collective-permute-start = (f32[18,8,128]{2,1,0:T(8,128)S(1)}, f32[18,8,128]{2,1,0:T(8,128)S(1)}, u32[]{:S(2)}, u32[]{:S(2)}) collective-permute-start(f32[18,8,128]{2,1,0:T(8,128)S(1)} %get-tuple-element.27), channel_id=1, source_target_pairs={{0,1},{1,2},{2,3},{3,4},{4,5},{5,6},{6,7},{7,0},{8,9},{9,10},{10,1... | collective-permute-start | bytes 221192 | tf_op jit(solution)/shard_map/ppermute | solution.py:476
  9.0 3.1 %collective-permute-start.1 = (f32[18,8,128]{2,1,0:T(8,128)S(1)}, f32[18,8,128]{2,1,0:T(8,128)S(1)}, u32[]{:S(2)}, u32[]{:S(2)}) collective-permute-start(f32[18,8,128]{2,1,0:T(8,128)S(1)} %get-tuple-element.28), channel_id=1, source_target_pairs={{0,7},{1,0},{2,1},{3,2},{4,3},{5,4},{6,5},{7,6},{8,15},{9,8},{10,9... | collective-permute-start | bytes 221192 | tf_op jit(solution)/shard_map/ppermute | solution.py:476
  12.1 0.0 copy-done
  12.1 1.7 %reduce-precision_convert_fusion = (bf16[33,576]{1,0:T(8,128)(2,1)S(1)}, bf16[33,576]{1,0:T(8,128)(2,1)S(1)}) fusion(bf16[1089,576]{1,0:T(8,128)(2,1)} %constant.67.clone, bf16[33,1089]{1,0:T(8,128)(2,1)S(1)} %copy-done), kind=kOutput, calls=%fused_computation.22 | convolution fusion | flops 41494464 | bytes 1402434 | tf_op jit(solution)/shard_map/dot_general | solution.py:556
  13.8 1.6 %shard_map.130 = (f32[72,8,256]{2,1,0:T(8,128)S(1)}, f32[2,72,256]{2,1,0:T(8,128)S(1)}, f32[2,72,256]{2,1,0:T(8,128)S(1)}) custom-call(f32[72,8,256]{2,1,0:T(8,128)S(1)} %copy-done.1, f32[72,8,256]{2,1,0:T(8,128)S(1)} %copy-done.3, f32[72,8,256]{2,1,0:T(8,128)S(1)} %copy-done.5), custom_call_target="tpu_custom_call" | custom-call | flops 10000000 | bytes 4000000 | tf_op jit(solution)/shard_map/pallas_call | solution.py:453
  15.4 0.0 copy-done.10
  15.4 0.2 convert_reduce_fusion.1
  15.6 0.1 select_reduce_fusion
  15.7 0.1 fusion.10.tail_coef_ref
  15.8 0.0 copy-start.11
  15.8 0.0 copy-start.12
  15.8 0.0 copy-start.2
  15.9 0.0 copy-start.4
  15.9 0.0 copy-start.6
  15.9 3.0 %copy.16.drops_ref = bf16[128,33,256]{2,1,0:T(8,128)(2,1)S(1)} copy(bf16[128,33,256]{2,0,1:T(8,128)(2,1)} %param.14) | data formatting | bytes 4325376 | tf_op args[3]
  18.9 0.0 copy-done.11
  18.9 0.1 convert_reduce_fusion
  19.0 0.0 collective-permute-done.left_ref
  19.0 0.0 collective-permute-done.1.right_ref
  19.0 0.0 copy-start.9
  19.0 1.9 %shard_map.132 = (f32[72,8,128]{2,1,0:T(8,128)S(1)}, f32[72,8,128]{2,1,0:T(8,128)S(1)}, f32[72,8,128]{2,1,0:T(8,128)S(1)}, f32[72,8,128]{2,1,0:T(8,128)S(1)}, f3...) custom-call(f32[18,8,128]{2,1,0:T(8,128)S(1)} %collective-permute-done.left_ref, ...), custom_call_target="tpu_custom_call" | custom-call | flops 10000000 | bytes 4000000 | tf_op jit(solution)/shard_map/pallas_call | solution.py:453
  20.9 0.1 collective-permute-start.2
  21.0 1.7 %collective-permute-start.3 = (f32[2,72,384]{2,1,0:T(8,128)S(1)}, f32[2,72,384]{2,1,0:T(8,128)S(1)}, u32[]{:S(2)}, u32[]{:S(2)}) collective-permute-start(f32[2,72,384]{2,1,0:T(8,128)S(1)} %get-tuple-element.36), channel_id=1, source_target_pairs={{0,24},{1,25},{2,26},{3,27},{4,28},{5,29},{6,30},{7,31},{8,0},{9,1... | collective-permute-start | bytes 663560 | tf_op jit(solution)/shard_map/ppermute | solution.py:476
  22.7 4.0 %collective-permute-done.2.up_ref = f32[2,72,384]{2,1,0:T(8,128)S(1)} collective-permute-done((f32[2,72,384]{2,1,0:T(8,128)S(1)}, f32[2,72,384]{2,1,0:T(8,128)S(1)}, u32[]{:S(2)}, u32[]{:S(2)}) %collective-permute-start.2) | collective-permute-done | bytes 221216 | tf_op jit(solution)/shard_map/ppermute | solution.py:476
  26.7 1.2 %collective-permute-done.3.down_ref = f32[2,72,384]{2,1,0:T(8,128)S(1)} collective-permute-done((f32[2,72,384]{2,1,0:T(8,128)S(1)}, f32[2,72,384]{2,1,0:T(8,128)S(1)}, u32[]{:S(2)}, u32[]{:S(2)}) %collective-permute-start.3) | collective-permute-done | bytes 221216 | tf_op jit(solution)/shard_map/ppermute | solution.py:476
  27.9 3.3 %shard_map.133 = (f32[72,8,256]{2,1,0:T(8,128)S(1)}, f32[72,8,256]{2,1,0:T(8,128)S(1)}, f32[72,8,384]{2,1,0:T(8,128)S(1)}, f32[1,72,384]{2,1,0:T(8,128)S(1)}, f32[1,72,384]{2,1,0:T(8,128)S(1)}) custom-call(f32[72,8,256]{2,1,0:T(8,128)S(1)} %copy-done.2, f32[72,8,256]{2,1,0:T(8,128)S(1)} %copy-done.4, f32[72,8,256]{2,1,0:T(8,128)S(1)} %copy-done.6, ...), custom_call_target="tpu_custom_call" | custom-call | flops 10000000 | bytes 4000000 | tf_op jit(solution)/shard_map/pallas_call | solution.py:453
  31.1 0.7 collective-permute-start.4
  31.8 1.3 %collective-permute-start.5 = (f32[1,72,384]{2,1,0:T(8,128)S(1)}, f32[1,72,384]{2,1,0:T(8,128)S(1)}, u32[]{:S(2)}, u32[]{:S(2)}) collective-permute-start(f32[1,72,384]{2,1,0:T(8,128)S(1)} %get-tuple-element.41), channel_id=1, source_target_pairs={{0,24},{1,25},{2,26},{3,27},{4,28},{5,29},{6,30},{7,31},{8,0},{9,1... | collective-permute-start | bytes 331784 | tf_op jit(solution)/shard_map/ppermute | solution.py:476
  33.2 0.1 pad_add_fusion.place_ref
  33.2 2.3 %collective-permute-done.4.up_ref = f32[1,72,384]{2,1,0:T(8,128)S(1)} collective-permute-done((f32[1,72,384]{2,1,0:T(8,128)S(1)}, f32[1,72,384]{2,1,0:T(8,128)S(1)}, u32[]{:S(2)}, u32[]{:S(2)}) %collective-permute-start.4) | collective-permute-done | bytes 110624 | tf_op jit(solution)/shard_map/ppermute | solution.py:476
  35.5 0.4 collective-permute-done.5.down_ref
  35.9 2.0 %shard_map.134 = (f32[72,8,256]{2,1,0:T(8,128)S(1)}, f32[128,256]{1,0:T(8,128)S(1)}) custom-call(f32[72,8,256]{2,1,0:T(8,128)S(1)} %copy-done.2, f32[72,8,256]{2,1,0:T(8,128)S(1)} %get-tuple-element.37.state_ref, f32[72,8,256]{2,1,0:T(8,128)S(1)} %get-tuple-element.38.smooth_ref, f32[72,8,384]{2,1,0:T(8,128)S(1)} %get-tuple-element.39.tend_ref, ...), custom_call_target="tpu_custom_call" | custom-call | flops 10000000 | bytes 4000000 | tf_op jit(solution)/shard_map/pallas_call | solution.py:453
  38.0 0.1 broadcast_in_dim.13.growth_ref
  38.1 10.7 %shard_map.135 = (bf16[128,33,256]{2,1,0:T(8,128)(2,1)S(1)}, f32[16,128]{1,0:T(8,128)S(1)}, bf16[32,16,128]{2,1,0:T(8,128)(2,1)S(1)}) custom-call(s32[128]{0:T(128)S(1)} %get-tuple-element.56.order_ref, s32[128]{0:T(128)S(1)} %get-tuple-element.55.count_ref, s32[4]{0:T(128)S(1)} %pad_add_fusion.place_ref, bf16[128,33,256]{2,1,0:T(8,128)(2,1)S(1)} %copy.16.drops_ref, ...), custom_call_target="tpu_custom_call" | custom-call | flops 10000000000 | bytes 4000000 | tf_op jit(solution)/shard_map/pallas_call | solution.py:453
  48.8 0.0 copy-start.7
  48.8 0.6 copy-done.7
  49.4 47.8 %all-to-all-start = ((bf16[32,16,128]{2,1,0:T(8,128)(2,1)}), bf16[32,16,128]{2,1,0:T(8,128)(2,1)S(1)}, u32[]{:S(2)}, u32[]{:S(2)}) async-start(bf16[32,16,128]{2,1,0:T(8,128)(2,1)} %copy-done.7), calls=%async_computation | async-start | bytes 262144 | tf_op jit(solution)/shard_map/all_to_all | solution.py:584
  97.3 0.1 stack.41.around_ref
  97.4 1.8 %copy.17 = bf16[128,33,256]{2,0,1:T(8,128)(2,1)} copy(bf16[128,33,256]{2,1,0:T(8,128)(2,1)S(1)} %get-tuple-element.53) | data formatting | bytes 4325376
  99.2 5.8 %all-to-all-done.got_ref = bf16[32,16,128]{2,1,0:T(8,128)(2,1)S(1)} async-done(((bf16[32,16,128]{2,1,0:T(8,128)(2,1)}), bf16[32,16,128]{2,1,0:T(8,128)(2,1)S(1)}, u32[]{:S(2)}, u32[]{:S(2)}) %all-to-all-start) | async-done | bytes 131104 | tf_op jit(solution)/shard_map/all_to_all | solution.py:584
  105.0 2.3 %shard_map.136 = (f32[72,8,256]{2,1,0:T(8,128)}, f32[16,256]{1,0:T(8,128)}) custom-call(s32[8]{0:T(128)S(1)} %stack.41.around_ref, f32[72,8,256]{2,1,0:T(8,128)S(1)} %get-tuple-element.42.base_ref, f32[16,128]{1,0:T(8,128)S(1)} %get-tuple-element.44.own_ref, bf16[32,16,128]{2,1,0:T(8,128)(2,1)S(1)} %all-to-all-done.got_ref, f32[72,16]{1,0:T(8,128)S(1)} %copy-done.8), custom_call_target="tpu_custom_call" | custom-call | flops 10000000 | bytes 4000000 | tf_op jit(solution)/shard_map/pallas_call | solution.py:453
  (14 shorter events, 0.1 us)
Async XLA Ops:
  0.6 11.4 %copy-start = (bf16[33,1089]{1,0:T(8,128)(2,1)S(1)}, bf16[33,1089]{1,0:T(8,128)(2,1)}, u32[]{:S(2)}) copy-start(bf16[33,1089]{1,0:T(8,128)(2,1)} %param.17) | copy-start | bytes 215626
  0.6 1.1 %copy-start.1 = (f32[72,8,256]{2,1,0:T(8,128)S(1)}, f32[72,8,256]{2,1,0:T(8,128)}, u32[]{:S(2)}) copy-start(f32[72,8,256]{2,1,0:T(8,128)} %q_ref.5) | copy-start | bytes 1769476
  1.7 1.1 copy-start.3
  2.8 1.1 copy-start.5
  5.9 9.5 %copy-start.10 = (s32[128]{0:T(128)S(1)}, s32[128]{0:T(128)}, u32[]{:S(2)}) copy-start(s32[128]{0:T(128)} %param.16) | copy-start | bytes 1540
  6.0 13.0 %collective-permute-start = (f32[18,8,128]{2,1,0:T(8,128)S(1)}, f32[18,8,128]{2,1,0:T(8,128)S(1)}, u32[]{:S(2)}, u32[]{:S(2)}) collective-permute-start(f32[18,8,128]{2,1,0:T(8,128)S(1)} %get-tuple-element.27), channel_id=1, source_target_pairs={{0,1},{1,2},{2,3},{3,4},{4,5},{5,6},{6,7},{7,0},{8,9},{9,10},{10,1... | collective-permute-start | bytes 221192 | tf_op jit(solution)/shard_map/ppermute | solution.py:476
  9.0 10.1 %collective-permute-start.1 = (f32[18,8,128]{2,1,0:T(8,128)S(1)}, f32[18,8,128]{2,1,0:T(8,128)S(1)}, u32[]{:S(2)}, u32[]{:S(2)}) collective-permute-start(f32[18,8,128]{2,1,0:T(8,128)S(1)} %get-tuple-element.28), channel_id=1, source_target_pairs={{0,7},{1,0},{2,1},{3,2},{4,3},{5,4},{6,5},{7,6},{8,15},{9,8},{10,9... | collective-permute-start | bytes 221192 | tf_op jit(solution)/shard_map/ppermute | solution.py:476
  15.8 3.1 %copy-start.11 = (f32[33]{0:T(128)S(1)}, f32[33]{0:T(128)}, u32[]{:S(2)}) copy-start(f32[33]{0:T(128)} %param.18) | copy-start | bytes 400
  15.8 3.1 %copy-start.12 = (s32[128,1]{0,1:T(1,128)S(1)}, s32[128,1]{0,1:T(1,128)}, u32[]{:S(2)}) copy-start(s32[128,1]{0,1:T(1,128)} %param.15) | copy-start | bytes 1540
  15.8 12.0 %copy-start.2 = (f32[72,8,256]{2,1,0:T(8,128)S(1)}, f32[72,8,256]{2,1,0:T(8,128)}, u32[]{:S(2)}) copy-start(f32[72,8,256]{2,1,0:T(8,128)} %q_ref.5) | copy-start | bytes 1769476
  15.9 12.0 %copy-start.4 = (f32[72,8,256]{2,1,0:T(8,128)S(1)}, f32[72,8,256]{2,1,0:T(8,128)}, u32[]{:S(2)}) copy-start(f32[72,8,256]{2,1,0:T(8,128)} %u_ref.3) | copy-start | bytes 1769476
  15.9 12.0 %copy-start.6 = (f32[72,8,256]{2,1,0:T(8,128)S(1)}, f32[72,8,256]{2,1,0:T(8,128)}, u32[]{:S(2)}) copy-start(f32[72,8,256]{2,1,0:T(8,128)} %v_ref.3) | copy-start | bytes 1769476
  19.0 16.9 %copy-start.9 = (f32[16,72]{1,0:T(8,128)S(1)}, f32[16,72]{1,0:T(8,128)}, u32[]{:S(2)}) copy-start(f32[16,72]{1,0:T(8,128)} %constant.66.clone.down_map_ref) | copy-start | bytes 13828
  20.9 5.8 %collective-permute-start.2 = (f32[2,72,384]{2,1,0:T(8,128)S(1)}, f32[2,72,384]{2,1,0:T(8,128)S(1)}, u32[]{:S(2)}, u32[]{:S(2)}) collective-permute-start(f32[2,72,384]{2,1,0:T(8,128)S(1)} %get-tuple-element.35), channel_id=1, source_target_pairs={{0,8},{1,9},{2,10},{3,11},{4,12},{5,13},{6,14},{7,15},{8,16},{9,17... | collective-permute-start | bytes 663560 | tf_op jit(solution)/shard_map/ppermute | solution.py:476
  21.0 6.9 %collective-permute-start.3 = (f32[2,72,384]{2,1,0:T(8,128)S(1)}, f32[2,72,384]{2,1,0:T(8,128)S(1)}, u32[]{:S(2)}, u32[]{:S(2)}) collective-permute-start(f32[2,72,384]{2,1,0:T(8,128)S(1)} %get-tuple-element.36), channel_id=1, source_target_pairs={{0,24},{1,25},{2,26},{3,27},{4,28},{5,29},{6,30},{7,31},{8,0},{9,1... | collective-permute-start | bytes 663560 | tf_op jit(solution)/shard_map/ppermute | solution.py:476
  31.1 4.4 %collective-permute-start.4 = (f32[1,72,384]{2,1,0:T(8,128)S(1)}, f32[1,72,384]{2,1,0:T(8,128)S(1)}, u32[]{:S(2)}, u32[]{:S(2)}) collective-permute-start(f32[1,72,384]{2,1,0:T(8,128)S(1)} %get-tuple-element.40), channel_id=1, source_target_pairs={{0,8},{1,9},{2,10},{3,11},{4,12},{5,13},{6,14},{7,15},{8,16},{9,17... | collective-permute-start | bytes 331784 | tf_op jit(solution)/shard_map/ppermute | solution.py:476
  31.8 4.1 %collective-permute-start.5 = (f32[1,72,384]{2,1,0:T(8,128)S(1)}, f32[1,72,384]{2,1,0:T(8,128)S(1)}, u32[]{:S(2)}, u32[]{:S(2)}) collective-permute-start(f32[1,72,384]{2,1,0:T(8,128)S(1)} %get-tuple-element.41), channel_id=1, source_target_pairs={{0,24},{1,25},{2,26},{3,27},{4,28},{5,29},{6,30},{7,31},{8,0},{9,1... | collective-permute-start | bytes 331784 | tf_op jit(solution)/shard_map/ppermute | solution.py:476
  48.8 0.7 copy-start.7
  49.4 55.6 %all-to-all-start = ((bf16[32,16,128]{2,1,0:T(8,128)(2,1)}), bf16[32,16,128]{2,1,0:T(8,128)(2,1)S(1)}, u32[]{:S(2)}, u32[]{:S(2)}) async-start(bf16[32,16,128]{2,1,0:T(8,128)(2,1)} %copy-done.7), calls=%async_computation | async-start | bytes 262144 | tf_op jit(solution)/shard_map/all_to_all | solution.py:584
  97.4 7.6 %copy-start.8 = (f32[72,16]{1,0:T(8,128)S(1)}, f32[72,16]{1,0:T(8,128)}, u32[]{:S(2)}) copy-start(f32[72,16]{1,0:T(8,128)} %constant.68.clone.up_map_ref) | copy-start | bytes 13828

commit v4 on v1

--- a/solution.py
+++ b/solution.py
@@ -265,7 +265,7 @@
 
 def crm_kernel(
     order_ref, count_ref, place_ref, drops_ref, cell_ref, slot_ref, coef_ref, growth_ref,
-    final_ref, heat_ref, send_ref, state_ref, pair_ref, twice_ref, heat_cell_ref, echo_cell_ref,
+    final_ref, heat_ref, send_ref, state_ref, heat_cell_ref, echo_cell_ref, *twice_refs,
 ):
     bins = drops_ref.shape[1]
     cells = drops_ref.shape[2]
@@ -277,22 +277,26 @@
 
     def grow(k, which, zero):
         grown = state_ref[k] + growth * cell_ref[pl.ds(which, 1), :]
+        halves = []
         for h in range(cells // 128):
             cut = slice(128 * h, 128 * h + 128)
             g = grown[0:32, cut]
             last = grown[32:40, cut]
-            twice_ref[2 * k + h, 0:32, :] = g
-            twice_ref[2 * k + h, 32:48, :] = g[0:16]
+            twice_ref = twice_refs[k]
+            twice_ref[h, 0:32, :] = g
+            twice_ref[h, 32:48, :] = g[0:16]
+            rows = []
             for d in range(16):
-                other = g if d % 8 == 0 else twice_ref[2 * k + h, pl.ds(zero + d, 32), :]
+                other = g if d == 0 else twice_ref[h, pl.ds(zero + d, 32), :]
                 if d == 8:
                     other = jnp.concatenate([g[8:], g[:8]], axis=0)
-                pair_ref[k, 32 * d : 32 * d + 32, cut] = (g * other).astype(BF16)
-            pair_ref[k, 512:528, cut] = (g[0:16] * g[16:32]).astype(BF16)
-            pair_ref[k, 528:560, cut] = (g * last[0:1]).astype(BF16)
+                rows.append((g * other).astype(BF16))
+            rows.append((g[0:16] * g[16:32]).astype(BF16))
+            rows.append((g * last[0:1]).astype(BF16))
             tail = jnp.concatenate([last * last, jnp.zeros((8, 128), F32)], axis=0)
-            pair_ref[k, 560:576, cut] = tail.astype(BF16)
-        return grown
+            rows.append(tail.astype(BF16))
+            halves.append(jnp.concatenate(rows, axis=0))
+        return grown, jnp.concatenate(halves, axis=1)
 
     def group(index, carry):
         base = index * GROUP
@@ -303,8 +307,8 @@
 
         def step(s, c):
             for k in range(GROUP):
-                grown = grow(k, which[k], place_ref[3])
-                change = jnp.dot(coef, pair_ref[k], preferred_element_type=F32)
+                grown, pairs = grow(k, which[k], place_ref[3])
+                change = jnp.dot(coef, pairs, preferred_element_type=F32)
                 moved = grown + (change[0:40] + change[40:80])
                 state_ref[k] = jnp.where(s < count[k], moved, state_ref[k])
             return c
@@ -563,9 +567,8 @@
          ((devices, CRM_LEV, 128), BF16)],
         [("s", order), ("s", ordered), ("s", place)]
         + v(drops, cell_forcing, slot_of[None, :], coef, growth_rows),
-        [((GROUP, 40, cells), F32), ((GROUP, 576, cells), BF16),
-         ((2 * GROUP, 48, 128), F32),
-         ((col_total, cells), F32), ((col_total, cells), F32)],
+        [((GROUP, 40, cells), F32), ((col_total, cells), F32),
+         ((col_total, cells), F32)] + [((2, 48, 128), F32)] * GROUP,
         flops=10_000_000_000,
     )
     got = lax.all_to_all(send, ("gcm", "crm"), split_axis=0, concat_axis=0, tiled=True)

time: 102 us -> 103 us (level); the launches traced: 101 us -> 104 us
  Pallas kernels: 23.6 us -> 67.4 us
  starting transfers between devices: 54.5 us -> 13.7 us
    pallas_call x7, Pallas kernels: 23.6 us -> 67.4 us  [call(): pl.pallas_call(kernel, out_shape=[jax.ShapeDtypeStruct(s, t) for s, t in...]
    all_to_all x1, starting transfers between devices: 44.6 us -> 3.79 us  [shards(): lax.all_to_all(send, ('gcm', 'crm'), split_axis=0, concat_axis=0, tiled=T...]
where the time goes in v4:
time: 103 us; the launch traced here: 104 us
  Pallas kernels  67.4 us (65%)
  starting transfers between devices  13.7 us (13%)
  waiting for transfers between devices  13.6 us (13%)
  local copies, waits for them, and re-layouts  7.21 us (7%)
    pallas_call x7, Pallas kernels, call(): pl.pallas_call(kernel, out_shape=[jax.ShapeDtypeStruct(s, t) for s, t in...  67.4 us
    ppermute x6, starting transfers between devices, shift(): return lax.ppermute(value, ('gcm', 'crm'), pairs)  9.91 us
    ppermute x6, waiting for transfers between devices, shift(): return lax.ppermute(value, ('gcm', 'crm'), pairs)  7.84 us
    unnamed x32, local copies, waits for them, and re-layouts  7.05 us
    all_to_all x1, waiting for transfers between devices, shards(): lax.all_to_all(send, ('gcm', 'crm'), split_axis=0, concat_axis=0, tiled=T...  5.76 us
    all_to_all x1, starting transfers between devices, shards(): lax.all_to_all(send, ('gcm', 'crm'), split_axis=0, concat_axis=0, tiled=T...  3.79 us
  transfers between devices with their start and end apart: 7, of which 5 were waited for; matrix products, arithmetic and copies ran while one was open for 4% of the time, Pallas kernels for 2%

profile of v4, /device:TPU:0, one launch (start us, length us, event | category | flops | bytes accessed | tf_op | source)
XLA Modules:
  0.0 103.7 jit_solution(10033154741460567356)
XLA Ops:
  0.6 0.0 copy-start
  0.6 0.0 copy-start.1
  0.7 1.1 %copy-done.1 = f32[72,8,256]{2,1,0:T(8,128)S(1)} copy-done((f32[72,8,256]{2,1,0:T(8,128)S(1)}, f32[72,8,256]{2,1,0:T(8,128)}, u32[]{:S(2)}) %copy-start.1) | copy-done | bytes 589848
  1.7 1.1 %copy-done.3 = f32[72,8,256]{2,1,0:T(8,128)S(1)} copy-done((f32[72,8,256]{2,1,0:T(8,128)S(1)}, f32[72,8,256]{2,1,0:T(8,128)}, u32[]{:S(2)}) %copy-start.3) | copy-done | bytes 589848
  2.8 1.1 %copy-done.5 = f32[72,8,256]{2,1,0:T(8,128)S(1)} copy-done((f32[72,8,256]{2,1,0:T(8,128)S(1)}, f32[72,8,256]{2,1,0:T(8,128)}, u32[]{:S(2)}) %copy-start.5) | copy-done | bytes 589848
  3.9 2.1 %shard_map.131 = (f32[18,8,128]{2,1,0:T(8,128)S(1)}, f32[18,8,128]{2,1,0:T(8,128)S(1)}) custom-call(f32[72,8,256]{2,1,0:T(8,128)S(1)} %copy-done.1, f32[72,8,256]{2,1,0:T(8,128)S(1)} %copy-done.3, f32[72,8,256]{2,1,0:T(8,128)S(1)} %copy-done.5), custom_call_target="tpu_custom_call" | custom-call | flops 10000000 | bytes 4000000 | tf_op jit(solution)/shard_map/pallas_call | solution.py:449
  6.0 3.0 %collective-permute-start = (f32[18,8,128]{2,1,0:T(8,128)S(1)}, f32[18,8,128]{2,1,0:T(8,128)S(1)}, u32[]{:S(2)}, u32[]{:S(2)}) collective-permute-start(f32[18,8,128]{2,1,0:T(8,128)S(1)} %get-tuple-element.27), channel_id=1, source_target_pairs={{0,1},{1,2},{2,3},{3,4},{4,5},{5,6},{6,7},{7,0},{8,9},{9,10},{10,1... | collective-permute-start | bytes 221192 | tf_op jit(solution)/shard_map/ppermute | solution.py:472
  8.9 3.1 %collective-permute-start.1 = (f32[18,8,128]{2,1,0:T(8,128)S(1)}, f32[18,8,128]{2,1,0:T(8,128)S(1)}, u32[]{:S(2)}, u32[]{:S(2)}) collective-permute-start(f32[18,8,128]{2,1,0:T(8,128)S(1)} %get-tuple-element.28), channel_id=1, source_target_pairs={{0,7},{1,0},{2,1},{3,2},{4,3},{5,4},{6,5},{7,6},{8,15},{9,8},{10,9... | collective-permute-start | bytes 221192 | tf_op jit(solution)/shard_map/ppermute | solution.py:472
  12.0 1.6 %shard_map.130 = (f32[72,8,256]{2,1,0:T(8,128)S(1)}, f32[2,72,256]{2,1,0:T(8,128)S(1)}, f32[2,72,256]{2,1,0:T(8,128)S(1)}) custom-call(f32[72,8,256]{2,1,0:T(8,128)S(1)} %copy-done.1, f32[72,8,256]{2,1,0:T(8,128)S(1)} %copy-done.3, f32[72,8,256]{2,1,0:T(8,128)S(1)} %copy-done.5), custom_call_target="tpu_custom_call" | custom-call | flops 10000000 | bytes 4000000 | tf_op jit(solution)/shard_map/pallas_call | solution.py:449
  13.7 0.2 convert_reduce_fusion.1
  13.8 0.1 select_reduce_fusion
  14.0 0.0 copy-start.13
  14.0 0.0 copy-start.11
  14.0 0.0 copy-start.14
  14.0 1.3 %copy.16.drops_ref = bf16[128,33,256]{2,1,0:T(8,128)(2,1)S(1)} copy(bf16[128,33,256]{2,0,1:T(8,128)(2,1)S(1)} %copy-done.10) | data formatting | bytes 4325376 | tf_op args[3]
  15.3 0.0 copy-start.2
  15.3 0.0 copy-start.4
  15.3 0.0 copy-start.6
  15.3 0.0 copy-done
  15.4 0.0 copy-done.11
  15.4 0.3 reduce-precision_convert_fusion
  15.7 0.1 convert_reduce_fusion
  15.8 0.0 collective-permute-done.left_ref
  15.8 0.0 collective-permute-done.1.right_ref
  15.9 0.0 copy-start.9
  15.9 1.9 %shard_map.132 = (f32[72,8,128]{2,1,0:T(8,128)S(1)}, f32[72,8,128]{2,1,0:T(8,128)S(1)}, f32[72,8,128]{2,1,0:T(8,128)S(1)}, f32[72,8,128]{2,1,0:T(8,128)S(1)}, f3...) custom-call(f32[18,8,128]{2,1,0:T(8,128)S(1)} %collective-permute-done.left_ref, ...), custom_call_target="tpu_custom_call" | custom-call | flops 10000000 | bytes 4000000 | tf_op jit(solution)/shard_map/pallas_call | solution.py:449
  17.7 0.1 collective-permute-start.2
  17.8 1.7 %collective-permute-start.3 = (f32[2,72,384]{2,1,0:T(8,128)S(1)}, f32[2,72,384]{2,1,0:T(8,128)S(1)}, u32[]{:S(2)}, u32[]{:S(2)}) collective-permute-start(f32[2,72,384]{2,1,0:T(8,128)S(1)} %get-tuple-element.36), channel_id=1, source_target_pairs={{0,24},{1,25},{2,26},{3,27},{4,28},{5,29},{6,30},{7,31},{8,0},{9,1... | collective-permute-start | bytes 663560 | tf_op jit(solution)/shard_map/ppermute | solution.py:472
  19.5 4.0 %collective-permute-done.2.up_ref = f32[2,72,384]{2,1,0:T(8,128)S(1)} collective-permute-done((f32[2,72,384]{2,1,0:T(8,128)S(1)}, f32[2,72,384]{2,1,0:T(8,128)S(1)}, u32[]{:S(2)}, u32[]{:S(2)}) %collective-permute-start.2) | collective-permute-done | bytes 221216 | tf_op jit(solution)/shard_map/ppermute | solution.py:472
  23.5 1.2 %collective-permute-done.3.down_ref = f32[2,72,384]{2,1,0:T(8,128)S(1)} collective-permute-done((f32[2,72,384]{2,1,0:T(8,128)S(1)}, f32[2,72,384]{2,1,0:T(8,128)S(1)}, u32[]{:S(2)}, u32[]{:S(2)}) %collective-permute-start.3) | collective-permute-done | bytes 221216 | tf_op jit(solution)/shard_map/ppermute | solution.py:472
  24.7 0.0 copy-done.4
  24.7 3.3 %shard_map.133 = (f32[72,8,256]{2,1,0:T(8,128)S(1)}, f32[72,8,256]{2,1,0:T(8,128)S(1)}, f32[72,8,384]{2,1,0:T(8,128)S(1)}, f32[1,72,384]{2,1,0:T(8,128)S(1)}, f32[1,72,384]{2,1,0:T(8,128)S(1)}) custom-call(f32[72,8,256]{2,1,0:T(8,128)S(1)} %copy-done.2, f32[72,8,256]{2,1,0:T(8,128)S(1)} %copy-done.4, f32[72,8,256]{2,1,0:T(8,128)S(1)} %copy-done.6, ...), custom_call_target="tpu_custom_call" | custom-call | flops 10000000 | bytes 4000000 | tf_op jit(solution)/shard_map/pallas_call | solution.py:449
  28.0 0.7 collective-permute-start.4
  28.7 1.3 %collective-permute-start.5 = (f32[1,72,384]{2,1,0:T(8,128)S(1)}, f32[1,72,384]{2,1,0:T(8,128)S(1)}, u32[]{:S(2)}, u32[]{:S(2)}) collective-permute-start(f32[1,72,384]{2,1,0:T(8,128)S(1)} %get-tuple-element.41), channel_id=1, source_target_pairs={{0,24},{1,25},{2,26},{3,27},{4,28},{5,29},{6,30},{7,31},{8,0},{9,1... | collective-permute-start | bytes 331784 | tf_op jit(solution)/shard_map/ppermute | solution.py:472
  30.0 0.1 pad_add_fusion.place_ref
  30.1 2.3 %collective-permute-done.4.up_ref = f32[1,72,384]{2,1,0:T(8,128)S(1)} collective-permute-done((f32[1,72,384]{2,1,0:T(8,128)S(1)}, f32[1,72,384]{2,1,0:T(8,128)S(1)}, u32[]{:S(2)}, u32[]{:S(2)}) %collective-permute-start.4) | collective-permute-done | bytes 110624 | tf_op jit(solution)/shard_map/ppermute | solution.py:472
  32.4 0.4 collective-permute-done.5.down_ref
  32.8 2.0 %shard_map.134 = (f32[72,8,256]{2,1,0:T(8,128)S(1)}, f32[128,256]{1,0:T(8,128)S(1)}) custom-call(f32[72,8,256]{2,1,0:T(8,128)S(1)} %copy-done.2, f32[72,8,256]{2,1,0:T(8,128)S(1)} %get-tuple-element.37.state_ref, f32[72,8,256]{2,1,0:T(8,128)S(1)} %get-tuple-element.38.smooth_ref, f32[72,8,384]{2,1,0:T(8,128)S(1)} %get-tuple-element.39.tend_ref, ...), custom_call_target="tpu_custom_call" | custom-call | flops 10000000 | bytes 4000000 | tf_op jit(solution)/shard_map/pallas_call | solution.py:449
  34.8 0.1 broadcast_in_dim.13.growth_ref
  34.9 54.3 %shard_map.135 = (bf16[128,33,256]{2,1,0:T(8,128)(2,1)S(1)}, f32[16,128]{1,0:T(8,128)S(1)}, bf16[32,16,128]{2,1,0:T(8,128)(2,1)S(1)}) custom-call(s32[128]{0:T(128)S(1)} %get-tuple-element.56.order_ref, s32[128]{0:T(128)S(1)} %get-tuple-element.55.count_ref, s32[4]{0:T(128)S(1)} %pad_add_fusion.place_ref, bf16[128,33,256]{2,1,0:T(8,128)(2,1)S(1)} %copy.16.drops_ref, ...), custom_call_target="tpu_custom_call" | custom-call | flops 10000000000 | bytes 4000000 | tf_op jit(solution)/shard_map/pallas_call | solution.py:449
  89.2 0.0 copy-start.7
  89.2 0.6 copy-done.7
  89.9 3.8 %all-to-all-start = ((bf16[32,16,128]{2,1,0:T(8,128)(2,1)}), bf16[32,16,128]{2,1,0:T(8,128)(2,1)S(1)}, u32[]{:S(2)}, u32[]{:S(2)}) async-start(bf16[32,16,128]{2,1,0:T(8,128)(2,1)} %copy-done.7), calls=%async_computation | async-start | bytes 262144 | tf_op jit(solution)/shard_map/all_to_all | solution.py:574
  93.7 0.1 stack.41.around_ref
  93.8 1.8 %copy.17 = bf16[128,33,256]{2,0,1:T(8,128)(2,1)} copy(bf16[128,33,256]{2,1,0:T(8,128)(2,1)S(1)} %get-tuple-element.53) | data formatting | bytes 4325376
  95.7 5.8 %all-to-all-done.got_ref = bf16[32,16,128]{2,1,0:T(8,128)(2,1)S(1)} async-done(((bf16[32,16,128]{2,1,0:T(8,128)(2,1)}), bf16[32,16,128]{2,1,0:T(8,128)(2,1)S(1)}, u32[]{:S(2)}, u32[]{:S(2)}) %all-to-all-start) | async-done | bytes 131104 | tf_op jit(solution)/shard_map/all_to_all | solution.py:574
  101.4 0.0 copy-done.8
  101.4 2.3 %shard_map.136 = (f32[72,8,256]{2,1,0:T(8,128)}, f32[16,256]{1,0:T(8,128)}) custom-call(s32[8]{0:T(128)S(1)} %stack.41.around_ref, f32[72,8,256]{2,1,0:T(8,128)S(1)} %get-tuple-element.42.base_ref, f32[16,128]{1,0:T(8,128)S(1)} %get-tuple-element.44.own_ref, bf16[32,16,128]{2,1,0:T(8,128)(2,1)S(1)} %all-to-all-done.got_ref, f32[72,16]{1,0:T(8,128)S(1)} %copy-done.8), custom_call_target="tpu_custom_call" | custom-call | flops 10000000 | bytes 4000000 | tf_op jit(solution)/shard_map/pallas_call | solution.py:449
  (15 shorter events, 0.0 us)
Async XLA Ops:
  0.6 14.7 %copy-start = (bf16[33,1089]{1,0:T(8,128)(2,1)S(1)}, bf16[33,1089]{1,0:T(8,128)(2,1)}, u32[]{:S(2)}) copy-start(bf16[33,1089]{1,0:T(8,128)(2,1)} %param.17) | copy-start | bytes 215626
  0.6 1.1 %copy-start.1 = (f32[72,8,256]{2,1,0:T(8,128)S(1)}, f32[72,8,256]{2,1,0:T(8,128)}, u32[]{:S(2)}) copy-start(f32[72,8,256]{2,1,0:T(8,128)} %q_ref.5) | copy-start | bytes 1769476
  1.7 1.1 %copy-start.3 = (f32[72,8,256]{2,1,0:T(8,128)S(1)}, f32[72,8,256]{2,1,0:T(8,128)}, u32[]{:S(2)}) copy-start(f32[72,8,256]{2,1,0:T(8,128)} %u_ref.3) | copy-start | bytes 1769476
  2.8 1.1 %copy-start.5 = (f32[72,8,256]{2,1,0:T(8,128)S(1)}, f32[72,8,256]{2,1,0:T(8,128)}, u32[]{:S(2)}) copy-start(f32[72,8,256]{2,1,0:T(8,128)} %v_ref.3) | copy-start | bytes 1769476
  3.9 9.8 %copy-start.12 = (s32[128]{0:T(128)S(1)}, s32[128]{0:T(128)}, u32[]{:S(2)}) copy-start(s32[128]{0:T(128)} %param.16) | copy-start | bytes 1540
  3.9 10.1 %copy-start.10 = (bf16[128,33,256]{2,0,1:T(8,128)(2,1)S(1)}, bf16[128,33,256]{2,0,1:T(8,128)(2,1)}, u32[]{:S(2)}) copy-start(bf16[128,33,256]{2,0,1:T(8,128)(2,1)} %param.14) | copy-start | bytes 6488068
  6.0 9.9 %collective-permute-start = (f32[18,8,128]{2,1,0:T(8,128)S(1)}, f32[18,8,128]{2,1,0:T(8,128)S(1)}, u32[]{:S(2)}, u32[]{:S(2)}) collective-permute-start(f32[18,8,128]{2,1,0:T(8,128)S(1)} %get-tuple-element.27), channel_id=1, source_target_pairs={{0,1},{1,2},{2,3},{3,4},{4,5},{5,6},{6,7},{7,0},{8,9},{9,10},{10,1... | collective-permute-start | bytes 221192 | tf_op jit(solution)/shard_map/ppermute | solution.py:472
  8.9 6.9 %collective-permute-start.1 = (f32[18,8,128]{2,1,0:T(8,128)S(1)}, f32[18,8,128]{2,1,0:T(8,128)S(1)}, u32[]{:S(2)}, u32[]{:S(2)}) collective-permute-start(f32[18,8,128]{2,1,0:T(8,128)S(1)} %get-tuple-element.28), channel_id=1, source_target_pairs={{0,7},{1,0},{2,1},{3,2},{4,3},{5,4},{6,5},{7,6},{8,15},{9,8},{10,9... | collective-permute-start | bytes 221192 | tf_op jit(solution)/shard_map/ppermute | solution.py:472
  14.0 1.3 %copy-start.13 = (f32[33]{0:T(128)S(1)}, f32[33]{0:T(128)}, u32[]{:S(2)}) copy-start(f32[33]{0:T(128)} %param.18) | copy-start | bytes 400
  14.0 1.4 %copy-start.11 = (bf16[1089,576]{1,0:T(8,128)(2,1)S(1)}, bf16[1089,576]{1,0:T(8,128)(2,1)}, u32[]{:S(2)}) copy-start(bf16[1089,576]{1,0:T(8,128)(2,1)} %constant.66.clone) | copy-start | bytes 3763588
  14.0 1.7 %copy-start.14 = (s32[128,1]{0,1:T(1,128)S(1)}, s32[128,1]{0,1:T(1,128)}, u32[]{:S(2)}) copy-start(s32[128,1]{0,1:T(1,128)} %param.15) | copy-start | bytes 1540
  15.3 9.4 %copy-start.2 = (f32[72,8,256]{2,1,0:T(8,128)S(1)}, f32[72,8,256]{2,1,0:T(8,128)}, u32[]{:S(2)}) copy-start(f32[72,8,256]{2,1,0:T(8,128)} %q_ref.5) | copy-start | bytes 1769476
  15.3 9.4 %copy-start.4 = (f32[72,8,256]{2,1,0:T(8,128)S(1)}, f32[72,8,256]{2,1,0:T(8,128)}, u32[]{:S(2)}) copy-start(f32[72,8,256]{2,1,0:T(8,128)} %u_ref.3) | copy-start | bytes 1769476
  15.3 9.4 %copy-start.6 = (f32[72,8,256]{2,1,0:T(8,128)S(1)}, f32[72,8,256]{2,1,0:T(8,128)}, u32[]{:S(2)}) copy-start(f32[72,8,256]{2,1,0:T(8,128)} %v_ref.3) | copy-start | bytes 1769476
  15.9 16.9 %copy-start.9 = (f32[16,72]{1,0:T(8,128)S(1)}, f32[16,72]{1,0:T(8,128)}, u32[]{:S(2)}) copy-start(f32[16,72]{1,0:T(8,128)} %constant.65.clone.down_map_ref) | copy-start | bytes 13828
  17.7 5.8 %collective-permute-start.2 = (f32[2,72,384]{2,1,0:T(8,128)S(1)}, f32[2,72,384]{2,1,0:T(8,128)S(1)}, u32[]{:S(2)}, u32[]{:S(2)}) collective-permute-start(f32[2,72,384]{2,1,0:T(8,128)S(1)} %get-tuple-element.35), channel_id=1, source_target_pairs={{0,8},{1,9},{2,10},{3,11},{4,12},{5,13},{6,14},{7,15},{8,16},{9,17... | collective-permute-start | bytes 663560 | tf_op jit(solution)/shard_map/ppermute | solution.py:472
  17.8 6.9 %collective-permute-start.3 = (f32[2,72,384]{2,1,0:T(8,128)S(1)}, f32[2,72,384]{2,1,0:T(8,128)S(1)}, u32[]{:S(2)}, u32[]{:S(2)}) collective-permute-start(f32[2,72,384]{2,1,0:T(8,128)S(1)} %get-tuple-element.36), channel_id=1, source_target_pairs={{0,24},{1,25},{2,26},{3,27},{4,28},{5,29},{6,30},{7,31},{8,0},{9,1... | collective-permute-start | bytes 663560 | tf_op jit(solution)/shard_map/ppermute | solution.py:472
  28.0 4.4 %collective-permute-start.4 = (f32[1,72,384]{2,1,0:T(8,128)S(1)}, f32[1,72,384]{2,1,0:T(8,128)S(1)}, u32[]{:S(2)}, u32[]{:S(2)}) collective-permute-start(f32[1,72,384]{2,1,0:T(8,128)S(1)} %get-tuple-element.40), channel_id=1, source_target_pairs={{0,8},{1,9},{2,10},{3,11},{4,12},{5,13},{6,14},{7,15},{8,16},{9,17... | collective-permute-start | bytes 331784 | tf_op jit(solution)/shard_map/ppermute | solution.py:472
  28.7 4.1 %collective-permute-start.5 = (f32[1,72,384]{2,1,0:T(8,128)S(1)}, f32[1,72,384]{2,1,0:T(8,128)S(1)}, u32[]{:S(2)}, u32[]{:S(2)}) collective-permute-start(f32[1,72,384]{2,1,0:T(8,128)S(1)} %get-tuple-element.41), channel_id=1, source_target_pairs={{0,24},{1,25},{2,26},{3,27},{4,28},{5,29},{6,30},{7,31},{8,0},{9,1... | collective-permute-start | bytes 331784 | tf_op jit(solution)/shard_map/ppermute | solution.py:472
  89.2 0.7 copy-start.7
  89.9 11.5 %all-to-all-start = ((bf16[32,16,128]{2,1,0:T(8,128)(2,1)}), bf16[32,16,128]{2,1,0:T(8,128)(2,1)S(1)}, u32[]{:S(2)}, u32[]{:S(2)}) async-start(bf16[32,16,128]{2,1,0:T(8,128)(2,1)} %copy-done.7), calls=%async_computation | async-start | bytes 262144 | tf_op jit(solution)/shard_map/all_to_all | solution.py:574
  93.8 7.6 %copy-start.8 = (f32[72,16]{1,0:T(8,128)S(1)}, f32[72,16]{1,0:T(8,128)}, u32[]{:S(2)}) copy-start(f32[72,16]{1,0:T(8,128)} %constant.67.clone.up_map_ref) | copy-start | bytes 13828

commit v5 on v2

--- a/solution.py
+++ b/solution.py
@@ -87,46 +87,49 @@
     return jnp.concatenate(halves, axis=2)
 
 
-def pack_kernel(q_hbm, u_hbm, v_hbm, right_ref, left_ref, q_ref, u_ref, v_ref, sems):
-    copies = []
-    for i, (src, dst) in enumerate(((q_hbm, q_ref), (u_hbm, u_ref), (v_hbm, v_ref))):
-        copies.append(pltpu.make_async_copy(src, dst, sems.at[i]))
-    for copy in copies:
-        copy.start()
-    for copy in copies:
-        copy.wait()
-    lane = iota((8, 128), 1)
-
-    def body(group, carry):
-        right = jnp.zeros((8, 128), F32)
-        left = jnp.zeros((8, 128), F32)
-        for j in range(4):
-            for f, ref in enumerate((q_ref, u_ref, v_ref)):
-                start = 32 * j + 8 * f
-                here = (lane >= start) & (lane < start + 8)
-                x = ref[group * 4 + j]
-                right = jnp.where(here, pltpu.roll(x[:, 128:256], (start - 120) % 128, 1), right)
-                first = x[:, 0:128]
-                if start:
-                    first = pltpu.roll(first, start, 1)
-                left = jnp.where(here, first, left)
-        right_ref[group] = right
-        left_ref[group] = left
-        return carry
-
-    lax.fori_loop(0, right_ref.shape[0], body, 0)
-
-
 def put_rows(x, levels, top_ref, bot_ref, i):
     top_ref[i, levels, :] = x[:, 0, :]
     bot_ref[i, levels, :] = x[:, 7, :]
 
 
-def first_kernel(q_ref, u_ref, v_ref, tend_ref, top_ref, bot_ref):
+def first_kernel(
+    q_hbm, u_hbm, v_hbm, tend_ref, top_ref, bot_ref, right_ref, left_ref, q_ref, u_ref, v_ref, sems
+):
     row_terms = derivative_terms((8, 128), 0)
     col_terms = derivative_terms((8, 128), 1)
+    lane = iota((8, 128), 1)
+    chunks = q_ref.shape[0] // CHUNK
+
+    def copies(chunk):
+        levels = pl.ds(pl.multiple_of(chunk * CHUNK, CHUNK), CHUNK)
+        return [
+            pltpu.make_async_copy(src.at[levels], dst.at[levels], sems.at[i, chunk])
+            for i, (src, dst) in enumerate(((q_hbm, q_ref), (u_hbm, u_ref), (v_hbm, v_ref)))
+        ]
+
+    for chunk in range(chunks):
+        for copy in copies(chunk):
+            copy.start()
 
     def body(chunk, carry):
+        for copy in copies(chunk):
+            copy.wait()
+        for half in range(CHUNK // 4):
+            right = jnp.zeros((8, 128), F32)
+            left = jnp.zeros((8, 128), F32)
+            for j in range(4):
+                for f, ref in enumerate((q_ref, u_ref, v_ref)):
+                    start = 32 * j + 8 * f
+                    here = (lane >= start) & (lane < start + 8)
+                    x = ref[chunk * CHUNK + half * 4 + j]
+                    moved = pltpu.roll(x[:, 128:256], (start - 120) % 128, 1)
+                    right = jnp.where(here, moved, right)
+                    first = x[:, 0:128]
+                    if start:
+                        first = pltpu.roll(first, start, 1)
+                    left = jnp.where(here, first, left)
+            right_ref[chunk * (CHUNK // 4) + half] = right
+            left_ref[chunk * (CHUNK // 4) + half] = left
         levels = pl.ds(pl.multiple_of(chunk * CHUNK, CHUNK), CHUNK)
         q = q_ref[levels]
         tend = tendency(q, u_ref[levels], v_ref[levels], row_terms, col_terms)
@@ -135,7 +138,7 @@
         put_rows(q, levels, top_ref, bot_ref, 1)
         return carry
 
-    lax.fori_loop(0, q_ref.shape[0] // CHUNK, body, 0)
+    lax.fori_loop(0, chunks, body, 0)
 
 
 def strip_kernel(
@@ -263,6 +266,13 @@
     cell_ref[...] = DT_CRM * jnp.dot(forcing, spread, preferred_element_type=F32)
 
 
+def coef_kernel(collision_ref, table_ref, after_ref, coef_ref):
+    total = jnp.dot(collision_ref[...], table_ref[...], preferred_element_type=F32) * DT_CRM
+    coarse = total.astype(BF16)
+    fine = total - coarse.astype(F32)
+    coef_ref[...] = jnp.concatenate([coarse.astype(F32), fine], axis=0).astype(BF16)
+
+
 def crm_kernel(
     order_ref, count_ref, place_ref, drops_ref, cell_ref, slot_ref, coef_ref, growth_ref,
     final_ref, heat_ref, send_ref, state_ref, pair_ref, twice_ref, heat_cell_ref, echo_cell_ref,
@@ -305,7 +315,7 @@
             for k in range(GROUP):
                 grown = grow(k, which[k], place_ref[3])
                 change = jnp.dot(coef, pair_ref[k], preferred_element_type=F32)
-                moved = grown + DT_CRM * change[0:40]
+                moved = grown + (change[0:40] + change[40:80])
                 state_ref[k] = jnp.where(s < count[k], moved, state_ref[k])
             return c
 
@@ -509,20 +519,25 @@
     wide = col_count + 128
     down_map, up_map = level_tables(levels, CRM_LEV)
 
-    to_right, to_left = call(
-        pack_kernel,
-        [((levels // 4, 8, 128), F32)] * 2,
+    tend, top, bot, to_right, to_left = call(
+        first_kernel,
+        [field, rows, rows] + [((levels // 4, 8, 128), F32)] * 2,
         [("h", tracer), ("h", wind_x), ("h", wind_y)],
         [field] * 3,
-        [pltpu.SemaphoreType.DMA((3,))],
+        [pltpu.SemaphoreType.DMA((3, levels // CHUNK))],
     )
     from_left = shift(to_right, 0, 1)
     from_right = shift(to_left, 0, -1)
-    tend, top, bot = call(first_kernel, [field, rows, rows], v(tracer, wind_x, wind_y))
     q_strip, u_strip, v_strip, tend_strip, top, bot = call(
         strip_kernel,
         [strip] * 4 + [((2, levels, wide), F32)] * 2,
         v(from_left, from_right, top, bot),
+    )
+    (coef,) = call(
+        coef_kernel,
+        [((80, 576), BF16)],
+        v(jnp.pad(collision, ((0, 40 - bins), (0, 0))), jnp.asarray(pair_table(bins), BF16))
+        + [("h", top)],
     )
     state, smooth, tend, top, bot = call(
         second_kernel,
@@ -544,9 +559,6 @@
     same = (owners[:, None] == owners[None, :]) & (index[:, None] < index[None, :])
     slot_of = owners * capacity + jnp.sum(same.astype(jnp.int32), axis=0)
     order, ordered = rank_order(counts)
-    table = jnp.asarray(pair_table(bins), BF16)
-    coef = jnp.dot(collision, table, preferred_element_type=F32)
-    coef = jnp.pad(coef.astype(BF16), ((0, 48 - bins), (0, 0)))
     growth_rows = jnp.broadcast_to(jnp.pad(growth, (0, 40 - bins))[:, None], (40, cells))
     n_gcm = lax.axis_size("gcm")
     n_crm = lax.axis_size("crm")

time: 99.3 us -> 106 us (1.067)
  Pallas kernels: 23.2 us -> 26.5 us
  starting transfers between devices: 53 us -> 55.1 us
  other arithmetic: 0.46 us -> 1.84 us
    pallas_call x7, Pallas kernels: 23.2 us -> 26.5 us  [call(): pl.pallas_call(kernel, out_shape=[jax.ShapeDtypeStruct(s, t) for s, t in...]
    all_to_all x1, starting transfers between devices: 43.1 us -> 45.2 us  [shards(): lax.all_to_all(send, ('gcm', 'crm'), split_axis=0, concat_axis=0, tiled=T...]
    unnamed x32 -> x26, local copies, waits for them, and re-layouts: 7.05 us -> 8.08 us
  transfers between devices with their start and end apart: 7 -> 7, of which waited for: 5 -> 5; matrix products, arithmetic and copies ran while one was open for 4% -> 6% of each run, Pallas kernels for 2% -> 0%
where the time goes in v5:
time: 106 us
  starting transfers between devices  55.1 us (52%)
  Pallas kernels  26.5 us (25%)
  waiting for transfers between devices  13.2 us (12%)
  local copies, waits for them, and re-layouts  8.25 us (8%)
  other arithmetic  1.84 us (2%)
    all_to_all x1, starting transfers between devices, shards(): lax.all_to_all(send, ('gcm', 'crm'), split_axis=0, concat_axis=0, tiled=T...  45.2 us
    pallas_call x7, Pallas kernels, call(): pl.pallas_call(kernel, out_shape=[jax.ShapeDtypeStruct(s, t) for s, t in...  26.5 us
    ppermute x6, starting transfers between devices, shift(): return lax.ppermute(value, ('gcm', 'crm'), pairs)  9.92 us
    unnamed x26, local copies, waits for them, and re-layouts  8.08 us
    ppermute x6, waiting for transfers between devices, shift(): return lax.ppermute(value, ('gcm', 'crm'), pairs)  7.47 us
    all_to_all x1, waiting for transfers between devices, shards(): lax.all_to_all(send, ('gcm', 'crm'), split_axis=0, concat_axis=0, tiled=T...  5.76 us
  transfers between devices with their start and end apart: 7, of which 5 were waited for; matrix products, arithmetic and copies ran while one was open for 6% of the time, Pallas kernels for 0%

profile of v5, /device:TPU:0, one launch (start us, length us, event | category | flops | bytes accessed | tf_op | source)
XLA Modules:
  0.0 105.8 jit_solution(10308580622901594751)
XLA Ops:
  0.6 0.0 copy-start
  0.6 1.1 copy-done
  1.7 1.1 %copy-done.2 = f32[72,8,256]{2,1,0:T(8,128)S(1)} copy-done((f32[72,8,256]{2,1,0:T(8,128)S(1)}, f32[72,8,256]{2,1,0:T(8,128)}, u32[]{:S(2)}) %copy-start.2) | copy-done | bytes 589848
  2.8 1.1 %copy-done.4 = f32[72,8,256]{2,1,0:T(8,128)S(1)} copy-done((f32[72,8,256]{2,1,0:T(8,128)S(1)}, f32[72,8,256]{2,1,0:T(8,128)}, u32[]{:S(2)}) %copy-start.4) | copy-done | bytes 589848
  3.8 4.6 %shard_map.130 = (f32[72,8,256]{2,1,0:T(8,128)S(1)}, f32[2,72,256]{2,1,0:T(8,128)S(1)}, f32[2,72,256]{2,1,0:T(8,128)S(1)}, f32[18,8,128]{2,1,0:T(8,128)S(1)}, f32[18,8,128]{2,1,0:T(8,128)S(1)}) custom-call(f32[72,8,256]{2,1,0:T(8,128)S(1)} %copy-done, f32[72,8,256]{2,1,0:T(8,128)S(1)} %copy-done.2, f32[72,8,256]{2,1,0:T(8,128)S(1)} %copy-done.4), custom_call_target="tpu_custom_call" | custom-call | flops 10000000 | bytes 4000000 | tf_op jit(solution)/shard_map/pallas_call | solution.py:455
  8.4 3.0 %collective-permute-start = (f32[18,8,128]{2,1,0:T(8,128)S(1)}, f32[18,8,128]{2,1,0:T(8,128)S(1)}, u32[]{:S(2)}, u32[]{:S(2)}) collective-permute-start(f32[18,8,128]{2,1,0:T(8,128)S(1)} %get-tuple-element.27), channel_id=1, source_target_pairs={{0,1},{1,2},{2,3},{3,4},{4,5},{5,6},{6,7},{7,0},{8,9},{9,10},{10,1... | collective-permute-start | bytes 221192 | tf_op jit(solution)/shard_map/ppermute | solution.py:478
  11.4 3.1 %collective-permute-start.1 = (f32[18,8,128]{2,1,0:T(8,128)S(1)}, f32[18,8,128]{2,1,0:T(8,128)S(1)}, u32[]{:S(2)}, u32[]{:S(2)}) collective-permute-start(f32[18,8,128]{2,1,0:T(8,128)S(1)} %get-tuple-element.28), channel_id=1, source_target_pairs={{0,7},{1,0},{2,1},{3,2},{4,3},{5,4},{6,5},{7,6},{8,15},{9,8},{10,9... | collective-permute-start | bytes 221192 | tf_op jit(solution)/shard_map/ppermute | solution.py:478
  14.5 0.9 convert_reduce_fusion.1
  15.4 0.8 select_reduce_fusion
  16.2 0.0 copy-start.10
  16.2 0.0 copy-start.9
  16.2 0.0 copy-start.11
  16.2 0.0 copy-start.1
  16.3 0.0 copy-start.3
  16.3 0.0 copy-start.5
  16.3 3.0 %copy.16.drops_ref = bf16[128,33,256]{2,1,0:T(8,128)(2,1)S(1)} copy(bf16[128,33,256]{2,0,1:T(8,128)(2,1)} %param.14) | data formatting | bytes 4325376 | tf_op args[3]
  19.3 0.0 copy-done.10
  19.3 0.0 copy-done.9
  19.3 0.0 copy-done.11
  19.3 0.1 convert_reduce_fusion
  19.4 0.0 collective-permute-done.left_ref
  19.4 0.0 collective-permute-done.1.right_ref
  19.5 0.0 copy-start.6
  19.5 1.9 %shard_map.131 = (f32[72,8,128]{2,1,0:T(8,128)S(1)}, f32[72,8,128]{2,1,0:T(8,128)S(1)}, f32[72,8,128]{2,1,0:T(8,128)S(1)}, f32[72,8,128]{2,1,0:T(8,128)S(1)}, f3...) custom-call(f32[18,8,128]{2,1,0:T(8,128)S(1)} %collective-permute-done.left_ref, ...), custom_call_target="tpu_custom_call" | custom-call | flops 10000000 | bytes 4000000 | tf_op jit(solution)/shard_map/pallas_call | solution.py:455
  21.3 0.1 collective-permute-start.2
  21.4 1.7 %collective-permute-start.3 = (f32[2,72,384]{2,1,0:T(8,128)S(1)}, f32[2,72,384]{2,1,0:T(8,128)S(1)}, u32[]{:S(2)}, u32[]{:S(2)}) collective-permute-start(f32[2,72,384]{2,1,0:T(8,128)S(1)} %get-tuple-element.36.after_ref), channel_id=1, source_target_pairs={{0,24},{1,25},{2,26},{3,27},{4,28},{5,29},{6,30},{7,31},{8,0},{9,1... | collective-permute-start | bytes 663560 | tf_op jit(solution)/shard_map/ppermute | solution.py:478
  23.1 4.0 %collective-permute-done.2.up_ref = f32[2,72,384]{2,1,0:T(8,128)S(1)} collective-permute-done((f32[2,72,384]{2,1,0:T(8,128)S(1)}, f32[2,72,384]{2,1,0:T(8,128)S(1)}, u32[]{:S(2)}, u32[]{:S(2)}) %collective-permute-start.2) | collective-permute-done | bytes 221216 | tf_op jit(solution)/shard_map/ppermute | solution.py:478
  27.1 1.2 %collective-permute-done.3.down_ref = f32[2,72,384]{2,1,0:T(8,128)S(1)} collective-permute-done((f32[2,72,384]{2,1,0:T(8,128)S(1)}, f32[2,72,384]{2,1,0:T(8,128)S(1)}, u32[]{:S(2)}, u32[]{:S(2)}) %collective-permute-start.3) | collective-permute-done | bytes 221216 | tf_op jit(solution)/shard_map/ppermute | solution.py:478
  28.3 0.0 copy-done.1
  28.3 0.0 copy-done.3
  28.3 0.0 copy-done.5
  28.3 3.3 %shard_map.132 = (f32[72,8,256]{2,1,0:T(8,128)S(1)}, f32[72,8,256]{2,1,0:T(8,128)S(1)}, f32[72,8,384]{2,1,0:T(8,128)S(1)}, f32[1,72,384]{2,1,0:T(8,128)S(1)}, f32[1,72,384]{2,1,0:T(8,128)S(1)}) custom-call(f32[72,8,256]{2,1,0:T(8,128)S(1)} %copy-done.1, f32[72,8,256]{2,1,0:T(8,128)S(1)} %copy-done.3, f32[72,8,256]{2,1,0:T(8,128)S(1)} %copy-done.5, ...), custom_call_target="tpu_custom_call" | custom-call | flops 10000000 | bytes 4000000 | tf_op jit(solution)/shard_map/pallas_call | solution.py:455
  31.6 0.7 collective-permute-start.4
  32.3 1.3 %collective-permute-start.5 = (f32[1,72,384]{2,1,0:T(8,128)S(1)}, f32[1,72,384]{2,1,0:T(8,128)S(1)}, u32[]{:S(2)}, u32[]{:S(2)}) collective-permute-start(f32[1,72,384]{2,1,0:T(8,128)S(1)} %get-tuple-element.41), channel_id=1, source_target_pairs={{0,24},{1,25},{2,26},{3,27},{4,28},{5,29},{6,30},{7,31},{8,0},{9,1... | collective-permute-start | bytes 331784 | tf_op jit(solution)/shard_map/ppermute | solution.py:478
  33.7 0.1 pad_add_fusion.place_ref
  33.7 0.4 shard_map.134.coef_ref
  34.1 1.9 %collective-permute-done.4.up_ref = f32[1,72,384]{2,1,0:T(8,128)S(1)} collective-permute-done((f32[1,72,384]{2,1,0:T(8,128)S(1)}, f32[1,72,384]{2,1,0:T(8,128)S(1)}, u32[]{:S(2)}, u32[]{:S(2)}) %collective-permute-start.4) | collective-permute-done | bytes 110624 | tf_op jit(solution)/shard_map/ppermute | solution.py:478
  36.0 0.4 collective-permute-done.5.down_ref
  36.4 0.0 copy-done.8
  36.4 2.0 %shard_map.133 = (f32[72,8,256]{2,1,0:T(8,128)S(1)}, f32[128,256]{1,0:T(8,128)S(1)}) custom-call(f32[72,8,256]{2,1,0:T(8,128)S(1)} %copy-done.1, f32[72,8,256]{2,1,0:T(8,128)S(1)} %get-tuple-element.37.state_ref, f32[72,8,256]{2,1,0:T(8,128)S(1)} %get-tuple-element.38.smooth_ref, f32[72,8,384]{2,1,0:T(8,128)S(1)} %get-tuple-element.39.tend_ref, ...), custom_call_target="tpu_custom_call" | custom-call | flops 10000000 | bytes 4000000 | tf_op jit(solution)/shard_map/pallas_call | solution.py:455
  38.5 0.1 broadcast_in_dim.13.growth_ref
  38.6 12.0 %shard_map.135 = (bf16[128,33,256]{2,1,0:T(8,128)(2,1)S(1)}, f32[16,128]{1,0:T(8,128)S(1)}, bf16[32,16,128]{2,1,0:T(8,128)(2,1)}) custom-call(s32[128]{0:T(128)S(1)} %get-tuple-element.56.order_ref, s32[128]{0:T(128)S(1)} %get-tuple-element.55.count_ref, s32[4]{0:T(128)S(1)} %pad_add_fusion.place_ref, bf16[128,33,256]{2,1,0:T(8,128)(2,1)S(1)} %copy.16.drops_ref, ...), custom_call_target="tpu_custom_call" | custom-call | flops 10000000000 | bytes 4000000 | tf_op jit(solution)/shard_map/pallas_call | solution.py:455
  50.6 45.2 %all-to-all-start = ((bf16[32,16,128]{2,1,0:T(8,128)(2,1)}), bf16[32,16,128]{2,1,0:T(8,128)(2,1)S(1)}, u32[]{:S(2)}, u32[]{:S(2)}) async-start(bf16[32,16,128]{2,1,0:T(8,128)(2,1)} %get-tuple-element.45), calls=%async_computation | async-start | bytes 262144 | tf_op jit(solution)/shard_map/all_to_all | solution.py:580
  95.8 0.1 stack.41.around_ref
  95.9 1.8 %copy.17 = bf16[128,33,256]{2,0,1:T(8,128)(2,1)} copy(bf16[128,33,256]{2,1,0:T(8,128)(2,1)S(1)} %get-tuple-element.53) | data formatting | bytes 4325376
  97.7 5.8 %all-to-all-done.got_ref = bf16[32,16,128]{2,1,0:T(8,128)(2,1)S(1)} async-done(((bf16[32,16,128]{2,1,0:T(8,128)(2,1)}), bf16[32,16,128]{2,1,0:T(8,128)(2,1)S(1)}, u32[]{:S(2)}, u32[]{:S(2)}) %all-to-all-start) | async-done | bytes 131104 | tf_op jit(solution)/shard_map/all_to_all | solution.py:580
  103.5 0.0 copy-done.7
  103.5 2.3 %shard_map.136 = (f32[72,8,256]{2,1,0:T(8,128)}, f32[16,256]{1,0:T(8,128)}) custom-call(s32[8]{0:T(128)S(1)} %stack.41.around_ref, f32[72,8,256]{2,1,0:T(8,128)S(1)} %get-tuple-element.42.base_ref, f32[16,128]{1,0:T(8,128)S(1)} %get-tuple-element.44.own_ref, bf16[32,16,128]{2,1,0:T(8,128)(2,1)S(1)} %all-to-all-done.got_ref, f32[72,16]{1,0:T(8,128)S(1)} %copy-done.7), custom_call_target="tpu_custom_call" | custom-call | flops 10000000 | bytes 4000000 | tf_op jit(solution)/shard_map/pallas_call | solution.py:455
  (8 shorter events, 0.0 us)
Async XLA Ops:
  0.6 1.1 %copy-start = (f32[72,8,256]{2,1,0:T(8,128)S(1)}, f32[72,8,256]{2,1,0:T(8,128)}, u32[]{:S(2)}) copy-start(f32[72,8,256]{2,1,0:T(8,128)} %q_ref.3) | copy-start | bytes 1769476
  1.7 1.1 %copy-start.2 = (f32[72,8,256]{2,1,0:T(8,128)S(1)}, f32[72,8,256]{2,1,0:T(8,128)}, u32[]{:S(2)}) copy-start(f32[72,8,256]{2,1,0:T(8,128)} %u_ref.1) | copy-start | bytes 1769476
  2.8 1.1 %copy-start.4 = (f32[72,8,256]{2,1,0:T(8,128)S(1)}, f32[72,8,256]{2,1,0:T(8,128)}, u32[]{:S(2)}) copy-start(f32[72,8,256]{2,1,0:T(8,128)} %v_ref.1) | copy-start | bytes 1769476
  8.4 11.0 %collective-permute-start = (f32[18,8,128]{2,1,0:T(8,128)S(1)}, f32[18,8,128]{2,1,0:T(8,128)S(1)}, u32[]{:S(2)}, u32[]{:S(2)}) collective-permute-start(f32[18,8,128]{2,1,0:T(8,128)S(1)} %get-tuple-element.27), channel_id=1, source_target_pairs={{0,1},{1,2},{2,3},{3,4},{4,5},{5,6},{6,7},{7,0},{8,9},{9,10},{10,1... | collective-permute-start | bytes 221192 | tf_op jit(solution)/shard_map/ppermute | solution.py:478
  11.4 8.0 %collective-permute-start.1 = (f32[18,8,128]{2,1,0:T(8,128)S(1)}, f32[18,8,128]{2,1,0:T(8,128)S(1)}, u32[]{:S(2)}, u32[]{:S(2)}) collective-permute-start(f32[18,8,128]{2,1,0:T(8,128)S(1)} %get-tuple-element.28), channel_id=1, source_target_pairs={{0,7},{1,0},{2,1},{3,2},{4,3},{5,4},{6,5},{7,6},{8,15},{9,8},{10,9... | collective-permute-start | bytes 221192 | tf_op jit(solution)/shard_map/ppermute | solution.py:478
  16.2 3.1 %copy-start.10 = (f32[33]{0:T(128)S(1)}, f32[33]{0:T(128)}, u32[]{:S(2)}) copy-start(f32[33]{0:T(128)} %param.18) | copy-start | bytes 400
  16.2 3.1 %copy-start.9 = (bf16[33,1089]{1,0:T(8,128)(2,1)S(1)}, bf16[33,1089]{1,0:T(8,128)(2,1)}, u32[]{:S(2)}) copy-start(bf16[33,1089]{1,0:T(8,128)(2,1)} %param.17) | copy-start | bytes 215626
  16.2 3.1 %copy-start.11 = (s32[128,1]{0,1:T(1,128)S(1)}, s32[128,1]{0,1:T(1,128)}, u32[]{:S(2)}) copy-start(s32[128,1]{0,1:T(1,128)} %param.15) | copy-start | bytes 1540
  16.2 12.0 %copy-start.1 = (f32[72,8,256]{2,1,0:T(8,128)S(1)}, f32[72,8,256]{2,1,0:T(8,128)}, u32[]{:S(2)}) copy-start(f32[72,8,256]{2,1,0:T(8,128)} %q_ref.3) | copy-start | bytes 1769476
  16.3 12.0 %copy-start.3 = (f32[72,8,256]{2,1,0:T(8,128)S(1)}, f32[72,8,256]{2,1,0:T(8,128)}, u32[]{:S(2)}) copy-start(f32[72,8,256]{2,1,0:T(8,128)} %u_ref.1) | copy-start | bytes 1769476
  16.3 12.0 %copy-start.5 = (f32[72,8,256]{2,1,0:T(8,128)S(1)}, f32[72,8,256]{2,1,0:T(8,128)}, u32[]{:S(2)}) copy-start(f32[72,8,256]{2,1,0:T(8,128)} %v_ref.1) | copy-start | bytes 1769476
  19.5 14.3 %copy-start.6 = (bf16[1089,576]{1,0:T(8,128)(2,1)S(1)}, bf16[1089,576]{1,0:T(8,128)(2,1)}, u32[]{:S(2)}) copy-start(bf16[1089,576]{1,0:T(8,128)(2,1)} %constant.63.clone.table_ref) | copy-start | bytes 3763588
  21.3 5.8 %collective-permute-start.2 = (f32[2,72,384]{2,1,0:T(8,128)S(1)}, f32[2,72,384]{2,1,0:T(8,128)S(1)}, u32[]{:S(2)}, u32[]{:S(2)}) collective-permute-start(f32[2,72,384]{2,1,0:T(8,128)S(1)} %get-tuple-element.35), channel_id=1, source_target_pairs={{0,8},{1,9},{2,10},{3,11},{4,12},{5,13},{6,14},{7,15},{8,16},{9,17... | collective-permute-start | bytes 663560 | tf_op jit(solution)/shard_map/ppermute | solution.py:478
  21.4 6.9 %collective-permute-start.3 = (f32[2,72,384]{2,1,0:T(8,128)S(1)}, f32[2,72,384]{2,1,0:T(8,128)S(1)}, u32[]{:S(2)}, u32[]{:S(2)}) collective-permute-start(f32[2,72,384]{2,1,0:T(8,128)S(1)} %get-tuple-element.36.after_ref), channel_id=1, source_target_pairs={{0,24},{1,25},{2,26},{3,27},{4,28},{5,29},{6,30},{7,31},{8,0},{9,1... | collective-permute-start | bytes 663560 | tf_op jit(solution)/shard_map/ppermute | solution.py:478
  28.3 8.1 %copy-start.8 = (f32[16,72]{1,0:T(8,128)S(1)}, f32[16,72]{1,0:T(8,128)}, u32[]{:S(2)}) copy-start(f32[16,72]{1,0:T(8,128)} %constant.64.clone.down_map_ref) | copy-start | bytes 13828
  31.6 4.4 %collective-permute-start.4 = (f32[1,72,384]{2,1,0:T(8,128)S(1)}, f32[1,72,384]{2,1,0:T(8,128)S(1)}, u32[]{:S(2)}, u32[]{:S(2)}) collective-permute-start(f32[1,72,384]{2,1,0:T(8,128)S(1)} %get-tuple-element.40), channel_id=1, source_target_pairs={{0,8},{1,9},{2,10},{3,11},{4,12},{5,13},{6,14},{7,15},{8,16},{9,17... | collective-permute-start | bytes 331784 | tf_op jit(solution)/shard_map/ppermute | solution.py:478
  32.3 4.1 %collective-permute-start.5 = (f32[1,72,384]{2,1,0:T(8,128)S(1)}, f32[1,72,384]{2,1,0:T(8,128)S(1)}, u32[]{:S(2)}, u32[]{:S(2)}) collective-permute-start(f32[1,72,384]{2,1,0:T(8,128)S(1)} %get-tuple-element.41), channel_id=1, source_target_pairs={{0,24},{1,25},{2,26},{3,27},{4,28},{5,29},{6,30},{7,31},{8,0},{9,1... | collective-permute-start | bytes 331784 | tf_op jit(solution)/shard_map/ppermute | solution.py:478
  50.6 52.9 %all-to-all-start = ((bf16[32,16,128]{2,1,0:T(8,128)(2,1)}), bf16[32,16,128]{2,1,0:T(8,128)(2,1)S(1)}, u32[]{:S(2)}, u32[]{:S(2)}) async-start(bf16[32,16,128]{2,1,0:T(8,128)(2,1)} %get-tuple-element.45), calls=%async_computation | async-start | bytes 262144 | tf_op jit(solution)/shard_map/all_to_all | solution.py:580
  95.9 7.6 %copy-start.7 = (f32[72,16]{1,0:T(8,128)S(1)}, f32[72,16]{1,0:T(8,128)}, u32[]{:S(2)}) copy-start(f32[72,16]{1,0:T(8,128)} %constant.65.clone.up_map_ref) | copy-start | bytes 13828

commit v6 on v5

--- a/solution.py
+++ b/solution.py
@@ -446,7 +446,7 @@
     lax.fori_loop(0, base_ref.shape[0] // CHUNK, body, 0)
 
 
-def call(kernel, outs, args, scratch=(), sems=(), flops=10_000_000):
+def call(kernel, outs, args, scratch=(), sems=(), flops=10_000_000, limit=40):
     spaces = {
         "s": pl.BlockSpec(memory_space=pltpu.SMEM),
         "v": pl.BlockSpec(memory_space=pltpu.VMEM),
@@ -458,7 +458,7 @@
         in_specs=[spaces[kind] for kind, _ in args],
         out_specs=[spaces["v"]] * len(outs),
         scratch_shapes=[pltpu.VMEM(s, t) for s, t in scratch] + list(sems),
-        compiler_params=pltpu.CompilerParams(vmem_limit_bytes=40 * MIB),
+        compiler_params=pltpu.CompilerParams(vmem_limit_bytes=limit * MIB),
         cost_estimate=pl.CostEstimate(flops=flops, bytes_accessed=4_000_000, transcendentals=0),
     )(*[value for _, value in args])
 
@@ -525,6 +525,7 @@
         [("h", tracer), ("h", wind_x), ("h", wind_y)],
         [field] * 3,
         [pltpu.SemaphoreType.DMA((3, levels // CHUNK))],
+        limit=62,
     )
     from_left = shift(to_right, 0, 1)
     from_right = shift(to_left, 0, -1)

time: 106 us -> 103 us (0.972)
  local copies, waits for them, and re-layouts: 8.25 us -> 5.1 us
    unnamed x26, local copies, waits for them, and re-layouts: 8.08 us -> 4.93 us
  transfers between devices with their start and end apart: 7 -> 7, of which waited for: 5 -> 5; matrix products, arithmetic and copies ran while one was open for 6% -> 7% of each run, Pallas kernels for 0% -> 0%
where the time goes in v6:
time: 103 us; the launch traced here: 102 us
  starting transfers between devices  55.4 us (54%)
  Pallas kernels  26 us (25%)
  waiting for transfers between devices  13.2 us (13%)
  local copies, waits for them, and re-layouts  5.1 us (5%)
  other arithmetic  1.84 us (2%)
    all_to_all x1, starting transfers between devices, shards(): lax.all_to_all(send, ('gcm', 'crm'), split_axis=0, concat_axis=0, tiled=T...  45.5 us
    pallas_call x7, Pallas kernels, call(): pl.pallas_call(kernel, out_shape=[jax.ShapeDtypeStruct(s, t) for s, t in...  26 us
    ppermute x6, starting transfers between devices, shift(): return lax.ppermute(value, ('gcm', 'crm'), pairs)  9.92 us
    ppermute x6, waiting for transfers between devices, shift(): return lax.ppermute(value, ('gcm', 'crm'), pairs)  7.46 us
    all_to_all x1, waiting for transfers between devices, shards(): lax.all_to_all(send, ('gcm', 'crm'), split_axis=0, concat_axis=0, tiled=T...  5.76 us
    unnamed x26, local copies, waits for them, and re-layouts  4.93 us
  transfers between devices with their start and end apart: 7, of which 5 were waited for; matrix products, arithmetic and copies ran while one was open for 7% of the time, Pallas kernels for 0%

profile of v6, /device:TPU:0, one launch (start us, length us, event | category | flops | bytes accessed | tf_op | source)
XLA Modules:
  0.0 102.5 jit_solution(11167685069986430707)
XLA Ops:
  0.6 4.1 %shard_map.130 = (f32[72,8,256]{2,1,0:T(8,128)}, f32[2,72,256]{2,1,0:T(8,128)}, f32[2,72,256]{2,1,0:T(8,128)}, f32[18,8,128]{2,1,0:T(8,128)}, f32[18,8,128]{2,1,0:T(8,128)}) custom-call(f32[72,8,256]{2,1,0:T(8,128)} %q_ref.3, f32[72,8,256]{2,1,0:T(8,128)} %u_ref.1, f32[72,8,256]{2,1,0:T(8,128)} %v_ref.1), custom_call_target="tpu_custom_call" | custom-call | flops 10000000 | bytes 4000000 | tf_op jit(solution)/shard_map/pallas_call | solution.py:455
  4.8 3.0 %collective-permute-start = (f32[18,8,128]{2,1,0:T(8,128)}, f32[18,8,128]{2,1,0:T(8,128)S(1)}, u32[]{:S(2)}, u32[]{:S(2)}) collective-permute-start(f32[18,8,128]{2,1,0:T(8,128)} %get-tuple-element.27), channel_id=1, source_target_pairs={{0,1},{1,2},{2,3},{3,4},{4,5},{5,6},{6,7},{7,0},{8,9},{9,10},{10,1... | collective-permute-start | bytes 221192 | tf_op jit(solution)/shard_map/ppermute | solution.py:478
  7.8 3.1 %collective-permute-start.1 = (f32[18,8,128]{2,1,0:T(8,128)}, f32[18,8,128]{2,1,0:T(8,128)S(1)}, u32[]{:S(2)}, u32[]{:S(2)}) collective-permute-start(f32[18,8,128]{2,1,0:T(8,128)} %get-tuple-element.28), channel_id=1, source_target_pairs={{0,7},{1,0},{2,1},{3,2},{4,3},{5,4},{6,5},{7,6},{8,15},{9,8},{10,9... | collective-permute-start | bytes 221192 | tf_op jit(solution)/shard_map/ppermute | solution.py:478
  10.9 0.9 convert_reduce_fusion.1
  11.8 0.8 select_reduce_fusion
  12.5 0.0 copy-start.10
  12.6 0.0 copy-start.9
  12.6 0.0 copy-start.11
  12.6 0.0 copy-start.5
  12.6 0.0 copy-start.6
  12.6 0.0 copy-start
  12.6 0.0 copy-start.1
  12.6 0.0 copy-start.2
  12.6 0.0 copy-start.4
  12.7 3.0 %copy.16.drops_ref = bf16[128,33,256]{2,1,0:T(8,128)(2,1)S(1)} copy(bf16[128,33,256]{2,0,1:T(8,128)(2,1)} %param.14) | data formatting | bytes 4325376 | tf_op args[3]
  15.7 0.0 copy-done.10
  15.7 0.0 copy-done.9
  15.7 0.0 copy-done.11
  15.7 0.1 convert_reduce_fusion
  15.8 0.0 collective-permute-done.left_ref
  15.8 0.0 collective-permute-done.1.right_ref
  15.9 0.0 copy-done.5
  15.9 0.0 copy-done.6
  15.9 0.0 copy-start.3
  15.9 1.9 %shard_map.131 = (f32[72,8,128]{2,1,0:T(8,128)S(1)}, f32[72,8,128]{2,1,0:T(8,128)S(1)}, f32[72,8,128]{2,1,0:T(8,128)S(1)}, f32[72,8,128]{2,1,0:T(8,128)S(1)}, f3...) custom-call(f32[18,8,128]{2,1,0:T(8,128)S(1)} %collective-permute-done.left_ref, ...), custom_call_target="tpu_custom_call" | custom-call | flops 10000000 | bytes 4000000 | tf_op jit(solution)/shard_map/pallas_call | solution.py:455
  17.8 0.1 collective-permute-start.2
  17.8 1.7 %collective-permute-start.3 = (f32[2,72,384]{2,1,0:T(8,128)S(1)}, f32[2,72,384]{2,1,0:T(8,128)S(1)}, u32[]{:S(2)}, u32[]{:S(2)}) collective-permute-start(f32[2,72,384]{2,1,0:T(8,128)S(1)} %get-tuple-element.36.after_ref), channel_id=1, source_target_pairs={{0,24},{1,25},{2,26},{3,27},{4,28},{5,29},{6,30},{7,31},{8,0},{9,1... | collective-permute-start | bytes 663560 | tf_op jit(solution)/shard_map/ppermute | solution.py:478
  19.6 4.0 %collective-permute-done.2.up_ref = f32[2,72,384]{2,1,0:T(8,128)S(1)} collective-permute-done((f32[2,72,384]{2,1,0:T(8,128)S(1)}, f32[2,72,384]{2,1,0:T(8,128)S(1)}, u32[]{:S(2)}, u32[]{:S(2)}) %collective-permute-start.2) | collective-permute-done | bytes 221216 | tf_op jit(solution)/shard_map/ppermute | solution.py:478
  23.5 1.2 %collective-permute-done.3.down_ref = f32[2,72,384]{2,1,0:T(8,128)S(1)} collective-permute-done((f32[2,72,384]{2,1,0:T(8,128)S(1)}, f32[2,72,384]{2,1,0:T(8,128)S(1)}, u32[]{:S(2)}, u32[]{:S(2)}) %collective-permute-start.3) | collective-permute-done | bytes 221216 | tf_op jit(solution)/shard_map/ppermute | solution.py:478
  24.7 0.0 copy-done
  24.7 0.0 copy-done.4
  24.7 0.0 copy-start.8
  24.7 3.3 %shard_map.132 = (f32[72,8,256]{2,1,0:T(8,128)S(1)}, f32[72,8,256]{2,1,0:T(8,128)S(1)}, f32[72,8,384]{2,1,0:T(8,128)S(1)}, f32[1,72,384]{2,1,0:T(8,128)S(1)}, f32[1,72,384]{2,1,0:T(8,128)S(1)}) custom-call(f32[72,8,256]{2,1,0:T(8,128)S(1)} %copy-done, f32[72,8,256]{2,1,0:T(8,128)S(1)} %copy-done.1, f32[72,8,256]{2,1,0:T(8,128)S(1)} %copy-done.2, ...), custom_call_target="tpu_custom_call" | custom-call | flops 10000000 | bytes 4000000 | tf_op jit(solution)/shard_map/pallas_call | solution.py:455
  28.0 0.7 collective-permute-start.4
  28.7 1.3 %collective-permute-start.5 = (f32[1,72,384]{2,1,0:T(8,128)S(1)}, f32[1,72,384]{2,1,0:T(8,128)S(1)}, u32[]{:S(2)}, u32[]{:S(2)}) collective-permute-start(f32[1,72,384]{2,1,0:T(8,128)S(1)} %get-tuple-element.41), channel_id=1, source_target_pairs={{0,24},{1,25},{2,26},{3,27},{4,28},{5,29},{6,30},{7,31},{8,0},{9,1... | collective-permute-start | bytes 331784 | tf_op jit(solution)/shard_map/ppermute | solution.py:478
  30.1 0.1 pad_add_fusion.place_ref
  30.1 0.4 shard_map.134.coef_ref
  30.5 1.9 %collective-permute-done.4.up_ref = f32[1,72,384]{2,1,0:T(8,128)S(1)} collective-permute-done((f32[1,72,384]{2,1,0:T(8,128)S(1)}, f32[1,72,384]{2,1,0:T(8,128)S(1)}, u32[]{:S(2)}, u32[]{:S(2)}) %collective-permute-start.4) | collective-permute-done | bytes 110624 | tf_op jit(solution)/shard_map/ppermute | solution.py:478
  32.4 0.4 collective-permute-done.5.down_ref
  32.8 2.0 %shard_map.133 = (f32[72,8,256]{2,1,0:T(8,128)S(1)}, f32[128,256]{1,0:T(8,128)S(1)}) custom-call(f32[72,8,256]{2,1,0:T(8,128)S(1)} %copy-done, f32[72,8,256]{2,1,0:T(8,128)S(1)} %get-tuple-element.37.state_ref, f32[72,8,256]{2,1,0:T(8,128)S(1)} %get-tuple-element.38.smooth_ref, f32[72,8,384]{2,1,0:T(8,128)S(1)} %get-tuple-element.39.tend_ref, ...), custom_call_target="tpu_custom_call" | custom-call | flops 10000000 | bytes 4000000 | tf_op jit(solution)/shard_map/pallas_call | solution.py:455
  34.9 0.1 broadcast_in_dim.13.growth_ref
  34.9 12.0 %shard_map.135 = (bf16[128,33,256]{2,1,0:T(8,128)(2,1)S(1)}, f32[16,128]{1,0:T(8,128)S(1)}, bf16[32,16,128]{2,1,0:T(8,128)(2,1)}) custom-call(s32[128]{0:T(128)S(1)} %get-tuple-element.56.order_ref, s32[128]{0:T(128)S(1)} %get-tuple-element.55.count_ref, s32[4]{0:T(128)S(1)} %pad_add_fusion.place_ref, bf16[128,33,256]{2,1,0:T(8,128)(2,1)S(1)} %copy.16.drops_ref, ...), custom_call_target="tpu_custom_call" | custom-call | flops 10000000000 | bytes 4000000 | tf_op jit(solution)/shard_map/pallas_call | solution.py:455
  47.0 45.5 %all-to-all-start = ((bf16[32,16,128]{2,1,0:T(8,128)(2,1)}), bf16[32,16,128]{2,1,0:T(8,128)(2,1)S(1)}, u32[]{:S(2)}, u32[]{:S(2)}) async-start(bf16[32,16,128]{2,1,0:T(8,128)(2,1)} %get-tuple-element.45), calls=%async_computation | async-start | bytes 262144 | tf_op jit(solution)/shard_map/all_to_all | solution.py:581
  92.5 0.1 stack.41.around_ref
  92.6 1.8 %copy.17 = bf16[128,33,256]{2,0,1:T(8,128)(2,1)} copy(bf16[128,33,256]{2,1,0:T(8,128)(2,1)S(1)} %get-tuple-element.53) | data formatting | bytes 4325376
  94.4 5.8 %all-to-all-done.got_ref = bf16[32,16,128]{2,1,0:T(8,128)(2,1)S(1)} async-done(((bf16[32,16,128]{2,1,0:T(8,128)(2,1)}), bf16[32,16,128]{2,1,0:T(8,128)(2,1)S(1)}, u32[]{:S(2)}, u32[]{:S(2)}) %all-to-all-start) | async-done | bytes 131104 | tf_op jit(solution)/shard_map/all_to_all | solution.py:581
  100.2 0.0 copy-done.7
  100.2 2.3 %shard_map.136 = (f32[72,8,256]{2,1,0:T(8,128)}, f32[16,256]{1,0:T(8,128)}) custom-call(s32[8]{0:T(128)S(1)} %stack.41.around_ref, f32[72,8,256]{2,1,0:T(8,128)S(1)} %get-tuple-element.42.base_ref, f32[16,128]{1,0:T(8,128)S(1)} %get-tuple-element.44.own_ref, bf16[32,16,128]{2,1,0:T(8,128)(2,1)S(1)} %all-to-all-done.got_ref, f32[72,16]{1,0:T(8,128)S(1)} %copy-done.7), custom_call_target="tpu_custom_call" | custom-call | flops 10000000 | bytes 4000000 | tf_op jit(solution)/shard_map/pallas_call | solution.py:455
  (8 shorter events, 0.0 us)
Async XLA Ops:
  4.8 11.1 %collective-permute-start = (f32[18,8,128]{2,1,0:T(8,128)}, f32[18,8,128]{2,1,0:T(8,128)S(1)}, u32[]{:S(2)}, u32[]{:S(2)}) collective-permute-start(f32[18,8,128]{2,1,0:T(8,128)} %get-tuple-element.27), channel_id=1, source_target_pairs={{0,1},{1,2},{2,3},{3,4},{4,5},{5,6},{6,7},{7,0},{8,9},{9,10},{10,1... | collective-permute-start | bytes 221192 | tf_op jit(solution)/shard_map/ppermute | solution.py:478
  7.8 8.1 %collective-permute-start.1 = (f32[18,8,128]{2,1,0:T(8,128)}, f32[18,8,128]{2,1,0:T(8,128)S(1)}, u32[]{:S(2)}, u32[]{:S(2)}) collective-permute-start(f32[18,8,128]{2,1,0:T(8,128)} %get-tuple-element.28), channel_id=1, source_target_pairs={{0,7},{1,0},{2,1},{3,2},{4,3},{5,4},{6,5},{7,6},{8,15},{9,8},{10,9... | collective-permute-start | bytes 221192 | tf_op jit(solution)/shard_map/ppermute | solution.py:478
  12.5 3.1 %copy-start.10 = (f32[33]{0:T(128)S(1)}, f32[33]{0:T(128)}, u32[]{:S(2)}) copy-start(f32[33]{0:T(128)} %param.18) | copy-start | bytes 400
  12.6 3.1 %copy-start.9 = (bf16[33,1089]{1,0:T(8,128)(2,1)S(1)}, bf16[33,1089]{1,0:T(8,128)(2,1)}, u32[]{:S(2)}) copy-start(bf16[33,1089]{1,0:T(8,128)(2,1)} %param.17) | copy-start | bytes 215626
  12.6 3.2 %copy-start.11 = (s32[128,1]{0,1:T(1,128)S(1)}, s32[128,1]{0,1:T(1,128)}, u32[]{:S(2)}) copy-start(s32[128,1]{0,1:T(1,128)} %param.15) | copy-start | bytes 1540
  12.6 3.3 %copy-start.5 = (f32[2,72,256]{2,1,0:T(8,128)S(1)}, f32[2,72,256]{2,1,0:T(8,128)}, u32[]{:S(2)}) copy-start(f32[2,72,256]{2,1,0:T(8,128)} %get-tuple-element.29.top_main) | copy-start | bytes 442372
  12.6 3.3 %copy-start.6 = (f32[2,72,256]{2,1,0:T(8,128)S(1)}, f32[2,72,256]{2,1,0:T(8,128)}, u32[]{:S(2)}) copy-start(f32[2,72,256]{2,1,0:T(8,128)} %get-tuple-element.30.bot_main) | copy-start | bytes 442372
  12.6 12.1 %copy-start = (f32[72,8,256]{2,1,0:T(8,128)S(1)}, f32[72,8,256]{2,1,0:T(8,128)}, u32[]{:S(2)}) copy-start(f32[72,8,256]{2,1,0:T(8,128)} %q_ref.3) | copy-start | bytes 1769476
  12.6 12.1 %copy-start.1 = (f32[72,8,256]{2,1,0:T(8,128)S(1)}, f32[72,8,256]{2,1,0:T(8,128)}, u32[]{:S(2)}) copy-start(f32[72,8,256]{2,1,0:T(8,128)} %u_ref.1) | copy-start | bytes 1769476
  12.6 12.1 %copy-start.2 = (f32[72,8,256]{2,1,0:T(8,128)S(1)}, f32[72,8,256]{2,1,0:T(8,128)}, u32[]{:S(2)}) copy-start(f32[72,8,256]{2,1,0:T(8,128)} %v_ref.1) | copy-start | bytes 1769476
  12.6 12.1 %copy-start.4 = (f32[72,8,256]{2,1,0:T(8,128)S(1)}, f32[72,8,256]{2,1,0:T(8,128)}, u32[]{:S(2)}) copy-start(f32[72,8,256]{2,1,0:T(8,128)} %get-tuple-element.26.tend_ref) | copy-start | bytes 1769476
  15.9 14.3 %copy-start.3 = (bf16[1089,576]{1,0:T(8,128)(2,1)S(1)}, bf16[1089,576]{1,0:T(8,128)(2,1)}, u32[]{:S(2)}) copy-start(bf16[1089,576]{1,0:T(8,128)(2,1)} %constant.63.clone.table_ref) | copy-start | bytes 3763588
  17.8 5.8 %collective-permute-start.2 = (f32[2,72,384]{2,1,0:T(8,128)S(1)}, f32[2,72,384]{2,1,0:T(8,128)S(1)}, u32[]{:S(2)}, u32[]{:S(2)}) collective-permute-start(f32[2,72,384]{2,1,0:T(8,128)S(1)} %get-tuple-element.35), channel_id=1, source_target_pairs={{0,8},{1,9},{2,10},{3,11},{4,12},{5,13},{6,14},{7,15},{8,16},{9,17... | collective-permute-start | bytes 663560 | tf_op jit(solution)/shard_map/ppermute | solution.py:478
  17.8 6.9 %collective-permute-start.3 = (f32[2,72,384]{2,1,0:T(8,128)S(1)}, f32[2,72,384]{2,1,0:T(8,128)S(1)}, u32[]{:S(2)}, u32[]{:S(2)}) collective-permute-start(f32[2,72,384]{2,1,0:T(8,128)S(1)} %get-tuple-element.36.after_ref), channel_id=1, source_target_pairs={{0,24},{1,25},{2,26},{3,27},{4,28},{5,29},{6,30},{7,31},{8,0},{9,1... | collective-permute-start | bytes 663560 | tf_op jit(solution)/shard_map/ppermute | solution.py:478
  24.7 8.1 %copy-start.8 = (f32[16,72]{1,0:T(8,128)S(1)}, f32[16,72]{1,0:T(8,128)}, u32[]{:S(2)}) copy-start(f32[16,72]{1,0:T(8,128)} %constant.64.clone.down_map_ref) | copy-start | bytes 13828
  28.0 4.4 %collective-permute-start.4 = (f32[1,72,384]{2,1,0:T(8,128)S(1)}, f32[1,72,384]{2,1,0:T(8,128)S(1)}, u32[]{:S(2)}, u32[]{:S(2)}) collective-permute-start(f32[1,72,384]{2,1,0:T(8,128)S(1)} %get-tuple-element.40), channel_id=1, source_target_pairs={{0,8},{1,9},{2,10},{3,11},{4,12},{5,13},{6,14},{7,15},{8,16},{9,17... | collective-permute-start | bytes 331784 | tf_op jit(solution)/shard_map/ppermute | solution.py:478
  28.7 4.1 %collective-permute-start.5 = (f32[1,72,384]{2,1,0:T(8,128)S(1)}, f32[1,72,384]{2,1,0:T(8,128)S(1)}, u32[]{:S(2)}, u32[]{:S(2)}) collective-permute-start(f32[1,72,384]{2,1,0:T(8,128)S(1)} %get-tuple-element.41), channel_id=1, source_target_pairs={{0,24},{1,25},{2,26},{3,27},{4,28},{5,29},{6,30},{7,31},{8,0},{9,1... | collective-permute-start | bytes 331784 | tf_op jit(solution)/shard_map/ppermute | solution.py:478
  47.0 53.2 %all-to-all-start = ((bf16[32,16,128]{2,1,0:T(8,128)(2,1)}), bf16[32,16,128]{2,1,0:T(8,128)(2,1)S(1)}, u32[]{:S(2)}, u32[]{:S(2)}) async-start(bf16[32,16,128]{2,1,0:T(8,128)(2,1)} %get-tuple-element.45), calls=%async_computation | async-start | bytes 262144 | tf_op jit(solution)/shard_map/all_to_all | solution.py:581
  92.6 7.6 %copy-start.7 = (f32[72,16]{1,0:T(8,128)S(1)}, f32[72,16]{1,0:T(8,128)}, u32[]{:S(2)}) copy-start(f32[72,16]{1,0:T(8,128)} %constant.65.clone.up_map_ref) | copy-start | bytes 13828
